TPU v7x, 32 devices: a whole 2x2x4 slice. The times are simulated.
32 devices in a mesh: dp: 4 (over x, core), context: 4 (over z), experts: 2 (over y).
Axes of the slice: x: 2, y: 2, z: 4, core: 2. Of those that a mesh axis runs over, the one named last changes fastest.
Arguments:
- tokens: bfloat16 [8, 1024, 768], P(('dp', 'experts'), 'context'), may hold values from -6 to 6
- norm1_gain: float32 [768], replicated, may hold values from 0.5 to 1.5
- qkv_weight: bfloat16 [768, 2304], replicated, may hold values from -0.21875 to 0.21875
- out_weight: bfloat16 [768, 768], replicated, may hold values from -2.5 to 2.5
- norm2_gain: float32 [768], replicated, may hold values from 0.5 to 1.5
- router_weight: bfloat16 [768, 4], replicated, may hold values from -0.15625 to 0.15625
- expert_gate: bfloat16 [4, 768, 2048], P('experts'), may hold values from -0.21875 to 0.21875
- expert_up: bfloat16 [4, 768, 2048], P('experts'), may hold values from -0.21875 to 0.21875
- expert_down: bfloat16 [4, 2048, 768], P('experts'), may hold values from -0.25 to 0.25
- shared_gate: bfloat16 [768, 2048], replicated, may hold values from -0.21875 to 0.21875
- shared_up: bfloat16 [768, 2048], replicated, may hold values from -0.21875 to 0.21875
- shared_down: bfloat16 [2048, 768], replicated, may hold values from -0.25 to 0.25
- routes: int32 [4, 8, 256, 2], P('context', ('dp', 'experts')), may hold values from 0 to 3, all different within a row; in each aligned block of 256 rows (0 to 255, 256 to 511, ..., all dimensions but the last counted through in order) at most 160 rows name the same one
- cotangent: bfloat16 [8, 1024, 768], P(('dp', 'experts'), 'context'), may hold values from -6 to 6
Outputs:
- output: bfloat16 [8, 1024, 768], P(('dp', 'experts'), 'context')
- input_grad: float32 [8, 1024, 768], P(('dp', 'experts'), 'context')
- norm1_grad: float32 [768], P(('dp', 'context'))
- qkv_grad: float32 [768, 2304], P(('dp', 'context'))
- out_grad: float32 [768, 768], P(('dp', 'context'))
- norm2_grad: float32 [768], P(('dp', 'context'))
- router_grad: float32 [768, 4], P(('dp', 'context'))
- expert_gate_grad: float32 [4, 768, 2048], P('experts', ('dp', 'context'))
- expert_up_grad: float32 [4, 768, 2048], P('experts', ('dp', 'context'))
- expert_down_grad: float32 [4, 2048, 768], P('experts', ('dp', 'context'))
- shared_gate_grad: float32 [768, 2048], P(('dp', 'context'))
- shared_up_grad: float32 [768, 2048], P(('dp', 'context'))
- shared_down_grad: float32 [2048, 768], P(('dp', 'context'))
Inputs may be any that keep to these rules, and one draw needn't show every extreme that they name: `routes`: each token names 2 different experts. Within the rows of one device (aligned blocks of 256 rows, leading dimensions taken in order) no expert is named more than 160 times, and this bound is reached.
All inputs are finite; a program needn't handle non-finite values.
Results may differ from a plain program's by a relative error of at most 0.03.
Values may be sent and summed in bfloat16 or wider, within the bound.
No kernel may reach another device: no remote copies, remote signals or barrier semaphores. Data moves between devices by JAX's collectives and lax.ppermute only.
A program may use at most 384 MiB of HBM per device.

v0:
```python
from functools import partial
import math

import jax
import jax.numpy as jnp
from jax import lax
from jax.sharding import PartitionSpec as P

HEAD_DIM = 64
BLOCK = 256


norm_eps = 1e-05
masked_score = -1e30
highest = lax.Precision.HIGHEST


def matmul(left, right):
    return jnp.dot(left, right, preferred_element_type=jnp.float32)


def contract(spec, left, right):
    return jnp.einsum(spec, left, right, preferred_element_type=jnp.float32)


def normalize(field):
    factor = lax.rsqrt(jnp.mean(field * field, axis=-1, keepdims=True) + norm_eps)
    return (field * factor, factor)


def norm_back(grad_out, normed, factor, gain):
    grad_norm = grad_out * gain
    inner = jnp.mean(grad_norm * normed, axis=-1, keepdims=True)
    return (factor * (grad_norm - normed * inner), jnp.sum(grad_out * normed, axis=0))


def rotation(positions, head_dim):
    half = head_dim // 2
    freqs = 10000.0 ** (-2.0 * jnp.arange(half, dtype=jnp.float32) / head_dim)
    angles = positions.astype(jnp.float32)[:, None] * freqs[None, :]
    return (jnp.cos(angles)[:, None, None, :], jnp.sin(angles)[:, None, None, :])


def rotate(field, cosine, sine):
    half = field.shape[-1] // 2
    first = field[..., :half]
    second = field[..., half:]
    return jnp.concatenate(
        [first * cosine - second * sine, second * cosine + first * sine], axis=-1
    )


def rotate_back(grad, cosine, sine):
    half = grad.shape[-1] // 2
    first = grad[..., :half]
    second = grad[..., half:]
    return jnp.concatenate(
        [first * cosine + second * sine, second * cosine - first * sine], axis=-1
    )


def silu_back(grad_hidden, gate_part, up_part):
    sigmoid_value = jax.nn.sigmoid(gate_part)
    active = gate_part * sigmoid_value
    grad_gate = grad_hidden * up_part * sigmoid_value * (1.0 + gate_part * (1.0 - sigmoid_value))
    grad_up = grad_hidden * active
    return (grad_gate.astype(jnp.bfloat16), grad_up.astype(jnp.bfloat16))


def score_block(queries, keys_part, query_block, start):
    size = keys_part.shape[0]
    seqs, heads, head_dim = (queries.shape[1], queries.shape[2], queries.shape[3])
    keys_four = keys_part.reshape(size, seqs, heads, head_dim)
    scores = contract("qshd,kshd->shqk", queries, keys_four) * head_dim ** (-0.5)
    key_block = (start + jnp.arange(size)) // BLOCK
    visible = key_block[None, :] <= query_block[:, None]
    return (jnp.where(visible, scores, masked_score), visible, keys_four)


def attend_piece(queries, query_block, state, keys_part, values_part, start):
    size = keys_part.shape[0]
    seqs, heads, head_dim = (queries.shape[1], queries.shape[2], queries.shape[3])

    def compute(current):
        best, total, accum = current
        scores, visible, keys_four = score_block(queries, keys_part, query_block, start)
        new_best = jnp.maximum(best, jnp.max(scores, axis=-1))
        weights = jnp.where(visible, jnp.exp(scores - new_best[..., None]), 0.0)
        factor = jnp.exp(best - new_best)
        values_four = values_part.reshape(size, seqs, heads, head_dim)
        total = total * factor + jnp.sum(weights, axis=-1)
        accum = accum * factor[..., None] + contract(
            "shqk,kshd->shqd", weights.astype(jnp.bfloat16), values_four
        )
        return (new_best, total, accum)

    needed = start // BLOCK <= jnp.max(query_block)
    return lax.cond(needed, compute, lambda current: current, state)


def fold_keys(queries, query_block, state, pieces):
    keys_all, values_all = pieces
    length = keys_all.shape[0]
    size = math.gcd(length, 512)

    def step(index, current):
        first = index * size
        keys_part = lax.dynamic_slice_in_dim(keys_all, first, size, 0)
        values_part = lax.dynamic_slice_in_dim(values_all, first, size, 0)
        return attend_piece(queries, query_block, current, keys_part, values_part, first)

    return lax.fori_loop(0, length // size, step, state)


def block_grads(queries, query_block, grad_ctx, delta, log_total, keys_part, values_part, start):
    size = keys_part.shape[0]
    seqs, heads, head_dim = (queries.shape[1], queries.shape[2], queries.shape[3])
    scores, visible, keys_four = score_block(queries, keys_part, query_block, start)
    probs = jnp.where(visible, jnp.exp(scores - log_total[..., None]), 0.0)
    values_four = values_part.reshape(size, seqs, heads, head_dim)
    grad_probs = contract("qshd,kshd->shqk", grad_ctx, values_four)
    grad_scores = (probs * (grad_probs - delta[..., None])).astype(jnp.bfloat16)
    return (probs, grad_scores, keys_four)


def key_value_terms(
    queries, query_block, grad_ctx, delta, log_total, keys_part, values_part, start
):
    size = keys_part.shape[0]
    seqs, heads, head_dim = (queries.shape[1], queries.shape[2], queries.shape[3])
    width = heads * head_dim
    probs, grad_scores, keys_four = block_grads(
        queries, query_block, grad_ctx, delta, log_total, keys_part, values_part, start
    )
    grad_values = contract("shqk,qshd->kshd", probs.astype(jnp.bfloat16), grad_ctx)
    grad_keys = contract("shqk,qshd->kshd", grad_scores, queries) * head_dim ** (-0.5)
    return jnp.concatenate(
        [grad_keys.reshape(size, seqs, width), grad_values.reshape(size, seqs, width)], axis=-1
    )


def query_grads(queries, query_block, grad_ctx, delta, log_total, keys_all, values_all):
    length = keys_all.shape[0]
    size = math.gcd(length, 512)

    def step(index, accum):
        first = index * size
        keys_part = lax.dynamic_slice_in_dim(keys_all, first, size, 0)
        values_part = lax.dynamic_slice_in_dim(values_all, first, size, 0)

        def compute(current):
            probs, grad_scores, keys_four = block_grads(
                queries, query_block, grad_ctx, delta, log_total, keys_part, values_part, first
            )
            return current + contract("shqk,kshd->qshd", grad_scores, keys_four)

        return lax.cond(
            first // BLOCK <= jnp.max(query_block), compute, lambda current: current, accum
        )

    return lax.fori_loop(0, length // size, step, jnp.zeros(queries.shape, jnp.float32))


def query_side_fold(keys_local, values_local, key_start, accum, pieces, start):
    queries_all, grad_all, delta_all, log_all = pieces
    length = queries_all.shape[0]
    size = math.gcd(length, 512)

    def step(index, current):
        first = index * size
        queries_part = lax.dynamic_slice_in_dim(queries_all, first, size, 0)
        grad_part = lax.dynamic_slice_in_dim(grad_all, first, size, 0)
        delta_part = jnp.transpose(lax.dynamic_slice_in_dim(delta_all, first, size, 0), (1, 2, 0))
        log_part = jnp.transpose(lax.dynamic_slice_in_dim(log_all, first, size, 0), (1, 2, 0))
        block_rows = (first + jnp.arange(size)) // BLOCK

        def compute(inner):
            return inner + key_value_terms(
                queries_part,
                block_rows,
                grad_part,
                delta_part,
                log_part,
                keys_local,
                values_local,
                key_start,
            )

        return lax.cond(
            jnp.max(block_rows) >= key_start // BLOCK, compute, lambda inner: inner, current
        )

    return lax.fori_loop(0, length // size, step, accum)


def reduce_experts(gate_grad, up_grad, down_grad):
    return (
        lax.psum_scatter(gate_grad, ("dp", "context"), scatter_dimension=1, tiled=True),
        lax.psum_scatter(up_grad, ("dp", "context"), scatter_dimension=1, tiled=True),
        lax.psum_scatter(down_grad, ("dp", "context"), scatter_dimension=1, tiled=True),
    )


def on_device(
    tokens,
    norm1_gain,
    qkv_weight,
    out_weight,
    norm2_gain,
    router_weight,
    expert_gate,
    expert_up,
    expert_down,
    shared_gate,
    shared_up,
    shared_down,
    routes,
    cotangent,
):
    seqs, span, width = tokens.shape
    heads = width // HEAD_DIM
    rows = seqs * span
    local = jnp.swapaxes(tokens, 0, 1).reshape(rows, width).astype(jnp.float32)
    key_start = lax.axis_index("context") * span
    positions = key_start + jnp.arange(span)
    query_block = positions // BLOCK
    cosine, sine = rotation(positions, HEAD_DIM)
    normed_one, factor_one = normalize(local)
    entry_one = (normed_one * norm1_gain).astype(jnp.bfloat16)
    projected = matmul(entry_one, qkv_weight).reshape(span, seqs, 3, heads, HEAD_DIM)
    queries = rotate(projected[:, :, 0], cosine, sine).astype(jnp.bfloat16)
    keys_local = (
        rotate(projected[:, :, 1], cosine, sine).astype(jnp.bfloat16).reshape(span, seqs, width)
    )
    values_local = projected[:, :, 2].astype(jnp.bfloat16).reshape(span, seqs, width)
    start_state = (
        jnp.full((seqs, heads, span), masked_score, jnp.float32),
        jnp.zeros((seqs, heads, span), jnp.float32),
        jnp.zeros((seqs, heads, span, HEAD_DIM), jnp.float32),
    )
    best, total, accum = fold_keys(
        queries,
        query_block,
        start_state,
        (
            lax.all_gather(keys_local, "context", axis=0, tiled=True),
            lax.all_gather(values_local, "context", axis=0, tiled=True),
        ),
    )
    context = jnp.transpose(accum / total[..., None], (2, 0, 1, 3))
    log_total = best + jnp.log(total)
    context_low = context.astype(jnp.bfloat16).reshape(rows, width)
    middle = local + matmul(context_low, out_weight)
    normed_two, factor_two = normalize(middle)
    entry_two = (normed_two * norm2_gain).astype(jnp.bfloat16)
    logits = matmul(entry_two, router_weight)
    total_experts = router_weight.shape[1]
    topk = routes.shape[-1]
    capacity = rows * topk * 5 // (4 * total_experts)
    route_rows = jnp.swapaxes(routes[0], 0, 1).reshape(rows, topk)
    chosen = route_rows[:, :, None] == jnp.arange(total_experts)[None, None, :]
    chosen_float = chosen.astype(jnp.float32)
    picked = jnp.sum(chosen_float * logits[:, None, :], axis=-1)
    picked = picked - jnp.max(picked, axis=-1, keepdims=True)
    raised = jnp.exp(picked)
    gates = raised / jnp.sum(raised, axis=-1, keepdims=True)
    counts = jnp.sum(chosen.astype(jnp.int32), axis=1)
    before = jnp.cumsum(counts, axis=0) - counts
    slots = jnp.sum(chosen.astype(jnp.int32) * before[:, None, :], axis=-1)
    targets = route_rows * capacity + slots
    placing = (
        jnp.transpose(targets)[:, :, None] == jnp.arange(total_experts * capacity)[None, None, :]
    ).astype(jnp.bfloat16)
    dispatch_hot = jnp.sum(placing, axis=0)
    buffer = (
        contract("mr,md->rd", dispatch_hot, entry_two)
        .astype(jnp.bfloat16)
        .reshape(total_experts, capacity, width)
    )
    received = lax.all_to_all(buffer, "experts", split_axis=0, concat_axis=1, tiled=True)
    gate_part = contract("erd,edf->erf", received, expert_gate)
    up_part = contract("erd,edf->erf", received, expert_up)
    hidden = (gate_part * jax.nn.sigmoid(gate_part) * up_part).astype(jnp.bfloat16)
    produced = contract("erf,efd->erd", hidden, expert_down).astype(jnp.bfloat16)
    shared_gate_part = matmul(entry_two, shared_gate)
    shared_up_part = matmul(entry_two, shared_up)
    shared_hidden = (shared_gate_part * jax.nn.sigmoid(shared_gate_part) * shared_up_part).astype(
        jnp.bfloat16
    )
    shared_out = matmul(shared_hidden, shared_down)
    returned = lax.all_to_all(produced, "experts", split_axis=1, concat_axis=0, tiled=True).reshape(
        total_experts * capacity, width
    )
    picked_rows = contract("kmr,rd->kmd", placing, returned)
    mixed = jnp.sum(jnp.transpose(gates)[:, :, None] * picked_rows, axis=0)
    result = (middle + mixed + shared_out).astype(jnp.bfloat16)
    output = jnp.swapaxes(result.reshape(span, seqs, width), 0, 1)
    grad_low = jnp.swapaxes(cotangent, 0, 1).reshape(rows, width)
    grad_out = grad_low.astype(jnp.float32)
    grad_gates = jnp.transpose(jnp.sum(picked_rows * grad_out[None], axis=-1))
    grad_rows = (jnp.transpose(gates)[:, :, None] * grad_out[None]).astype(jnp.bfloat16)
    grad_slots = (
        contract("kmr,kmd->rd", placing, grad_rows)
        .astype(jnp.bfloat16)
        .reshape(total_experts, capacity, width)
    )
    grad_produced = lax.all_to_all(grad_slots, "experts", split_axis=0, concat_axis=1, tiled=True)
    expert_down_term = contract("erf,erd->efd", hidden, grad_produced)
    grad_hidden = contract("erd,efd->erf", grad_produced, expert_down)
    grad_gate_part, grad_up_part = silu_back(grad_hidden, gate_part, up_part)
    expert_gate_term = contract("erd,erf->edf", received, grad_gate_part)
    expert_up_term = contract("erd,erf->edf", received, grad_up_part)
    grad_received = (
        contract("erf,edf->erd", grad_gate_part, expert_gate)
        + contract("erf,edf->erd", grad_up_part, expert_up)
    ).astype(jnp.bfloat16)
    expert_parts = None
    shared_down_term = contract("mf,md->fd", shared_hidden, grad_low)
    grad_shared_hidden = contract("md,fd->mf", grad_low, shared_down)
    grad_shared_gate, grad_shared_up = silu_back(
        grad_shared_hidden, shared_gate_part, shared_up_part
    )
    shared_gate_term = contract("md,mf->df", entry_two, grad_shared_gate)
    shared_up_term = contract("md,mf->df", entry_two, grad_shared_up)
    grad_entry_two = contract("mf,df->md", grad_shared_gate, shared_gate) + contract(
        "mf,df->md", grad_shared_up, shared_up
    )
    grad_pick = gates * (grad_gates - jnp.sum(gates * grad_gates, axis=-1, keepdims=True))
    grad_logits = jnp.sum(chosen_float * grad_pick[:, :, None], axis=1)
    router_term = jnp.einsum(
        "md,me->de", entry_two.astype(jnp.float32), grad_logits, precision=highest
    )
    grad_entry_two = grad_entry_two + jnp.einsum(
        "me,de->md", grad_logits, router_weight.astype(jnp.float32), precision=highest
    )
    grad_returned = lax.all_to_all(
        grad_received, "experts", split_axis=1, concat_axis=0, tiled=True
    ).reshape(total_experts * capacity, width)
    grad_entry_two = grad_entry_two + contract("mr,rd->md", dispatch_hot, grad_returned)
    grad_middle_norm, norm2_term = norm_back(grad_entry_two, normed_two, factor_two, norm2_gain)
    grad_middle = grad_out + grad_middle_norm
    grad_attn = grad_middle.astype(jnp.bfloat16)
    out_term = contract("md,me->de", context_low, grad_attn)
    grad_ctx = (
        contract("me,de->md", grad_attn, out_weight)
        .astype(jnp.bfloat16)
        .reshape(span, seqs, heads, HEAD_DIM)
    )
    delta = jnp.transpose(jnp.sum(grad_ctx.astype(jnp.float32) * context, axis=-1), (1, 2, 0))
    keys_all, values_all = (
        lax.all_gather(keys_local, "context", axis=0, tiled=True),
        lax.all_gather(values_local, "context", axis=0, tiled=True),
    )
    grad_queries = query_grads(
        queries, query_block, grad_ctx, delta, log_total, keys_all, values_all
    ) * HEAD_DIM ** (-0.5)
    delta_rows = jnp.transpose(delta, (2, 0, 1))
    log_rows = jnp.transpose(log_total, (2, 0, 1))
    pull_step = partial(query_side_fold, keys_local, values_local, key_start)
    empty_grads = jnp.zeros((span, seqs, 2 * width), jnp.float32)
    grad_kv = pull_step(
        empty_grads,
        (
            lax.all_gather(queries, "context", axis=0, tiled=True),
            lax.all_gather(grad_ctx, "context", axis=0, tiled=True),
            lax.all_gather(delta_rows.astype(jnp.bfloat16), "context", axis=0, tiled=True).astype(
                jnp.float32
            ),
            lax.all_gather(log_rows.astype(jnp.bfloat16), "context", axis=0, tiled=True).astype(
                jnp.float32
            ),
        ),
        jnp.int32(0),
    )
    grad_keys = grad_kv[..., :width].reshape(span, seqs, heads, HEAD_DIM)
    grad_values = grad_kv[..., width:].reshape(span, seqs, heads, HEAD_DIM)
    grad_projected = jnp.stack(
        [
            rotate_back(grad_queries, cosine, sine),
            rotate_back(grad_keys, cosine, sine),
            grad_values,
        ],
        axis=2,
    )
    grad_projected = grad_projected.astype(jnp.bfloat16).reshape(rows, 3 * width)
    qkv_term = contract("md,me->de", entry_one, grad_projected)
    grad_entry_one = contract("me,de->md", grad_projected, qkv_weight)
    grad_local_norm, norm1_term = norm_back(grad_entry_one, normed_one, factor_one, norm1_gain)
    input_grad = jnp.swapaxes((grad_middle + grad_local_norm).reshape(span, seqs, width), 0, 1)
    expert_parts = reduce_experts(expert_gate_term, expert_up_term, expert_down_term)
    spread = (
        lax.psum_scatter(norm1_term, ("dp", "context"), scatter_dimension=0, tiled=True),
        lax.psum_scatter(qkv_term, ("dp", "context"), scatter_dimension=0, tiled=True),
        lax.psum_scatter(out_term, ("dp", "context"), scatter_dimension=0, tiled=True),
        lax.psum_scatter(norm2_term, ("dp", "context"), scatter_dimension=0, tiled=True),
        lax.psum_scatter(router_term, ("dp", "context"), scatter_dimension=0, tiled=True),
        lax.psum_scatter(shared_gate_term, ("dp", "context"), scatter_dimension=0, tiled=True),
        lax.psum_scatter(shared_up_term, ("dp", "context"), scatter_dimension=0, tiled=True),
        lax.psum_scatter(shared_down_term, ("dp", "context"), scatter_dimension=0, tiled=True),
    )
    (
        norm1_part,
        qkv_part,
        out_part,
        norm2_part,
        router_part,
        shared_gate_piece,
        shared_up_piece,
        shared_down_piece,
    ) = spread
    summed = (
        lax.psum(norm1_part.astype(jnp.bfloat16), "experts").astype(jnp.float32),
        lax.psum(qkv_part.astype(jnp.bfloat16), "experts").astype(jnp.float32),
        lax.psum(out_part.astype(jnp.bfloat16), "experts").astype(jnp.float32),
        lax.psum(norm2_part.astype(jnp.bfloat16), "experts").astype(jnp.float32),
        lax.psum(router_part.astype(jnp.bfloat16), "experts").astype(jnp.float32),
        lax.psum(shared_gate_piece.astype(jnp.bfloat16), "experts").astype(jnp.float32),
        lax.psum(shared_up_piece.astype(jnp.bfloat16), "experts").astype(jnp.float32),
        lax.psum(shared_down_piece.astype(jnp.bfloat16), "experts").astype(jnp.float32),
    )
    return (
        output,
        input_grad,
        summed[0],
        summed[1],
        summed[2],
        summed[3],
        summed[4],
        expert_parts[0],
        expert_parts[1],
        expert_parts[2],
        summed[5],
        summed[6],
        summed[7],
    )


def solution(mesh):
    return jax.shard_map(
        on_device,
        mesh=mesh,
        in_specs=(
            P(("dp", "experts"), "context", None),
            P(),
            P(),
            P(),
            P(),
            P(),
            P("experts", None, None),
            P("experts", None, None),
            P("experts", None, None),
            P(),
            P(),
            P(),
            P("context", ("dp", "experts"), None, None),
            P(("dp", "experts"), "context", None),
        ),
        out_specs=(
            P(("dp", "experts"), "context", None),
            P(("dp", "experts"), "context", None),
            P(("dp", "context")),
            P(("dp", "context"), None),
            P(("dp", "context"), None),
            P(("dp", "context")),
            P(("dp", "context"), None),
            P("experts", ("dp", "context"), None),
            P("experts", ("dp", "context"), None),
            P("experts", ("dp", "context"), None),
            P(("dp", "context"), None),
            P(("dp", "context"), None),
            P(("dp", "context"), None),
        ),
        check_vma=False,
    )
```

profile of v0, /device:TPU:0, one launch (start us, length us, event | category | flops | bytes accessed | tf_op | source)
XLA Modules:
  0.0 1229.5 jit_solution(9517427123366155983)
XLA Ops:
  8.6 5.8 copy.99
  32.0 29.7 %all-gather.5.cloned.1.call-done = bf16[1024,1,768]{0,2,1:T(8,128)(2,1)} async-done(((bf16[256,1,768]{0,2,1:T(8,128)(2,1)}), bf16[1024,1,768]{0,2,1:T(8,128)(2,1)}) %all-gather.5.cloned.1.call-update) | async-done | bytes 1572880 | tf_op jit(solution)/shard_map/all_gather | solution.py:246
  61.8 38.1 %all-gather.7.cloned.1.call-done = bf16[1024,1,768]{0,2,1:T(8,128)(2,1)} async-done(((bf16[256,1,768]{0,2,1:T(8,128)(2,1)}), bf16[1024,1,768]{0,2,1:T(8,128)(2,1)}) %all-gather.7.cloned.1.call-update) | async-done | bytes 1572880 | tf_op jit(solution)/shard_map/all_gather | solution.py:247
  101.4 15.3 %while.59 = (s32[]{:T(128)}, f32[1,12,256]{2,1,0:T(8,128)S(1)}, f32[1,12,256]{2,1,0:T(8,128)}, f32[1,12,256,64]{2,3,1,0:T(8,128)}, s32[]{:T(128)}, /*index=5*/bf...) while((s32[]{:T(128)}, f32[1,12,256]{2,1,0:T(8,128)S(1)}, ...), condition=%wide.region_7.8_spmd.clone, body=%wide.region_2.7_spmd.clone.sunk | while | flops 423647776 | bytes 27887836 | solution.py:112
  104.3 9.6 conditional.9
  151.0 5.5 multiply_convert_fusion.7
  175.2 9.5 multiply_convert_fusion.4
  184.6 6.0 convolution_convert_fusion
  197.5 5.9 fusion.145
  258.8 20.3 %all_gather.22 = bf16[1024,1,12]{0,2,1:T(8,128)(2,1)S(1)} all-gather(bf16[256,1,12]{0,2,1:T(8,128)(2,1)S(1)} %get-tuple-element.1297), channel_id=1, replica_groups=mesh['dp'=4,'context'=4,'experts'=2] {'context'}, dimensions={0}, use_global_device_ids=true | all-gather | bytes 30720 | tf_op jit(solution)/shard_map/all_gather | solution.py:369
  281.1 13.4 %all_gather.23 = bf16[1024,1,12]{0,2,1:T(8,128)(2,1)S(1)} all-gather(bf16[256,1,12]{0,2,1:T(8,128)(2,1)S(1)} %bitcast_convert_fusion.3), channel_id=1, replica_groups=mesh['dp'=4,'context'=4,'experts'=2] {'context'}, dimensions={0}, use_global_device_ids=true | all-gather | bytes 30720 | tf_op jit(solution)/shard_map/all_gather | solution.py:366
  296.1 16.5 %while.60 = (s32[]{:T(128)}, f32[256,1,12,64]{0,3,2,1:T(8,128)}, s32[]{:T(128)}, bf16[1024,1,768]{0,2,1:T(8,128)(2,1)}, bf16[256,1,12,64]{0,3,2,1:T(8,128)(2,1)S...) while((s32[]{:T(128)}, f32[256,1,12,64]{0,3,2,1:T(8,128)}, ...), condition=%wide.region_26.27_spmd.clone, body=%wide.region_23.26_spmd.clone.sunk | while | flops 615331328 | bytes 23898188 | solution.py:161
  297.3 14.0 %conditional.10 = (f32[256,1,12,64]{0,3,2,1:T(8,128)}) conditional(s32[]{:T(128)} %convert_element_type.466, f32[256,1,12,64]{0,3,2,1:T(8,128)} %get-tuple-element.1648, (s32[]{:T(128)}, pred[]{:T(512)}, bf16[1024,1,768]{0,2,1:T(8,128)(2,1)}, s32[256]{0:T(256)S(1)}, bf16[256,1,12,64]{0,3,2,1:T(8,128)(2,1)S(1)}, ...), branch_computations={%region_24.24_spmd, %region_25.25_spmd} | conditional | flops 615327744 | bytes 23893352 | solution.py:157
  304.2 7.1 fusion.38
  315.9 46.8 %while.58 = (s32[]{:T(128)}, f32[256,1,1536]{0,2,1:T(8,128)}, s32[]{:T(128)}, f32[1024,1,12]{0,2,1:T(8,128)}, f32[1024,1,12]{0,2,1:T(8,128)}, /*index=5*/bf16[10...) while((s32[]{:T(128)}, f32[256,1,1536]{0,2,1:T(8,128)}, ...), condition=%wide.region_31.32_spmd, body=%wide.region_27.31_spmd.sunk | while | flops 825307648 | bytes 32842052 | solution.py:193
  318.6 20.5 %conditional.8 = (f32[256,1,1536]{0,2,1:T(8,128)}) conditional(s32[]{:T(128)} %convert_element_type.464, f32[256,1,1536]{0,2,1:T(8,128)} %get-tuple-element.1604, (bf16[1024,1,12,64]{0,3,2,1:T(8,128)(2,1)}, s32[]{:T(128)}, s32[]{:T(128)}, s32[512]{0:T(512)S(1)}, bf16[256,1,12,64]{0,3,2,1:T(8,128)(2,1)S(1)}, /*index=5*/f32[1,12,512]{2,1,0:T(8,128)}, ...), branch_computations={%region_29.29_spmd, %region_30.30_spmd} | conditional | flops 825298944 | bytes 32741416 | solution.py:189
  324.3 7.3 fusion.60
  341.8 20.9 %conditional.8 = (f32[256,1,1536]{0,2,1:T(8,128)}) conditional(s32[]{:T(128)} %convert_element_type.464, f32[256,1,1536]{0,2,1:T(8,128)} %get-tuple-element.1604, (bf16[1024,1,12,64]{0,3,2,1:T(8,128)(2,1)}, s32[]{:T(128)}, s32[]{:T(128)}, s32[512]{0:T(512)S(1)}, bf16[256,1,12,64]{0,3,2,1:T(8,128)(2,1)S(1)}, /*index=5*/f32[1,12,512]{2,1,0:T(8,128)}, ...), branch_computations={%region_29.29_spmd, %region_30.30_spmd} | conditional | flops 825298944 | bytes 32741416 | solution.py:189
  347.5 7.4 fusion.60
  376.1 59.9 %reduce-scatter.22.cloned.1.call-done = f32[48,2048]{1,0:T(8,128)} async-done(((f32[768,2048]{1,0:T(8,128)}), f32[48,2048]{1,0:T(8,128)}) %reduce-scatter.22.cloned.1.call-update) | async-done | bytes 393232 | tf_op jit(solution)/shard_map/reduce_scatter | solution.py:397
  437.7 86.7 %reduce-scatter.24.cloned.1.call-done = f32[48,2048]{1,0:T(8,128)} async-done(((f32[768,2048]{1,0:T(8,128)}), f32[48,2048]{1,0:T(8,128)}) %reduce-scatter.24.cloned.1.call-update) | async-done | bytes 393232 | tf_op jit(solution)/shard_map/reduce_scatter | solution.py:398
  526.1 87.3 %reduce-scatter.26.cloned.1.call-done = f32[128,768]{1,0:T(8,128)} async-done(((f32[2048,768]{1,0:T(8,128)}), f32[128,768]{1,0:T(8,128)}) %reduce-scatter.26.cloned.1.call-update) | async-done | bytes 393232 | tf_op jit(solution)/shard_map/reduce_scatter | solution.py:399
  615.1 91.6 %reduce-scatter.12.cloned.1.call-done = f32[48,2304]{1,0:T(8,128)} async-done(((f32[768,2304]{1,0:T(8,128)}), f32[48,2304]{1,0:T(8,128)}) %reduce-scatter.12.cloned.1.call-update) | async-done | bytes 442384 | tf_op jit(solution)/shard_map/reduce_scatter | solution.py:393
  708.5 10.0 fusion.150
  718.6 10.1 fusion.148
  729.0 10.1 fusion.149
  744.5 21.7 %reduce-scatter.28.cloned.1.call-done = f32[48,4]{1,0:T(8,128)} async-done(((f32[768,4]{1,0:T(8,128)}), f32[48,4]{1,0:T(8,128)}) %reduce-scatter.28.cloned.1.call-update) | async-done | bytes 784
  772.1 32.4 %all-reduce.2 = (bf16[768]{0:T(1024)(128)(2,1)}, bf16[768]{0:T(1024)(128)(2,1)}) all-reduce(f32[768]{0:T(1024)} %get-tuple-element.1225, f32[768]{0:T(1024)S(1)} %copy-done.55), channel_id=2, replica_groups=mesh['dp'=4,'context'=4,'experts'=2] {'dp','context'}, use_global_device_ids=true, to_apply=%region_34.35.clone | all-reduce | flops 1536 | bytes 9216
  807.0 5.6 all-reduce.3
  827.1 118.4 %reduce-scatter.20.cloned.1.call-done = f32[2,128,768]{2,1,0:T(8,128)} async-done(((f32[2,2048,768]{2,1,0:T(8,128)}), f32[2,128,768]{2,1,0:T(8,128)}) %reduce-scatter.20.cloned.1.call-update) | async-done | bytes 786448 | tf_op jit(solution)/shard_map/reduce_scatter | solution.py:200
  945.5 138.6 %reduce-scatter.16.cloned.1.call-done = f32[2,48,2048]{2,1,0:T(8,128)} async-done(((f32[2,768,2048]{2,1,0:T(8,128)}), f32[2,48,2048]{2,1,0:T(8,128)}) %reduce-scatter.16.cloned.1.call-update) | async-done | bytes 786448 | tf_op jit(solution)/shard_map/reduce_scatter | solution.py:198
  1084.1 138.4 %reduce-scatter.18.cloned.1.call-done = f32[2,48,2048]{2,1,0:T(8,128)} async-done(((f32[2,768,2048]{2,1,0:T(8,128)}), f32[2,48,2048]{2,1,0:T(8,128)}) %reduce-scatter.18.cloned.1.call-update) | async-done | bytes 786448 | tf_op jit(solution)/shard_map/reduce_scatter | solution.py:199
  (329 shorter events, 242.8 us)
Async XLA Ops:
  7.2 143.8 %copy-start = (bf16[2048,768]{1,0:T(8,128)(2,1)S(1)}, bf16[2048,768]{1,0:T(8,128)(2,1)}, u32[]{:S(2)}) copy-start(bf16[2048,768]{1,0:T(8,128)(2,1)} %param.37) | copy-start | bytes 9437188
  7.2 54.6 %all-gather.5.cloned.1.call-start = ((), (), s32[]{:S(2)}) async-start(), calls=%async_computation.13 | async-start | bytes 1966080 | tf_op jit(solution)/shard_map/all_gather | solution.py:246
  8.6 5.8 copy-start.49
  8.6 5.8 copy-start.12
  8.6 5.8 copy-start.36
  20.1 5.9 copy-start.42
  20.1 10.1 copy-start.19
  21.2 78.7 %all-gather.7.cloned.1.call-start = ((), (), s32[]{:S(2)}) async-start(), calls=%async_computation.14 | async-start | bytes 1966080 | tf_op jit(solution)/shard_map/all_gather | solution.py:247
  23.2 291.4 %all-gather.9.cloned.1.call-start = ((), (), s32[]{:S(2)}) async-start(), calls=%async_computation.15 | async-start | bytes 1966080 | tf_op jit(solution)/shard_map/all_gather | solution.py:364
  121.1 123.5 %copy-start.5 = (bf16[256,768]{1,0:T(8,128)(2,1)}, bf16[256,768]{1,0:T(8,128)(2,1)S(1)}, u32[]{:S(2)}) copy-start(bf16[256,768]{1,0:T(8,128)(2,1)S(1)} %multiply_convert_fusion.12) | copy-start | bytes 1179652
  128.6 17.7 %all-to-all-start.2 = ((bf16[4,160,768]{2,1,0:T(8,128)(2,1)}), bf16[4,160,768]{2,1,0:T(8,128)(2,1)}, u32[]{:S(2)}, u32[]{:S(2)}) async-start(bf16[4,160,768]{2,1,0:T(8,128)(2,1)} %bitcast.334), calls=%async_computation.2 | async-start | bytes 1966080 | tf_op jit(solution)/shard_map/all_to_all | solution.py:307
  133.0 5.8 copy-start.23
  146.3 17.1 %all-to-all-start = ((bf16[4,160,768]{2,1,0:T(8,128)(2,1)}), bf16[4,160,768]{2,1,0:T(8,128)(2,1)}, u32[]{:S(2)}, u32[]{:S(2)}) async-start(bf16[4,160,768]{2,1,0:T(8,128)(2,1)} %bitcast.322), calls=%async_computation | async-start | bytes 1966080 | tf_op jit(solution)/shard_map/all_to_all | solution.py:280
  164.6 5.4 copy-start.4
  184.6 6.0 copy-start.28
  192.6 17.8 %all-to-all-start.1 = ((bf16[2,320,768]{2,0,1:T(2,128)(2,1)}), bf16[2,320,768]{2,0,1:T(2,128)(2,1)}, u32[]{:S(2)}, u32[]{:S(2)}) async-start(bf16[2,320,768]{2,0,1:T(2,128)(2,1)} %copy.103), calls=%async_computation.1 | async-start | bytes 1966080 | tf_op jit(solution)/shard_map/all_to_all | solution.py:291
  197.5 6.0 copy-start.27
  210.4 15.9 %all-to-all-start.3 = ((bf16[2,320,768]{2,0,1:T(2,128)(2,1)}), bf16[2,320,768]{2,0,1:T(2,128)(2,1)}, u32[]{:S(2)}, u32[]{:S(2)}) async-start(bf16[2,320,768]{2,0,1:T(2,128)(2,1)} %copy.107), calls=%async_computation.3 | async-start | bytes 1966080 | tf_op jit(solution)/shard_map/all_to_all | solution.py:336
  214.8 99.8 %all-gather.11.cloned.1.call-start = ((), (), s32[]{:S(2)}) async-start(), calls=%async_computation.16 | async-start | bytes 1966080 | tf_op jit(solution)/shard_map/all_gather | solution.py:365
  236.3 138.2 %reduce-scatter.14.cloned.1.call-start = ((), (), s32[]{:S(2)}) async-start(), calls=%async_computation.18 | async-start | bytes 2506752 | tf_op jit(solution)/shard_map/reduce_scatter | solution.py:394
  239.5 196.5 %reduce-scatter.22.cloned.1.call-start = ((), (), s32[]{:S(2)}) async-start(), calls=%async_computation.22 | async-start | bytes 6684672 | tf_op jit(solution)/shard_map/reduce_scatter | solution.py:397
  244.5 279.9 %reduce-scatter.24.cloned.1.call-start = ((), (), s32[]{:S(2)}) async-start(), calls=%async_computation.23 | async-start | bytes 6684672 | tf_op jit(solution)/shard_map/reduce_scatter | solution.py:398
  249.4 363.9 %reduce-scatter.26.cloned.1.call-start = ((), (), s32[]{:S(2)}) async-start(), calls=%async_computation.24 | async-start | bytes 6684672 | tf_op jit(solution)/shard_map/reduce_scatter | solution.py:399
  255.4 40.6 %copy-start.3 = (bf16[256,1,12,64]{0,3,2,1:T(8,128)(2,1)S(1)}, bf16[256,1,12,64]{0,3,2,1:T(8,128)(2,1)}, u32[]{:S(2)}) copy-start(bf16[256,1,12,64]{0,3,2,1:T(8,128)(2,1)} %get-tuple-element.1707) | copy-start | bytes 1179652
  255.4 451.3 %reduce-scatter.12.cloned.1.call-start = ((), (), s32[]{:S(2)}) async-start(), calls=%async_computation.17 | async-start | bytes 7520256 | tf_op jit(solution)/shard_map/reduce_scatter | solution.py:393
  281.0 15.0 %copy-start.41 = (f32[256,12]{0,1:T(8,128)}, f32[256,12]{0,1:T(8,128)S(1)}, u32[]{:S(2)}) copy-start(f32[256,12]{0,1:T(8,128)S(1)} %fusion.114) | copy-start | bytes 36868
  372.1 394.1 %reduce-scatter.28.cloned.1.call-start = ((), (), s32[]{:S(2)}) async-start(), calls=%async_computation.25 | async-start | bytes 417792
  374.4 444.1 %all-reduce.7.cloned.1.call-start = ((), (), s32[]{:S(2)}) async-start(), calls=%async_computation.26 | async-start | bytes 1769472 | tf_op jit(solution)/shard_map/psum | solution.py:413
  708.4 237.1 %reduce-scatter.20.cloned.1.call-start = ((), (), s32[]{:S(2)}) async-start(), calls=%async_computation.21 | async-start | bytes 13369344 | tf_op jit(solution)/shard_map/reduce_scatter | solution.py:200
  718.5 365.6 %reduce-scatter.16.cloned.1.call-start = ((), (), s32[]{:S(2)}) async-start(), calls=%async_computation.19 | async-start | bytes 13369344 | tf_op jit(solution)/shard_map/reduce_scatter | solution.py:198
  728.7 493.8 %reduce-scatter.18.cloned.1.call-start = ((), (), s32[]{:S(2)}) async-start(), calls=%async_computation.20 | async-start | bytes 13369344 | tf_op jit(solution)/shard_map/reduce_scatter | solution.py:199
  741.0 26.1 %copy-start.14 = (bf16[1,256,768]{2,1,0:T(8,128)(2,1)S(1)}, bf16[1,256,768]{2,1,0:T(8,128)(2,1)}, u32[]{:S(2)}) copy-start(bf16[1,256,768]{2,1,0:T(8,128)(2,1)} %param.26) | copy-start | bytes 1179652
  (54 other events, 127.2 us)
Sparse Core Ops, SparseCore 0:
  21.3 40.3 all-gather.4
  63.9 35.9 all-gather.6
  102.0 35.9 all-gather.8
  236.5 45.5 all-gather.10
  285.6 61.7 reduce-scatter.13
  351.7 84.2 reduce-scatter.21
  439.9 84.4 reduce-scatter.23
  528.9 84.4 reduce-scatter.25
  617.4 89.2 reduce-scatter.11
  711.0 55.1 reduce-scatter.27
  770.0 36.2 all-reduce.6
  810.7 134.7 reduce-scatter.19
  950.1 133.9 reduce-scatter.15
  1088.6 133.9 reduce-scatter.17
where the time goes:
time: 1240 us; the launch traced here: 1230 us
  waiting for transfers between devices  824 us (66%)
  matrix products  181 us (15%)
  blocking collectives  71.6 us (6%)
  other arithmetic  61.5 us (5%)
  local copies, waits for them, and re-layouts  51.9 us (4%)
  starting transfers between devices  19.3 us (2%)
  between operations  15.9 us (1%)
    dot_general x33, matrix products, contract(): return jnp.einsum(spec, left, right, preferred_element_type=jnp.float32)  163 us
    reduce_scatter x1, waiting for transfers between devices, reduce_experts(): lax.psum_scatter(gate_grad, ('dp', 'context'), scatter_dimension=1, tiled...  139 us
    reduce_scatter x1, waiting for transfers between devices, reduce_experts(): lax.psum_scatter(up_grad, ('dp', 'context'), scatter_dimension=1, tiled=T...  138 us
    reduce_scatter x1, waiting for transfers between devices, reduce_experts(): lax.psum_scatter(down_grad, ('dp', 'context'), scatter_dimension=1, tiled...  118 us
    reduce_scatter x1, waiting for transfers between devices, on_device(): lax.psum_scatter(qkv_term, ('dp', 'context'), scatter_dimension=0, tiled=...  91.6 us
    reduce_scatter x1, waiting for transfers between devices, on_device(): lax.psum_scatter(shared_down_term, ('dp', 'context'), scatter_dimension=0...  87.3 us
    reduce_scatter x1, waiting for transfers between devices, on_device(): lax.psum_scatter(shared_up_term, ('dp', 'context'), scatter_dimension=0,...  86.7 us
    reduce_scatter x1, waiting for transfers between devices, on_device(): lax.psum_scatter(shared_gate_term, ('dp', 'context'), scatter_dimension=0...  59.9 us
  transfers between devices with their start and end apart: 18, of which 13 were waited for; matrix products, arithmetic and copies ran while one was open for 22% of the time, Pallas kernels for 0%

commit v1 on v0

--- a/solution.py
+++ b/solution.py
@@ -3,11 +3,15 @@
 
 import jax
 import jax.numpy as jnp
+import numpy as np
 from jax import lax
+from jax.experimental import pallas as pl
+from jax.experimental.pallas import tpu as pltpu
 from jax.sharding import PartitionSpec as P
 
 HEAD_DIM = 64
 BLOCK = 256
+DP, CONTEXT, EXPERTS = "dp", "context", "experts"
 
 
 norm_eps = 1e-05
@@ -195,9 +199,9 @@
 
 def reduce_experts(gate_grad, up_grad, down_grad):
     return (
-        lax.psum_scatter(gate_grad, ("dp", "context"), scatter_dimension=1, tiled=True),
-        lax.psum_scatter(up_grad, ("dp", "context"), scatter_dimension=1, tiled=True),
-        lax.psum_scatter(down_grad, ("dp", "context"), scatter_dimension=1, tiled=True),
+        lax.psum_scatter(gate_grad, (DP, CONTEXT), scatter_dimension=1, tiled=True),
+        lax.psum_scatter(up_grad, (DP, CONTEXT), scatter_dimension=1, tiled=True),
+        lax.psum_scatter(down_grad, (DP, CONTEXT), scatter_dimension=1, tiled=True),
     )
 
 
@@ -221,7 +225,7 @@
     heads = width // HEAD_DIM
     rows = seqs * span
     local = jnp.swapaxes(tokens, 0, 1).reshape(rows, width).astype(jnp.float32)
-    key_start = lax.axis_index("context") * span
+    key_start = lax.axis_index(CONTEXT) * span
     positions = key_start + jnp.arange(span)
     query_block = positions // BLOCK
     cosine, sine = rotation(positions, HEAD_DIM)
@@ -243,8 +247,8 @@
         query_block,
         start_state,
         (
-            lax.all_gather(keys_local, "context", axis=0, tiled=True),
-            lax.all_gather(values_local, "context", axis=0, tiled=True),
+            lax.all_gather(keys_local, CONTEXT, axis=0, tiled=True),
+            lax.all_gather(values_local, CONTEXT, axis=0, tiled=True),
         ),
     )
     context = jnp.transpose(accum / total[..., None], (2, 0, 1, 3))
@@ -277,7 +281,7 @@
         .astype(jnp.bfloat16)
         .reshape(total_experts, capacity, width)
     )
-    received = lax.all_to_all(buffer, "experts", split_axis=0, concat_axis=1, tiled=True)
+    received = lax.all_to_all(buffer, EXPERTS, split_axis=0, concat_axis=1, tiled=True)
     gate_part = contract("erd,edf->erf", received, expert_gate)
     up_part = contract("erd,edf->erf", received, expert_up)
     hidden = (gate_part * jax.nn.sigmoid(gate_part) * up_part).astype(jnp.bfloat16)
@@ -288,7 +292,7 @@
         jnp.bfloat16
     )
     shared_out = matmul(shared_hidden, shared_down)
-    returned = lax.all_to_all(produced, "experts", split_axis=1, concat_axis=0, tiled=True).reshape(
+    returned = lax.all_to_all(produced, EXPERTS, split_axis=1, concat_axis=0, tiled=True).reshape(
         total_experts * capacity, width
     )
     picked_rows = contract("kmr,rd->kmd", placing, returned)
@@ -304,7 +308,7 @@
         .astype(jnp.bfloat16)
         .reshape(total_experts, capacity, width)
     )
-    grad_produced = lax.all_to_all(grad_slots, "experts", split_axis=0, concat_axis=1, tiled=True)
+    grad_produced = lax.all_to_all(grad_slots, EXPERTS, split_axis=0, concat_axis=1, tiled=True)
     expert_down_term = contract("erf,erd->efd", hidden, grad_produced)
     grad_hidden = contract("erd,efd->erf", grad_produced, expert_down)
     grad_gate_part, grad_up_part = silu_back(grad_hidden, gate_part, up_part)
@@ -334,7 +338,7 @@
         "me,de->md", grad_logits, router_weight.astype(jnp.float32), precision=highest
     )
     grad_returned = lax.all_to_all(
-        grad_received, "experts", split_axis=1, concat_axis=0, tiled=True
+        grad_received, EXPERTS, split_axis=1, concat_axis=0, tiled=True
     ).reshape(total_experts * capacity, width)
     grad_entry_two = grad_entry_two + contract("mr,rd->md", dispatch_hot, grad_returned)
     grad_middle_norm, norm2_term = norm_back(grad_entry_two, normed_two, factor_two, norm2_gain)
@@ -348,8 +352,8 @@
     )
     delta = jnp.transpose(jnp.sum(grad_ctx.astype(jnp.float32) * context, axis=-1), (1, 2, 0))
     keys_all, values_all = (
-        lax.all_gather(keys_local, "context", axis=0, tiled=True),
-        lax.all_gather(values_local, "context", axis=0, tiled=True),
+        lax.all_gather(keys_local, CONTEXT, axis=0, tiled=True),
+        lax.all_gather(values_local, CONTEXT, axis=0, tiled=True),
     )
     grad_queries = query_grads(
         queries, query_block, grad_ctx, delta, log_total, keys_all, values_all
@@ -361,12 +365,12 @@
     grad_kv = pull_step(
         empty_grads,
         (
-            lax.all_gather(queries, "context", axis=0, tiled=True),
-            lax.all_gather(grad_ctx, "context", axis=0, tiled=True),
-            lax.all_gather(delta_rows.astype(jnp.bfloat16), "context", axis=0, tiled=True).astype(
+            lax.all_gather(queries, CONTEXT, axis=0, tiled=True),
+            lax.all_gather(grad_ctx, CONTEXT, axis=0, tiled=True),
+            lax.all_gather(delta_rows.astype(jnp.bfloat16), CONTEXT, axis=0, tiled=True).astype(
                 jnp.float32
             ),
-            lax.all_gather(log_rows.astype(jnp.bfloat16), "context", axis=0, tiled=True).astype(
+            lax.all_gather(log_rows.astype(jnp.bfloat16), CONTEXT, axis=0, tiled=True).astype(
                 jnp.float32
             ),
         ),
@@ -389,14 +393,14 @@
     input_grad = jnp.swapaxes((grad_middle + grad_local_norm).reshape(span, seqs, width), 0, 1)
     expert_parts = reduce_experts(expert_gate_term, expert_up_term, expert_down_term)
     spread = (
-        lax.psum_scatter(norm1_term, ("dp", "context"), scatter_dimension=0, tiled=True),
-        lax.psum_scatter(qkv_term, ("dp", "context"), scatter_dimension=0, tiled=True),
-        lax.psum_scatter(out_term, ("dp", "context"), scatter_dimension=0, tiled=True),
-        lax.psum_scatter(norm2_term, ("dp", "context"), scatter_dimension=0, tiled=True),
-        lax.psum_scatter(router_term, ("dp", "context"), scatter_dimension=0, tiled=True),
-        lax.psum_scatter(shared_gate_term, ("dp", "context"), scatter_dimension=0, tiled=True),
-        lax.psum_scatter(shared_up_term, ("dp", "context"), scatter_dimension=0, tiled=True),
-        lax.psum_scatter(shared_down_term, ("dp", "context"), scatter_dimension=0, tiled=True),
+        lax.psum_scatter(norm1_term, (DP, CONTEXT), scatter_dimension=0, tiled=True),
+        lax.psum_scatter(qkv_term, (DP, CONTEXT), scatter_dimension=0, tiled=True),
+        lax.psum_scatter(out_term, (DP, CONTEXT), scatter_dimension=0, tiled=True),
+        lax.psum_scatter(norm2_term, (DP, CONTEXT), scatter_dimension=0, tiled=True),
+        lax.psum_scatter(router_term, (DP, CONTEXT), scatter_dimension=0, tiled=True),
+        lax.psum_scatter(shared_gate_term, (DP, CONTEXT), scatter_dimension=0, tiled=True),
+        lax.psum_scatter(shared_up_term, (DP, CONTEXT), scatter_dimension=0, tiled=True),
+        lax.psum_scatter(shared_down_term, (DP, CONTEXT), scatter_dimension=0, tiled=True),
     )
     (
         norm1_part,
@@ -409,14 +413,14 @@
         shared_down_piece,
     ) = spread
     summed = (
-        lax.psum(norm1_part.astype(jnp.bfloat16), "experts").astype(jnp.float32),
-        lax.psum(qkv_part.astype(jnp.bfloat16), "experts").astype(jnp.float32),
-        lax.psum(out_part.astype(jnp.bfloat16), "experts").astype(jnp.float32),
-        lax.psum(norm2_part.astype(jnp.bfloat16), "experts").astype(jnp.float32),
-        lax.psum(router_part.astype(jnp.bfloat16), "experts").astype(jnp.float32),
-        lax.psum(shared_gate_piece.astype(jnp.bfloat16), "experts").astype(jnp.float32),
-        lax.psum(shared_up_piece.astype(jnp.bfloat16), "experts").astype(jnp.float32),
-        lax.psum(shared_down_piece.astype(jnp.bfloat16), "experts").astype(jnp.float32),
+        lax.psum(norm1_part.astype(jnp.bfloat16), EXPERTS).astype(jnp.float32),
+        lax.psum(qkv_part.astype(jnp.bfloat16), EXPERTS).astype(jnp.float32),
+        lax.psum(out_part.astype(jnp.bfloat16), EXPERTS).astype(jnp.float32),
+        lax.psum(norm2_part.astype(jnp.bfloat16), EXPERTS).astype(jnp.float32),
+        lax.psum(router_part.astype(jnp.bfloat16), EXPERTS).astype(jnp.float32),
+        lax.psum(shared_gate_piece.astype(jnp.bfloat16), EXPERTS).astype(jnp.float32),
+        lax.psum(shared_up_piece.astype(jnp.bfloat16), EXPERTS).astype(jnp.float32),
+        lax.psum(shared_down_piece.astype(jnp.bfloat16), EXPERTS).astype(jnp.float32),
     )
     return (
         output,
@@ -435,40 +439,1111 @@
     )
 
 
+group = (DP, EXPERTS)
+keep_masks = (0, 1, 4, 5)
+all_masks = keep_masks + tuple(mask ^ 2 for mask in keep_masks)
+f32 = jnp.float32
+bf16 = jnp.bfloat16
+far, copied, held = range(3)
+
+
+def dot_nn(left, right):
+    return lax.dot_general(left, right, (((1,), (0,)), ((), ())), preferred_element_type=f32)
+
+
+def dot_nt(left, right):
+    return lax.dot_general(left, right, (((1,), (1,)), ((), ())), preferred_element_type=f32)
+
+
+def dot_tn(left, right):
+    return lax.dot_general(left, right, (((0,), (0,)), ((), ())), preferred_element_type=f32)
+
+
+def spin(field, cosine, sine_up, sine_down):
+    up = pltpu.roll(field, 32, 1)
+    down = pltpu.roll(field, 96, 1)
+    return field * cosine + up * sine_up + down * sine_down
+
+
+def spin_back(grad, cosine, sine_up, sine_down):
+    up = pltpu.roll(grad, 32, 1)
+    down = pltpu.roll(grad, 96, 1)
+    return grad * cosine - up * sine_up - down * sine_down
+
+
+def spin_tables(length):
+    lane = np.arange(128)
+    freqs = 10000.0 ** (-2.0 * (lane % 32) / HEAD_DIM)
+    angles = np.arange(length)[:, None] * freqs[None, :]
+    second = (lane % HEAD_DIM) >= HEAD_DIM // 2
+    sine = np.sin(angles)
+    tables = (np.cos(angles), np.where(second, sine, 0.0), np.where(second, 0.0, -sine))
+    return [jnp.asarray(table, f32) for table in tables]
+
+
+def lane_half(rows):
+    return lax.broadcasted_iota(jnp.int32, (rows, 128), 1) // HEAD_DIM
+
+
+def key_bias(blocks, rows, here):
+    block = lax.broadcasted_iota(jnp.int32, (1, blocks * rows), 1) // rows
+    return jnp.where(block <= here, 0.0, masked_score)
+
+
+class Copies:
+    def __init__(self, sems):
+        self.sems, self.count = sems, 0
+
+    def start(self, source, target):
+        copy = pltpu.make_async_copy(source, target, self.sems.at[self.count])
+        self.count += 1
+        copy.start()
+        return copy
+
+
+def attend_kernel(blocks, place, *refs):
+    tokens = refs[:blocks]
+    (routes, gain1, qkv_w, out_w, gain2, cos_hbm, up_hbm, down_hbm) = refs[blocks:blocks + 8]
+    (entry_hbm, queries_hbm, keys_hbm, values_hbm, log_hbm, context_hbm, middle, entry_two) = refs[
+        blocks + 8:blocks + 16
+    ]
+    (cos, sin_up, sin_down, entry, queries, keys, values, log_total, context, sems) = refs[blocks + 16:]
+    rows, width = middle.shape
+    pairs = width // 128
+    here = place[0]
+    copies = Copies(sems)
+    tables_in = []
+    for r in range(blocks):
+        block = pl.ds(pl.multiple_of(jnp.maximum(here - r, 0) * rows, rows), rows)
+        for source, target in ((cos_hbm, cos), (up_hbm, sin_up), (down_hbm, sin_down)):
+            tables_in.append(copies.start(source.at[block], target.at[r * rows:(r + 1) * rows]))
+
+    for r in range(blocks):
+        x = tokens[r][...].astype(f32)
+        factor = lax.rsqrt(jnp.mean(x * x, axis=-1, keepdims=True) + norm_eps)
+        entry[r * rows:(r + 1) * rows, :] = (x * factor * gain1[...]).astype(bf16)
+    outs = [copies.start(entry, entry_hbm)]
+    for copy in tables_in:
+        copy.wait()
+
+    tile = 384
+    for start in range(0, width, tile):
+        part = dot_nn(entry[:rows, :], qkv_w[:, start:start + tile])
+        for lane in range(0, tile, 128):
+            queries[:, start + lane:start + lane + 128] = spin(
+                part[:, lane:lane + 128], cos[:rows, :], sin_up[:rows, :], sin_down[:rows, :]
+            ).astype(bf16)
+    for start in range(0, width, tile):
+        part = dot_nn(entry[...], qkv_w[:, width + start:width + start + tile])
+        for lane in range(0, tile, 128):
+            keys[:, start + lane:start + lane + 128] = spin(
+                part[:, lane:lane + 128], cos[...], sin_up[...], sin_down[...]
+            ).astype(bf16)
+        values[:, start:start + tile] = dot_nn(
+            entry[...], qkv_w[:, 2 * width + start:2 * width + start + tile]
+        ).astype(bf16)
+    outs += [copies.start(queries, queries_hbm), copies.start(keys, keys_hbm), copies.start(values, values_hbm)]
+    half = lane_half(rows)
+    bias = key_bias(blocks, rows, here)
+
+    def attend(pair, carry):
+        lanes = pl.ds(pl.multiple_of(pair * 128, 128), 128)
+        both = queries[:, lanes] * HEAD_DIM ** (-0.5)
+        results, logs = [], []
+        for head in range(2):
+            query = jnp.where(half == head, both, jnp.zeros_like(both))
+            scores = dot_nt(query, keys[:, lanes]) + bias
+            best = jnp.max(scores, axis=-1, keepdims=True)
+            weights = jnp.exp(scores - best)
+            total = jnp.sum(weights, axis=-1, keepdims=True)
+            results.append(dot_nn(weights.astype(bf16), values[:, lanes]) / total)
+            logs.append(best + jnp.log(total))
+        context[:, lanes] = jnp.where(half == 0, results[0], results[1]).astype(bf16)
+        log_total[pair] = jnp.where(half == 0, logs[0], logs[1])
+        return carry
+
+    lax.fori_loop(0, pairs, attend, 0)
+    outs += [copies.start(log_total, log_hbm), copies.start(context, context_hbm)]
+    mid = tokens[0][...].astype(f32) + dot_nn(context[...], out_w[...])
+    middle[...] = mid
+    factor = lax.rsqrt(jnp.mean(mid * mid, axis=-1, keepdims=True) + norm_eps)
+    entry_two[:rows, :] = (mid * factor * gain2[...]).astype(bf16)
+    entry_two[rows:, :] = jnp.zeros((entry_two.shape[0] - rows, width), bf16)
+    entry_two[rows:rows + 8, :rows] = jnp.concatenate(
+        [routes[...].astype(f32), jnp.zeros((8 - routes.shape[0], rows), f32)], axis=0
+    ).astype(bf16)
+    for copy in outs:
+        copy.wait()
+
+
+def pick_kernel(n_context, place, gate, up, down, gate_out, up_out, down_out):
+    side = place[5]
+    lane = lax.broadcasted_iota(jnp.int32, (gate.shape[0], 128), 1)
+    for source, target in ((gate, gate_out), (up, up_out)):
+        for z in range(0, n_context, 2):
+            one = source[:, z * 128:(z + 1) * 128].astype(f32)
+            two = source[:, (z + 1) * 128:(z + 2) * 128].astype(f32)
+            left = jnp.where(side == 0, one, pltpu.roll(one, 64, 1))
+            right = jnp.where(side == 0, pltpu.roll(two, 64, 1), two)
+            target[:, z * 64:z * 64 + 128] = jnp.where(lane < 64, left, right).astype(bf16)
+    for z in range(n_context):
+        start = pl.multiple_of(z * 128 + side * 64, 64)
+        down_out[z * 64:(z + 1) * 64, :] = down[pl.ds(start, 64), :]
+
+
+def sum_kernel(n_context, counts, place, *refs):
+    outs = refs[-n_context:]
+    here = place[6]
+    piece = outs[0].shape[0]
+    for r, out in enumerate(outs):
+        block = lax.rem(here + r, n_context)
+        rows = pl.ds(pl.multiple_of(block * piece, piece), piece)
+        first, start = 0, 0
+        for count in counts:
+            total = refs[first][rows, :].astype(f32)
+            for value in refs[first + 1:first + count]:
+                total = total + value[rows, :].astype(f32)
+            out[:, start:start + total.shape[1]] = total.astype(bf16)
+            first, start = first + count, start + total.shape[1]
+
+
+def silu_parts(gate_part, up_part):
+    sigmoid_value = jax.nn.sigmoid(gate_part)
+    active = gate_part * sigmoid_value
+    return sigmoid_value, active, (active * up_part).astype(bf16)
+
+
+def silu_grads(grad_hidden, gate_part, up_part, sigmoid_value, active):
+    grad_gate = grad_hidden * up_part * sigmoid_value * (1.0 + gate_part * (1.0 - sigmoid_value))
+    return grad_gate.astype(bf16), (grad_hidden * active).astype(bf16)
+
+
+def run_through(x_all, dz_all, weights, produced, received, hidden, dgate, dup):
+    gate_w, up_w, down_w = weights
+    tile = x_all.shape[0] // 2
+    for t in range(2):
+        rows = slice(t * tile, (t + 1) * tile)
+        gate_part = dot_nn(x_all[rows, :], gate_w[...])
+        up_part = dot_nn(x_all[rows, :], up_w[...])
+        sigmoid_value, active, u = silu_parts(gate_part, up_part)
+        hidden[rows, :] = u
+        out = dot_nn(u, down_w[...])
+        grad_hidden = dot_nt(dz_all[rows, :], down_w[...])
+        da, db = silu_grads(grad_hidden, gate_part, up_part, sigmoid_value, active)
+        dgate[rows, :] = da
+        dup[rows, :] = db
+        grad = dot_nt(da, gate_w[...]) + dot_nt(db, up_w[...])
+        produced[rows, :] = out.astype(produced.dtype)
+        received[rows, :] = grad.astype(received.dtype)
+
+
+def run_weights(copies, sources, targets, core, chip, run):
+    gate_hbm, up_hbm, down_hbm = sources
+    gate_w, up_w, down_w = targets
+    columns = gate_w.shape[1]
+    part = pl.ds(pl.multiple_of((2 * chip + run) * columns, columns), columns)
+    return [
+        copies.start(gate_hbm.at[core, :, part], gate_w),
+        copies.start(up_hbm.at[core, :, part], up_w),
+        copies.start(down_hbm.at[core, part, :], down_w),
+    ]
+
+
+def enter_kernel(masks, n_context, n_dp, layout, place, *refs):
+    inputs = refs[:8]
+    (cot_hbm, router, gate_hbm, up_hbm, down_hbm) = refs[8:13]
+    outs_hbm, bundle = refs[13:17], refs[17]
+    (aux, hots, produced, received) = kept = refs[18:22]
+    (x_all, dz_all, field, cot, gate_w, up_w, down_w, hidden, dgate, dup, notes, sems) = refs[22:]
+    index, dp, expert, core, chip = place[0], place[1], place[2], place[3], place[4]
+    rows = cot.shape[0] // 8
+    slots = hots.shape[1]
+    copies = Copies(sems)
+    ins = []
+    for i in range(8):
+        rows_of = slice(i * rows, (i + 1) * rows)
+        ins.append((
+            copies.start(inputs[i].at[rows:], notes.at[i]),
+            copies.start(inputs[i].at[:rows], field.at[rows_of]),
+            copies.start(cot_hbm.at[lax.bitwise_xor(index, masks[i])], cot.at[rows_of]),
+        ))
+    weights = (gate_w, up_w, down_w)
+    weights_in = run_weights(copies, (gate_hbm, up_hbm, down_hbm), weights, core, chip, 0)
+
+    lanes = lax.broadcasted_iota(jnp.int32, (slots, 128), 1)
+    mine = (lanes == expert).astype(f32)
+    expert_row = expert.astype(f32)
+    before = (
+        lax.broadcasted_iota(jnp.int32, (rows, rows), 0) < lax.broadcasted_iota(jnp.int32, (rows, rows), 1)
+    ).astype(bf16)
+    slot_of = lax.broadcasted_iota(jnp.int32, (slots, rows), 0).astype(f32)
+    for i in range(8):
+        rows_of = slice(i * rows, (i + 1) * rows)
+        slots_of = slice(i * slots, (i + 1) * slots)
+        if i % 4 == 0:
+            for copy in sum(ins[i:i + 4], ()):
+                copy.wait()
+        routes = notes[i, :, :rows].astype(f32)
+        first, second = routes[0:1, :], routes[1:2, :]
+        named = jnp.logical_or(first == expert_row, second == expert_row).astype(f32)
+        slot = dot_nn(jnp.broadcast_to(named, (16, rows)).astype(bf16), before)[0:1, :]
+        hot_f = jnp.where(slot_of == slot, named, 0.0)
+        partner = jnp.where(first == expert_row, second, first)
+        other = jnp.sum(hot_f * partner, axis=-1, keepdims=True)
+        hot = hot_f.astype(bf16)
+        hots[i] = hot
+        x = dot_nn(hot, field[rows_of, :]).astype(bf16)
+        x_all[slots_of, :] = x
+        g_slot = dot_nn(hot, cot[rows_of, :])
+        logits = dot_nn(x, router[...])
+        theirs = (lanes.astype(f32) == other).astype(f32)
+        gate = jax.nn.sigmoid(jnp.sum((mine - theirs) * logits, axis=-1, keepdims=True))
+        dz_all[slots_of, :] = (gate * g_slot).astype(bf16)
+        aux[slots_of, :] = jnp.where(lanes == 64, gate, gate * (1.0 - gate) * (mine - theirs))
+    outs = [copies.start(source, target) for source, target in zip(kept[:2], outs_hbm[:2])]
+
+    for copy in weights_in:
+        copy.wait()
+    run_through(x_all, dz_all, weights, produced, received, hidden, dgate, dup)
+    outs += [copies.start(source, target) for source, target in zip(kept[2:], outs_hbm[2:])]
+    expert_grads(
+        bundle, x_all, dz_all, hidden, dgate, dup, 0, n_dp * layout.run_place, layout.run_place, dp, n_context, n_dp
+    )
+    for copy in outs:
+        copy.wait()
+
+
+def leave_kernel(masks, n_context, n_dp, layout, place, *refs):
+    kept_hbm, inputs, cot_hbm = refs[:4], refs[4:12], refs[12]
+    (router_t, gate_s_hbm, up_s_hbm, down_s_hbm, gate_hbm, up_hbm, down_hbm) = refs[13:20]
+    (grad_keep_hbm, grad_send_hbm, mix_keep_hbm, mix_send_hbm, router_grad, bundle) = refs[20:26]
+    (aux, hots, produced0, received0) = kept = refs[26:30]
+    (
+        x_all, dz_all, g_all, produced, received, field, cot, gate_w, up_w, down_w, gate_s_w, up_s_w, down_s_w,
+        hidden, dgate, dup, hidden_s, dgate_s, dup_s, grad_tokens, mix_tokens, slot_out, sems,
+    ) = refs[30:]
+    index, dp, core, chip = place[0], place[1], place[3], place[4]
+    rows = cot.shape[0] // 8
+    width = field.shape[1]
+    slots = hots.shape[1]
+    copies = Copies(sems)
+    kept_in = [copies.start(source, target) for source, target in zip(kept_hbm[:2], kept[:2])]
+    ins = []
+    for i in range(8):
+        rows_of = slice(i * rows, (i + 1) * rows)
+        ins.append((
+            copies.start(inputs[i].at[:rows], field.at[rows_of]),
+            copies.start(cot_hbm.at[lax.bitwise_xor(index, masks[i])], cot.at[rows_of]),
+        ))
+    weights = (gate_w, up_w, down_w)
+    weights_in = run_weights(copies, (gate_hbm, up_hbm, down_hbm), weights, core, chip, 1)
+    shared_in = [
+        copies.start(source, target)
+        for source, target in (
+            (gate_s_hbm, gate_s_w), (up_s_hbm, up_s_w), (down_s_hbm, down_s_w), *zip(kept_hbm[2:], kept[2:])
+        )
+    ]
+    for copy in kept_in:
+        copy.wait()
+    for i in range(8):
+        rows_of = slice(i * rows, (i + 1) * rows)
+        slots_of = slice(i * slots, (i + 1) * slots)
+        for copy in ins[i]:
+            copy.wait()
+        x_all[slots_of, :] = dot_nn(hots[i], field[rows_of, :]).astype(bf16)
+        g_slot = dot_nn(hots[i], cot[rows_of, :])
+        g_all[slots_of, :] = g_slot.astype(bf16)
+        dz_all[slots_of, :] = (aux[slots_of, 64:65] * g_slot).astype(bf16)
+    for copy in weights_in:
+        copy.wait()
+    run_through(x_all, dz_all, weights, produced, received, hidden, dgate, dup)
+
+    for copy in shared_in:
+        copy.wait()
+    z = produced[...] + produced0[...].astype(f32)
+    gate = aux[:, 64:65]
+    pick = jnp.sum(z.astype(bf16).astype(f32) * g_all[...].astype(f32), axis=-1, keepdims=True)
+    lanes = lax.broadcasted_iota(jnp.int32, aux.shape, 1)
+    dlogits = (jnp.where(lanes < 64, aux[...], 0.0) * pick).astype(bf16)
+    slot_out[:, width:] = (gate * z).astype(bf16)
+    grad = received[...] + received0[...].astype(f32)
+    slot_out[:, :width] = (grad + dot_nn(dlogits, router_t[...])).astype(bf16)
+    router_grad[...] = dot_tn(x_all[...], dlogits)
+    outs = []
+    for t in range(4):
+        tile = slice(2 * t * rows, 2 * (t + 1) * rows)
+        gate_part = dot_nn(field[tile, :], gate_s_w[...])
+        up_part = dot_nn(field[tile, :], up_s_w[...])
+        sigmoid_value, active, u = silu_parts(gate_part, up_part)
+        hidden_s[tile, :] = u
+        mixed = dot_nn(u, down_s_w[...])
+        grad_hidden = dot_nt(cot[tile, :], down_s_w[...])
+        da, db = silu_grads(grad_hidden, gate_part, up_part, sigmoid_value, active)
+        dgate_s[tile, :] = da
+        dup_s[tile, :] = db
+        grad_in = dot_nt(da, gate_s_w[...]) + dot_nt(db, up_s_w[...])
+        for half in range(2):
+            i = 2 * t + half
+            rows_of = slice(half * rows, (half + 1) * rows)
+            back = dot_tn(hots[i], slot_out[i * slots:(i + 1) * slots, :])
+            grad_tokens[i] = (grad_in[rows_of, :] + back[:, :width]).astype(bf16)
+            mix_tokens[i] = (mixed[rows_of, :] + back[:, width:]).astype(bf16)
+        for i in (2 * t, 2 * t + 1):
+            for source, targets in (
+                (grad_tokens, (grad_keep_hbm, grad_send_hbm)), (mix_tokens, (mix_keep_hbm, mix_send_hbm))
+            ):
+                outs.append(copies.start(source.at[i], targets[i // 4].at[i % 4]))
+
+    every = slice(None)
+    shared_place, run_place = layout.shared_place, layout.run_place
+    slab_rows = shared_place + run_place
+    for mat, source in enumerate((dgate_s, dup_s)):
+        offset = mat * layout.shared_blocks * layout.piece
+        matrix_grads(bundle, field, source, offset, slab_rows, dp, n_context, n_dp)
+    grad = dot_tn(hidden_s[...], cot[...]).astype(bf16)
+    down_rows = layout.down_rows
+    total_rows = bundle.shape[0] // n_context
+    for z in range(n_context):
+        for lane in range(width // 128):
+            start = z * total_rows + n_dp * slab_rows + lane * down_rows
+            bundle[start:start + down_rows, :] = grad[z * down_rows:(z + 1) * down_rows, lane * 128:(lane + 1) * 128]
+    expert_grads(
+        bundle, x_all, dz_all, hidden, dgate, dup, shared_place, total_rows - width, slab_rows, dp, n_context, n_dp
+    )
+    for copy in outs:
+        copy.wait()
+
+
+def store_grads(bundle, grad, part, offset, place_rows, dp, n_context, piece):
+    total_rows = bundle.shape[0] // n_context
+    slab = lax.bitwise_xor(part, dp) * place_rows
+    for z in range(n_context):
+        for lane in range(grad.shape[1] // 128):
+            start = z * total_rows + slab + offset + lane * piece
+            bundle[pl.ds(pl.multiple_of(start, 16), piece), :] = grad[
+                z * piece:(z + 1) * piece, lane * 128:(lane + 1) * 128
+            ]
+
+
+def matrix_grads(bundle, left, right, offset, place_rows, dp, n_context, n_dp):
+    block = left.shape[1] // n_dp
+    tile = 2 * block
+    for t in range(n_dp // 2):
+        grad = dot_tn(left[:, t * tile:(t + 1) * tile], right[...]).astype(bf16)
+        for half in range(2):
+            store_grads(
+                bundle, grad[half * block:(half + 1) * block], 2 * t + half, offset, place_rows, dp, n_context,
+                block // n_context,
+            )
+
+
+def expert_grads(bundle, x, dz, hidden, dgate, dup, offset, down_at, place_rows, dp, n_context, n_dp):
+    width, columns = x.shape[1], hidden.shape[1]
+    tile = 2 * width // n_dp
+    total_rows = bundle.shape[0] // n_context
+    for mat, source in enumerate((dgate, dup)):
+        matrix_grads(
+            bundle, x, source, offset + mat * (columns // 128) * (width // n_dp // n_context), place_rows, dp,
+            n_context, n_dp,
+        )
+    for t in range(n_dp // 2):
+        grad = dot_tn(dz[:, t * tile:(t + 1) * tile], hidden[...]).astype(bf16)
+        for z in range(n_context):
+            start = z * total_rows + down_at + t * tile
+            bundle[start:start + tile, :] = grad[:, z * 128:(z + 1) * 128]
+
+
+class Layout:
+    def __init__(self, width, hidden, n_dp, n_context):
+        self.piece = width // n_dp // n_context
+        self.shared_blocks, self.blocks = hidden // 8 // 128, hidden // 4 // 128
+        self.shared_place = 2 * self.shared_blocks * self.piece
+        self.run_place = 2 * self.blocks * self.piece
+        self.down_rows = hidden // 8 // n_context
+        self.shared_down = self.down_rows * (width // 128)
+
+
+def feed_grads_kernel(n_dp, layout, place, *refs):
+    refs = list(refs)
+
+    def take(count):
+        part = refs[:count]
+        del refs[:count]
+        return part
+
+    runs = [take(n_dp), take(n_dp)]
+    shared_far = take(n_dp)
+    downs, got_downs = take(2), take(2)
+    (gate, up, down, gate_s, up_s, down_s) = refs
+    dp, side = place[1], place[5]
+    core = place[3]
+    piece = layout.piece
+    hidden = gate.shape[2]
+    columns = layout.blocks * 128
+    width = down.shape[2]
+
+    for mask in range(n_dp):
+        source = lax.bitwise_xor(dp, mask)
+        which = lax.bitwise_and(source, 1)
+        for run in range(2):
+            begin = (source // 2) * (2 * columns) + run * columns
+            for mat, target in enumerate((gate, up)):
+                for lane in range(layout.blocks):
+                    start = run * layout.shared_place + (mat * layout.blocks + lane) * piece
+                    target[which, :, pl.ds(pl.multiple_of(begin + lane * 128, 128), 128)] = runs[run][mask][
+                        start:start + piece, :
+                    ].astype(f32)
+    shared_down = layout.shared_down
+    kept = jnp.where(core == 0, downs[0][...], downs[1][shared_down:, :])
+    got = jnp.where(core == 0, got_downs[0][...], got_downs[1][...])
+    down[core] = kept.astype(f32).T
+    down[1 - core] = got.astype(f32).T
+
+    lane_of = lax.broadcasted_iota(jnp.int32, (piece, 128), 1)
+    for mask in range(n_dp):
+        source = lax.bitwise_xor(dp, mask)
+        for mat, target in enumerate((gate_s, up_s)):
+            for lane in range(layout.shared_blocks):
+                start = (mat * layout.shared_blocks + lane) * piece
+                own = runs[1][mask][start:start + piece, :].astype(f32)
+                far = shared_far[mask][start:start + piece, :].astype(f32)
+                first = jnp.where(side == 0, own, far)
+                second = jnp.where(side == 0, far, own)
+                begin = source * (hidden // n_dp) + lane * 256
+                target[:, pl.ds(pl.multiple_of(begin, 128), 128)] = jnp.where(
+                    lane_of < 64, first, pltpu.roll(second, 64, 1)
+                )
+                target[:, pl.ds(pl.multiple_of(begin + 128, 128), 128)] = jnp.where(
+                    lane_of < 64, pltpu.roll(first, 64, 1), second
+                )
+    down_rows = layout.down_rows
+    for lane in range(width // 128):
+        rows = slice(lane * down_rows, (lane + 1) * down_rows)
+        far_rows = slice(layout.shared_place + rows.start, layout.shared_place + rows.stop)
+        lanes = slice(lane * 128, (lane + 1) * 128)
+        down_s[pl.ds(pl.multiple_of(side * down_rows, 16), down_rows), lanes] = downs[1][rows, :].astype(f32)
+        down_s[pl.ds(pl.multiple_of((1 - side) * down_rows, 16), down_rows), lanes] = shared_far[0][
+            far_rows, :
+        ].astype(f32)
+
+
+def last_kernel(blocks, place, *refs):
+    packs, (token, gain1, grad_own, grad_middle) = refs[:2], refs[2:6]
+    pulled = refs[6:5 + blocks]
+    (input_grad, qkv, out, norm1, norm2, router) = refs[5 + blocks:]
+    side = place[5]
+    piece, width = out.shape
+    own, far_half = packs[0][...].astype(f32), packs[1][...].astype(f32)
+    whole, start = [], 0
+    for columns in ((3 * width // 2 + width + 128) // 2, (3 * width // 2 + 128) // 2):
+        here, there = own[:, start:start + columns], far_half[:, start:start + columns]
+        whole.append(jnp.concatenate([jnp.where(side == 0, here, there), jnp.where(side == 0, there, here)], axis=1))
+        start += columns
+    tile = width // 2
+    for mat in range(3):
+        for half in range(2):
+            qkv[:, mat * width + half * tile:mat * width + (half + 1) * tile] = whole[half][
+                :, mat * tile:(mat + 1) * tile
+            ]
+    out[...] = whole[0][:, 3 * tile:3 * tile + width]
+    small = whole[1][:, 3 * tile:3 * tile + 128]
+    small = jnp.concatenate([small, jnp.zeros((128 - piece, 128), f32)], axis=0).T
+    router[...] = small[:router.shape[0], :piece]
+    norm2[...] = small[8:9, :piece]
+    norm1[...] = small[9:10, :piece]
+
+    x = token[...].astype(f32)
+    factor = lax.rsqrt(jnp.mean(x * x, axis=-1, keepdims=True) + norm_eps)
+    normed = x * factor
+    grad_entry = grad_own[...]
+    for part in pulled:
+        grad_entry = grad_entry + part[...].astype(f32)
+    grad_norm = grad_entry * gain1[...]
+    inner = jnp.mean(grad_norm * normed, axis=-1, keepdims=True)
+    input_grad[...] = grad_middle[...] + factor * (grad_norm - normed * inner)
+
+
+def load_turns(copies, sources, targets, blocks, rows, here):
+    started = []
+    for r in range(blocks):
+        block = pl.ds(pl.multiple_of(jnp.maximum(here - r, 0) * rows, rows), rows)
+        for source, target in zip(sources, targets):
+            started.append(copies.start(source.at[block], target.at[r * rows:(r + 1) * rows]))
+    return started
+
+
+def attend_back(first, pairs, bias, queries, keys, values, log_total, grad_ctx, turns, grad_q, grad_kv):
+    cos, sin_up, sin_down = turns
+    rows = queries.shape[0]
+    width = queries.shape[1]
+    scale = HEAD_DIM ** (-0.5)
+    half = lane_half(rows)
+
+    def attend(pair, carry):
+        lanes = pl.ds(pl.multiple_of(pair * 128, 128), 128)
+        both_q = queries[:, lanes] * scale
+        both_g = grad_ctx[:, pl.ds(pl.multiple_of((first + pair) * 128, 128), 128)]
+        both_l = log_total[pair]
+        dq = dk = dv = None
+        for head in range(2):
+            query = jnp.where(half == head, both_q, jnp.zeros_like(both_q))
+            grad = jnp.where(half == head, both_g, jnp.zeros_like(both_g))
+            log_row = both_l[:, head * HEAD_DIM:head * HEAD_DIM + 1]
+            prob = jnp.exp(dot_nt(query, keys[:, lanes]) + bias - log_row)
+            grad_prob = dot_nt(grad, values[:, lanes])
+            delta = jnp.sum(prob * grad_prob, axis=-1, keepdims=True)
+            grad_score = (prob * (grad_prob - delta)).astype(bf16)
+            dq_head = dot_nn(grad_score, keys[:, lanes])
+            dk_head = dot_tn(grad_score, query)
+            dv_head = dot_tn(prob.astype(bf16), grad)
+            if head == 0:
+                dq, dk, dv = dq_head, dk_head, dv_head
+            else:
+                dq, dk, dv = jnp.where(half == 0, dq, dq_head), dk + dk_head, dv + dv_head
+        grad_q[:, lanes] = spin_back(dq * scale, cos[:rows, :], sin_up[:rows, :], sin_down[:rows, :]).astype(bf16)
+        far_lanes = pl.ds(pl.multiple_of(width + pair * 128, 128), 128)
+        grad_kv[:, lanes] = spin_back(dk, cos[...], sin_up[...], sin_down[...]).astype(bf16)
+        grad_kv[:, far_lanes] = dv.astype(bf16)
+        return carry
+
+    lax.fori_loop(0, pairs, attend, 0)
+
+
+def store_pack(keep, send, value, start, dp, side, n_dp):
+    n_half = keep.shape[-1]
+    block = value.shape[0] // n_dp
+    if start < n_half < start + value.shape[1]:
+        store_pack(keep, send, value[:, :n_half - start], start, dp, side, n_dp)
+        store_pack(keep, send, value[:, n_half - start:], n_half, dp, side, n_dp)
+        return
+    side_of = start // n_half
+    lanes = slice(start - side_of * n_half, start - side_of * n_half + value.shape[1])
+    flip_side = lax.bitwise_xor(side_of, side)
+    for part in range(n_dp):
+        piece = value[part * block:(part + 1) * block, :].astype(bf16)
+        flip = lax.bitwise_xor(part, dp)
+
+        @pl.when(lax.bitwise_and(flip, 1) == 0)
+        def _():
+            keep[flip // 2, flip_side, :, lanes] = piece
+
+        @pl.when(lax.bitwise_and(flip, 1) == 1)
+        def _():
+            send[flip // 2, flip_side, :, lanes] = piece
+
+
+def back_kernel(blocks, n_dp, place, *refs):
+    parts = refs[:4]
+    (
+        middle, cot, gain2, out_w, queries_hbm, keys_hbm, values_hbm, log_hbm, context_hbm, entry_hbm, *turns_hbm
+    ) = refs[4:17]
+    (grad_middle, grad_ctx, grad_q, grad_kv, notes, keep, send) = refs[17:24]
+    (queries, keys, values, log_total, context, entry, cos, sin_up, sin_down, sems) = refs[24:]
+    rows, width = middle.shape
+    here, dp, side = place[6], place[1], place[5]
+    copies = Copies(sems)
+    part = slice(0, queries.shape[1])
+    turns = (cos, sin_up, sin_down)
+    first_in = [
+        copies.start(source, target)
+        for source, target in (
+            (queries_hbm.at[:, part], queries), (keys_hbm.at[:, part], keys), (values_hbm.at[:, part], values),
+            (log_hbm.at[:log_total.shape[0]], log_total),
+        )
+    ]
+    first_in += load_turns(copies, turns_hbm, turns, blocks, rows, here)
+    late_in = [copies.start(context_hbm, context), copies.start(entry_hbm, entry)]
+
+    grad_two = parts[0][...].astype(f32)
+    for value in parts[1:]:
+        grad_two = grad_two + value[...].astype(f32)
+    mid = middle[...]
+    factor = lax.rsqrt(jnp.mean(mid * mid, axis=-1, keepdims=True) + norm_eps)
+    normed = mid * factor
+    notes[...] = jnp.zeros_like(notes)
+    notes[0:1, :] = jnp.sum(grad_two * normed, axis=0, keepdims=True)
+    grad_norm = grad_two * gain2[...]
+    inner = jnp.mean(grad_norm * normed, axis=-1, keepdims=True)
+    grad_mid = cot[...].astype(f32) + factor * (grad_norm - normed * inner)
+    grad_middle[...] = grad_mid
+    grad_attn = grad_mid.astype(bf16)
+    grad_ctx[...] = dot_nt(grad_attn, out_w[...]).astype(bf16)
+    for copy in first_in:
+        copy.wait()
+    attend_back(
+        0, log_total.shape[0], key_bias(blocks, rows, here), queries, keys, values, log_total, grad_ctx, turns, grad_q,
+        grad_kv,
+    )
+    for copy in late_in:
+        copy.wait()
+    tile = queries.shape[1]
+    store_pack(keep, send, dot_tn(entry[:rows, :], grad_q[...]), 0, dp, side, n_dp)
+    for mat in range(2):
+        grad = dot_tn(entry[...], grad_kv[:, mat * tile:(mat + 1) * tile])
+        store_pack(keep, send, grad, (1 + mat) * tile, dp, side, n_dp)
+    for start in range(0, width, tile):
+        store_pack(keep, send, dot_tn(context[...], grad_attn[:, start:start + tile]), 3 * tile + start, dp, side, n_dp)
+    used = 3 * tile + width
+    store_pack(keep, send, jnp.zeros((width, 2 * keep.shape[-1] - used), f32), used, dp, side, n_dp)
+
+
+def rest_kernel(blocks, n_dp, place, *refs):
+    tokens_hbm = refs[:blocks]
+    (notes, router_part, grad_ctx) = refs[blocks:blocks + 3]
+    (
+        queries_hbm, keys_hbm, values_hbm, log_hbm, entry_hbm, qkv_hbm, grad_q_hbm, grad_kv_hbm, *turns_hbm
+    ) = refs[blocks + 3:blocks + 14]
+    outs = refs[blocks + 14:]
+    grad_own, grad_far, (keep, send) = outs[0], outs[1:blocks], outs[blocks:blocks + 2]
+    (
+        tokens, queries, keys, values, log_total, entry, qkv_w, grad_q0, grad_kv0, cos, sin_up, sin_down, grad_q,
+        grad_kv, sems,
+    ) = outs[blocks + 2:]
+    rows, width = grad_ctx.shape
+    here, dp, side = place[6], place[1], place[5]
+    copies = Copies(sems)
+    tile = queries.shape[1]
+    pairs = log_total.shape[0]
+    part = slice(tile, 2 * tile)
+    turns = (cos, sin_up, sin_down)
+    first_in = [
+        copies.start(source, target)
+        for source, target in (
+            (queries_hbm.at[:, part], queries), (keys_hbm.at[:, part], keys), (values_hbm.at[:, part], values),
+            (log_hbm.at[pairs:], log_total),
+        )
+    ]
+    first_in += load_turns(copies, turns_hbm, turns, blocks, rows, here)
+    late_in = [
+        copies.start(source, target)
+        for source, target in (
+            (entry_hbm, entry), (qkv_hbm, qkv_w), (grad_q_hbm, grad_q0), (grad_kv_hbm, grad_kv0),
+            *((tokens_hbm[r], tokens.at[r]) for r in range(blocks)),
+        )
+    ]
+    for copy in first_in:
+        copy.wait()
+    attend_back(
+        pairs, pairs, key_bias(blocks, rows, here), queries, keys, values, log_total, grad_ctx, turns, grad_q, grad_kv
+    )
+    for copy in late_in:
+        copy.wait()
+    store_pack(keep, send, dot_tn(entry[:rows, :], grad_q[...]), 0, dp, side, n_dp)
+    for mat in range(2):
+        grad = dot_tn(entry[...], grad_kv[:, mat * tile:(mat + 1) * tile])
+        store_pack(keep, send, grad, (1 + mat) * tile, dp, side, n_dp)
+
+    total = jnp.zeros((1, width), f32)
+    for r in range(blocks):
+        block = slice(r * rows, (r + 1) * rows)
+        grad_entry = None
+        for half, source in enumerate((grad_kv0, grad_kv)):
+            for mat in range(2):
+                start = (1 + mat) * width + half * tile
+                term = dot_nt(source[block, mat * tile:(mat + 1) * tile], qkv_w[:, start:start + tile])
+                grad_entry = term if grad_entry is None else grad_entry + term
+        if r == 0:
+            grad_entry = grad_entry + dot_nt(grad_q0[...], qkv_w[:, :tile]) + dot_nt(
+                grad_q[...], qkv_w[:, tile:2 * tile]
+            )
+            grad_own[...] = grad_entry
+        else:
+            grad_far[r - 1][...] = grad_entry.astype(bf16)
+        x = tokens[r].astype(f32)
+        factor = lax.rsqrt(jnp.mean(x * x, axis=-1, keepdims=True) + norm_eps)
+        total = total + jnp.sum(grad_entry * (x * factor), axis=0, keepdims=True)
+    notes_t = notes[...].T
+    total_t = jnp.broadcast_to(total, (8, width)).T
+    lane = lax.broadcasted_iota(jnp.int32, (width, 128), 1)
+    small = router_part[...] + jnp.where(lane == 8, notes_t[:, 0:1], 0.0) + jnp.where(
+        lane == 9, total_t[:, 0:1], 0.0
+    )
+    store_pack(keep, send, small, 3 * tile, dp, side, n_dp)
+
+
+def call(kernel, outs, scratch, scalars, operands, after=(), limit=60, aliases=None):
+    whole = pl.BlockSpec(memory_space=pltpu.VMEM)
+    anywhere = pl.BlockSpec(memory_space=pl.ANY)
+    values, specs = [], []
+    for value, kind in [*operands, *((value, far) for value in after)]:
+        value = pltpu.with_memory_space_constraint(value, pltpu.VMEM if kind == held else pltpu.HBM)
+        if isinstance(kind, int):
+            kind = anywhere if kind == far else whole
+        values.append(value)
+        specs.append(kind)
+    taken, ignored = len(operands), len(after)
+
+    def body(place, *refs):
+        kernel(place, *refs[:taken], *refs[taken + ignored:])
+
+    return pl.pallas_call(
+        body,
+        grid_spec=pltpu.PrefetchScalarGridSpec(
+            num_scalar_prefetch=1,
+            grid=(1,),
+            in_specs=specs,
+            out_specs=[anywhere if kind == far else whole for _, _, kind in outs],
+            scratch_shapes=scratch,
+        ),
+        out_shape=[
+            pltpu.HBM(shape, dtype) for shape, dtype, _ in outs
+        ],
+        input_output_aliases=aliases or {},
+        compiler_params=pltpu.CompilerParams(vmem_limit_bytes=limit * 2**20),
+        cost_estimate=pl.CostEstimate(flops=10**8, bytes_accessed=0, transcendentals=0),
+    )(scalars, *values)
+
+
+def hold_until(scalars, values, after):
+    return call(
+        lambda place, *refs: None,
+        [(value.shape, value.dtype, far) for value in values],
+        [],
+        scalars,
+        [(value, far) for value in values],
+        after,
+        limit=1,
+        aliases={1 + k: k for k in range(len(values))},
+    )
+
+
+def swap(value, mask):
+    return lax.ppermute(value, group, [(i, i ^ mask) for i in range(8)])
+
+
+def on_block(
+    n_context,
+    tokens,
+    norm1_gain,
+    qkv_weight,
+    out_weight,
+    norm2_gain,
+    router_weight,
+    expert_gate,
+    expert_up,
+    expert_down,
+    shared_gate,
+    shared_up,
+    shared_down,
+    routes,
+    cotangent,
+):
+    rows, width = tokens.shape[1:]
+    hidden = shared_gate.shape[1]
+    n_experts = router_weight.shape[1]
+    blocks = n_context
+    n_dp = 4
+    slots = rows * routes.shape[-1] * 5 // (4 * n_experts)
+    dp = lax.axis_index(DP)
+    here = lax.axis_index(CONTEXT)
+    side = lax.axis_index(EXPERTS)
+    core, chip = dp % 2, dp // 2
+    index = dp * 2 + side
+    expert = 2 * side + core
+    pairs = width // 128
+
+    own = tokens[0]
+    cot = cotangent[0]
+    cot_all = lax.all_gather(cot, group, axis=0)
+    field = [own, lax.ppermute(own, CONTEXT, [(i, i + 1) for i in range(n_context - 1)])]
+    field.append(lax.ppermute(field[1], CONTEXT, [(i, i + 1) for i in range(1, n_context - 1)]))
+    field += [
+        lax.ppermute(own, CONTEXT, [(i, i + r) for i in range(n_context - r)]) for r in range(3, blocks)
+    ]
+    tables = spin_tables(n_context * rows)
+    gain1, gain2 = norm1_gain[None, :], norm2_gain[None, :]
+    scalars = jnp.stack([index, dp, expert, core, chip, side, here])
+    piece = width // n_dp // n_context
+    half_columns = hidden // 2
+    chunk_columns = hidden // 4
+    shared_columns = hidden // 8
+    quarter = hidden // n_dp
+
+    def many(kind, *values):
+        return [(value, kind) for value in values]
+
+    router = jnp.pad(router_weight, ((0, 0), (0, 128 - n_experts)))
+    router_t = jnp.pad(router_weight.T, ((0, 128 - n_experts), (0, 0)))
+
+    picked_up = ((width, shared_columns), bf16, copied)
+    picked = call(
+        partial(pick_kernel, n_context),
+        [picked_up, picked_up, ((shared_columns, width), bf16, copied)],
+        [],
+        scalars,
+        [
+            (shared_gate, pl.BlockSpec((width, quarter), lambda i, s: (0, s[1]))),
+            (shared_up, pl.BlockSpec((width, quarter), lambda i, s: (0, s[1]))),
+            (shared_down, pl.BlockSpec((quarter, width), lambda i, s: (s[1], 0))),
+        ],
+        [router, router_t],
+        limit=10,
+    )
+
+    act = (rows, width)
+    wide = (blocks * rows, width)
+    sent = (rows + 16, width)
+    logs = (pairs, rows, 128)
+    turn = (blocks * rows, 128)
+    entry, queries, keys, values, log_total, context, middle, entry_two = call(
+        partial(attend_kernel, blocks),
+        [
+            (wide, bf16, far), (act, bf16, far), (wide, bf16, far), (wide, bf16, far), (logs, f32, far),
+            (act, bf16, far), (act, f32, copied), (sent, bf16, copied),
+        ],
+        [
+            *[pltpu.VMEM(turn, f32)] * 3, pltpu.VMEM(wide, bf16), pltpu.VMEM(act, bf16), pltpu.VMEM(wide, bf16),
+            pltpu.VMEM(wide, bf16), pltpu.VMEM(logs, f32), pltpu.VMEM(act, bf16), pltpu.SemaphoreType.DMA((32,)),
+        ],
+        jnp.stack([here]),
+        [
+            *many(copied, *field, routes[0, 0].T, gain1), *many(held, qkv_weight, out_weight),
+            (gain2, copied), *many(far, *tables),
+        ],
+        [picked[0]],
+        limit=24,
+    )
+
+    near = {0: entry_two}
+    near[1], near[4] = swap(entry_two, 1), swap(entry_two, 4)
+    near[5] = swap(near[1], 4)
+    for mask in keep_masks:
+        near[mask ^ 2] = swap(near[mask], 2)
+
+    slot_act, slot_chunk, slot_notes = (8 * slots, width), (8 * slots, chunk_columns), (8 * slots, 128)
+    row_act, row_hidden = (8 * rows, width), (8 * rows, shared_columns)
+    layout = Layout(width, hidden, n_dp, n_context)
+    rows0 = n_context * (n_dp * layout.run_place + width)
+    rows1 = n_context * (n_dp * (layout.shared_place + layout.run_place) + layout.shared_down + width)
+    run_scratch = [
+        *[pltpu.VMEM((width, chunk_columns), bf16)] * 2, pltpu.VMEM((chunk_columns, width), bf16),
+    ]
+    kept = [(slot_notes, f32), ((8, slots, rows), bf16), *[(slot_act, bf16)] * 2]
+    every = [near[mask] for mask in all_masks]
+    *entered, bundle0 = call(
+        partial(enter_kernel, all_masks, n_context, n_dp, layout),
+        [*[(*out, far) for out in kept], ((rows0, 128), bf16, copied)],
+        [
+            *[pltpu.VMEM(*out) for out in kept], *[pltpu.VMEM(slot_act, bf16)] * 2, *[pltpu.VMEM(row_act, bf16)] * 2,
+            *run_scratch, *[pltpu.VMEM(slot_chunk, bf16)] * 3, pltpu.VMEM((8, 16, width), bf16),
+            pltpu.SemaphoreType.DMA((40,)),
+        ],
+        scalars,
+        [*many(far, *every, cot_all), (router, copied), *many(far, expert_gate, expert_up, expert_down)],
+        limit=56,
+    )
+    sum0 = lax.psum_scatter(bundle0, CONTEXT, scatter_dimension=0, tiled=True)
+    four = (4, rows, width)
+    grad_keep, grad_send, mix_keep, mix_send, router_part, bundle1 = call(
+        partial(leave_kernel, all_masks, n_context, n_dp, layout),
+        [*[(four, bf16, far)] * 4, ((width, 128), f32, copied), ((rows1, 128), bf16, copied)],
+        [
+            *[pltpu.VMEM(*out) for out in kept], *[pltpu.VMEM(slot_act, bf16)] * 3, *[pltpu.VMEM(slot_act, f32)] * 2,
+            *[pltpu.VMEM(row_act, bf16)] * 2, *run_scratch, *[pltpu.VMEM((width, shared_columns), bf16)] * 2, pltpu.VMEM((shared_columns, width), bf16),
+            *[pltpu.VMEM(slot_chunk, bf16)] * 3, *[pltpu.VMEM(row_hidden, bf16)] * 3,
+            *[pltpu.VMEM((8, rows, width), bf16)] * 2, pltpu.VMEM((8 * slots, 2 * width), bf16),
+            pltpu.SemaphoreType.DMA((56,)),
+        ],
+        scalars,
+        [
+            *many(far, *entered, *every, cot_all), (router_t, copied),
+            *many(far, *picked, expert_gate, expert_up, expert_down),
+        ],
+        limit=58,
+    )
+    sum1 = lax.psum_scatter(bundle1, CONTEXT, scatter_dimension=0, tiled=True)
+
+    def add_blocks(left, right):
+        return [
+            (left[k].astype(f32) + right[k].astype(f32)).astype(bf16) for k in range(left.shape[0])
+        ]
+
+    grad_sums = add_blocks(grad_keep, swap(grad_send, 2))
+    parts = [grad_sums[0], *[swap(value, mask) for value, mask in zip(grad_sums[1:], keep_masks[1:])]]
+
+    mix_sums = add_blocks(mix_keep, swap(mix_send, 2))
+    sent_mix = hold_until(scalars, mix_sums[1:], parts[1:])
+    mix_parts = [middle, mix_sums[0], *[swap(value, mask) for value, mask in zip(sent_mix, keep_masks[1:])]]
+
+    tile = width // 2
+    pack_rows = width // n_dp
+    half_act, half_wide, half_logs = (rows, tile), (blocks * rows, tile), (pairs // 2, rows, 128)
+    pack0 = (2, 2, pack_rows, (3 * tile + width + 128) // 2)
+    pack1 = (2, 2, pack_rows, (3 * tile + 128) // 2)
+    half_heads = [
+        pltpu.VMEM(half_act, bf16), pltpu.VMEM(half_wide, bf16), pltpu.VMEM(half_wide, bf16), pltpu.VMEM(half_logs, f32)
+    ]
+    turn_scratch = [pltpu.VMEM(turn, f32)] * 3
+    grad_middle, grad_ctx, grad_q, grad_kv, notes, keep0, send0 = call(
+        partial(back_kernel, blocks, n_dp),
+        [
+            (act, f32, copied), (act, bf16, copied), (half_act, bf16, copied), (wide, bf16, copied),
+            ((8, width), f32, copied), (pack0, bf16, copied), (pack0, bf16, copied),
+        ],
+        [
+            *half_heads, pltpu.VMEM(act, bf16), pltpu.VMEM(wide, bf16), *turn_scratch, pltpu.SemaphoreType.DMA((24,)),
+        ],
+        scalars,
+        [
+            *many(copied, *parts, middle, cot, gain2, out_weight),
+            *many(far, queries, keys, values, log_total, context, entry, *tables),
+        ],
+        sent_mix,
+        limit=44,
+    )
+
+    def by_chips(keep, send):
+        other = swap(send, 2)
+        sums = [(keep[i, j].astype(f32) + other[i, j].astype(f32)).astype(bf16) for i in range(2) for j in range(2)]
+        return [sums[0], swap(sums[1], 1), swap(sums[2], 4), swap(sums[3], 5)]
+
+    def by_context(sets, after):
+        columns = sum(arrived[0].shape[1] for arrived in sets)
+        shares = call(
+            partial(sum_kernel, n_context, [len(arrived) for arrived in sets]),
+            [((piece, columns), bf16, copied)] * n_context, [], scalars,
+            many(copied, *[value for arrived in sets for value in arrived]), after, limit=16,
+        )
+        return [shares[0]] + [
+            lax.ppermute(shares[r], CONTEXT, [(i, (i + r) % n_context) for i in range(n_context)])
+            for r in range(1, n_context)
+        ]
+
+    def total(shares):
+        value = sum(value.astype(f32) for value in shares).astype(bf16)
+        return [value, swap(value, 1)]
+
+    send0, = hold_until(scalars, [send0], mix_parts[2:])
+    arrived0 = by_chips(keep0, send0)
+    results = call(
+        partial(rest_kernel, blocks, n_dp),
+        [(act, f32, copied), *[(act, bf16, copied)] * (blocks - 1), *[(pack1, bf16, copied)] * 2],
+        [
+            pltpu.VMEM((blocks, rows, width), bf16), *half_heads, pltpu.VMEM(wide, bf16),
+            pltpu.VMEM(qkv_weight.shape, bf16), pltpu.VMEM(half_act, bf16), pltpu.VMEM(wide, bf16), *turn_scratch,
+            pltpu.VMEM(half_act, bf16), pltpu.VMEM(wide, bf16), pltpu.SemaphoreType.DMA((32,)),
+        ],
+        scalars,
+        [
+            *many(far, *field), *many(copied, notes, router_part, grad_ctx),
+            *many(far, queries, keys, values, log_total, entry, qkv_weight, grad_q, grad_kv, *tables),
+        ],
+        [arrived0[0]],
+        limit=44,
+    )
+    grad_own, keep1 = results[0], results[blocks]
+    *grad_far, send1 = hold_until(scalars, [*results[1:blocks], results[blocks + 1]], arrived0[1:])
+    run0 = [sum0[m * layout.run_place:(m + 1) * layout.run_place] for m in range(n_dp)]
+    run0 = [run0[0]] + [swap(run0[m], 2 * m) for m in range(1, n_dp)]
+    down0 = sum0[n_dp * layout.run_place:]
+    got_down0 = lax.ppermute(down0, DP, [(i, i ^ 1) for i in range(n_dp) if i % 2 == 1])
+    output = sum(value.astype(f32) for value in mix_parts).astype(bf16)[None]
+
+    arrived1 = by_chips(keep1, send1)
+    pulled = [
+        lax.ppermute(grad_far[r - 1], CONTEXT, [(i, i - r) for i in range(r, n_context)])
+        for r in range(1, blocks)
+    ]
+    sum1, = hold_until(scalars, [sum1], [arrived1[0], *pulled[2:]])
+    slab_rows = layout.shared_place + layout.run_place
+    run1 = [sum1[m * slab_rows:(m + 1) * slab_rows] for m in range(n_dp)]
+    downs1 = sum1[n_dp * slab_rows:]
+    shared = [slab[:layout.shared_place] for slab in run1]
+    shared[0] = jnp.concatenate([shared[0], downs1[:layout.shared_down]], axis=0)
+    shared_far = [swap(value, 2 * m + 1) for m, value in enumerate(shared)]
+    run1 = [run1[0]] + [swap(run1[m], 2 * m) for m in range(1, n_dp)]
+    got_down1 = lax.ppermute(
+        downs1[layout.shared_down:], DP, [(i, i ^ 1) for i in range(n_dp) if i % 2 == 0]
+    )
+
+    shares = by_context([arrived0, arrived1], [pulled[1], *run0[1:], got_down0, *run1[1:], *shared_far, got_down1])
+    gate_grad, up_grad, down_grad, gate_s_grad, up_s_grad, down_s_grad = call(
+        partial(feed_grads_kernel, n_dp, layout),
+        [
+            (shape, f32, copied)
+            for shape in (
+                (2, piece, hidden), (2, piece, hidden), (2, 128, width), (piece, hidden), (piece, hidden),
+                (hidden // n_dp // n_context, width),
+            )
+        ],
+        [],
+        scalars,
+        many(copied, *run0, *run1, *shared_far, down0, downs1, got_down0, got_down1),
+        [shares[0], *pulled],
+        limit=32,
+    )
+    shares = [shares[0], *hold_until(scalars, shares[1:], [down_s_grad])]
+    input_grad, qkv_grad, out_grad, norm1_grad, norm2_grad, router_grad = call(
+        partial(last_kernel, blocks),
+        [
+            (shape, f32, copied)
+            for shape in (act, (piece, 3 * width), (piece, width), (1, piece), (1, piece), (n_experts, piece))
+        ],
+        [],
+        scalars,
+        many(copied, *total(shares), own, gain1, grad_own, grad_middle, *pulled),
+        limit=32,
+    )
+    return (
+        output, input_grad[None], norm1_grad[0], qkv_grad, out_grad, norm2_grad[0], router_grad.T,
+        gate_grad, up_grad, down_grad, gate_s_grad, up_s_grad, down_s_grad,
+    )
+
+
+def on_any(mesh, *args):
+    tokens, router_weight, expert_gate, shared_gate = args[0], args[5], args[6], args[9]
+    sizes = dict(mesh.shape)
+    fits = (
+        sizes[DP] == 4
+        and sizes[EXPERTS] == 2
+        and tokens.shape[0] == 1
+        and tokens.shape[1] == BLOCK
+        and expert_gate.shape[0] == 2
+        and tokens.shape[2] % 128 == 0
+        and tokens.shape[2] // sizes[DP] % (16 * sizes[CONTEXT]) == 0
+        and shared_gate.shape[1] % (1024) == 0
+        and sizes[CONTEXT] == 4
+        and shared_gate.shape[1] == 128 * sizes[DP] * sizes[CONTEXT]
+    )
+    if fits:
+        return on_block(sizes[CONTEXT], *args)
+    return on_device(*args)
+
+
 def solution(mesh):
     return jax.shard_map(
-        on_device,
+        partial(on_any, mesh),
         mesh=mesh,
         in_specs=(
-            P(("dp", "experts"), "context", None),
+            P((DP, EXPERTS), CONTEXT, None),
             P(),
             P(),
             P(),
             P(),
             P(),
-            P("experts", None, None),
-            P("experts", None, None),
-            P("experts", None, None),
+            P(EXPERTS, None, None),
+            P(EXPERTS, None, None),
+            P(EXPERTS, None, None),
             P(),
             P(),
             P(),
-            P("context", ("dp", "experts"), None, None),
-            P(("dp", "experts"), "context", None),
+            P(CONTEXT, (DP, EXPERTS), None, None),
+            P((DP, EXPERTS), CONTEXT, None),
         ),
         out_specs=(
-            P(("dp", "experts"), "context", None),
-            P(("dp", "experts"), "context", None),
-            P(("dp", "context")),
-            P(("dp", "context"), None),
-            P(("dp", "context"), None),
-            P(("dp", "context")),
-            P(("dp", "context"), None),
-            P("experts", ("dp", "context"), None),
-            P("experts", ("dp", "context"), None),
-            P("experts", ("dp", "context"), None),
-            P(("dp", "context"), None),
-            P(("dp", "context"), None),
-            P(("dp", "context"), None),
+            P((DP, EXPERTS), CONTEXT, None),
+            P((DP, EXPERTS), CONTEXT, None),
+            P((DP, CONTEXT)),
+            P((DP, CONTEXT), None),
+            P((DP, CONTEXT), None),
+            P((DP, CONTEXT)),
+            P((DP, CONTEXT), None),
+            P(EXPERTS, (DP, CONTEXT), None),
+            P(EXPERTS, (DP, CONTEXT), None),
+            P(EXPERTS, (DP, CONTEXT), None),
+            P((DP, CONTEXT), None),
+            P((DP, CONTEXT), None),
+            P((DP, CONTEXT), None),
         ),
         check_vma=False,
     )

time: 1240 us -> 318 us (0.26)
  waiting for transfers between devices: 824 us -> 90.4 us
  matrix products: 181 us -> 0 us
  Pallas kernels: 0 us -> 125 us
  blocking collectives: 71.6 us -> 0 us
  other arithmetic: 61.5 us -> 9.78 us
  starting transfers between devices: 19.3 us -> 50.5 us
  local copies, waits for them, and re-layouts: 51.9 us -> 21 us
    reduce_scatter x8 -> x2, waiting for transfers between devices: 721 us -> 0.04 us  [the longest x1 0.02 us: on_block(): sum0 = lax.psum_scatter(bundle0, CONTEXT, scatter_dimension=0, tiled=True)]
    dot_general x40 -> x0, matrix products: 180 us -> none  [the longest x33 163 us: contract(): return jnp.einsum(spec, left, right, preferred_element_type=jnp.float32)]
    pallas_call x0 -> x14, Pallas kernels: none -> 125 us  [call(): pl.pallas_call(body, grid_spec=pltpu.PrefetchScalarGridSpec(num_scalar_pr...]
    ppermute x0 -> x45, waiting for transfers between devices: none -> 89.6 us  [the longest x34 53.8 us: swap(): return lax.ppermute(value, group, [(i, i ^ mask) for i in range(8)])]
    all_gather x4 -> x1, waiting for transfers between devices: 67.8 us -> 0.01 us  [on_block(): cot_all = lax.all_gather(cot, group, axis=0)]
    ppermute x0 -> x45, starting transfers between devices: none -> 50.4 us  [the longest x34 28.5 us: swap(): return lax.ppermute(value, group, [(i, i ^ mask) for i in range(8)])]
    all_gather x2 -> x0, blocking collectives: 33.7 us -> none  [the longest x1 20.3 us: on_device(): lax.all_gather(log_rows.astype(jnp.bfloat16), 'context', axis=0, tiled=True)]
    unnamed x1 -> x0, blocking collectives: 32.4 us -> none
  transfers between devices with their start and end apart: 18 -> 48, of which waited for: 13 -> 20; matrix products, arithmetic and copies ran while one was open for 22% -> 7% of each run, Pallas kernels for 0% -> 32%
where the time goes in v1:
time: 318 us; the launch traced here: 312 us
  Pallas kernels  125 us (39%)
  waiting for transfers between devices  90.4 us (28%)
  starting transfers between devices  50.5 us (16%)
  local copies, waits for them, and re-layouts  21 us (7%)
  between operations  14.9 us (5%)
  other arithmetic  9.78 us (3%)
    pallas_call x14, Pallas kernels, call(): pl.pallas_call(body, grid_spec=pltpu.PrefetchScalarGridSpec(num_scalar_pr...  125 us
    ppermute x34, waiting for transfers between devices, swap(): return lax.ppermute(value, group, [(i, i ^ mask) for i in range(8)])  53.8 us
    ppermute x34, starting transfers between devices, swap(): return lax.ppermute(value, group, [(i, i ^ mask) for i in range(8)])  28.5 us
    ppermute x3, waiting for transfers between devices, on_block(): lax.ppermute(grad_far[r - 1], CONTEXT, [(i, i - r) for i in range(r, n_co...  24.8 us
    unnamed x115, local copies, waits for them, and re-layouts  9.36 us
  transfers between devices with their start and end apart: 48, of which 20 were waited for; matrix products, arithmetic and copies ran while one was open for 7% of the time, Pallas kernels for 32%

profile of v1, /device:TPU:0, one launch (start us, length us, event | category | flops | bytes accessed | tf_op | source)
XLA Modules:
  0.0 311.6 jit_solution(7221617194206869396)
XLA Ops:
  8.0 5.7 %collective-permute-start = (bf16[256,768]{1,0:T(8,128)(2,1)}, bf16[256,768]{1,0:T(8,128)(2,1)}, u32[]{:S(2)}, u32[]{:S(2)}) collective-permute-start(bf16[256,768]{1,0:T(8,128)(2,1)} %bitcast.56), channel_id=1, source_target_pairs={{0,2},{2,4},{4,6},{1,3},{3,5},{5,7},{8,10},{10,12},{12,14},{9,11},... | collective-permute-start | bytes 1179656 | tf_op jit(solution)/shard_map/ppermute | solution.py:1248
  13.7 3.3 %collective-permute-start.2 = (bf16[256,768]{1,0:T(8,128)(2,1)}, bf16[256,768]{1,0:T(8,128)(2,1)}, u32[]{:S(2)}, u32[]{:S(2)}) collective-permute-start(bf16[256,768]{1,0:T(8,128)(2,1)} %bitcast.57), channel_id=1, source_target_pairs={{0,6},{1,7},{8,14},{9,15},{16,22},{17,23},{24,30},{25,31}} | collective-permute-start | bytes 1179656 | tf_op jit(solution)/shard_map/ppermute | solution.py:1251
  17.0 5.7 %collective-permute-done.refs_1_ = bf16[256,768]{1,0:T(8,128)(2,1)} collective-permute-done((bf16[256,768]{1,0:T(8,128)(2,1)}, bf16[256,768]{1,0:T(8,128)(2,1)}, u32[]{:S(2)}, u32[]{:S(2)}) %collective-permute-start) | collective-permute-done | bytes 393248 | tf_op jit(solution)/shard_map/ppermute | solution.py:1248
  29.8 4.0 %shard_map.264 = (bf16[768,256]{1,0:T(8,128)(2,1)}, bf16[768,256]{1,0:T(8,128)(2,1)}, bf16[256,768]{1,0:T(8,128)(2,1)}) custom-call(s32[7]{0:T(128)S(1)} %stack.32.place, bf16[768,2048]{1,0:T(8,128)(2,1)} %refs_0_.1, bf16[768,2048]{1,0:T(8,128)(2,1)} %refs_1_.1, bf16[2048,768]{1,0:T(8,128)(2,1)} %refs_2_.1, bf16[768,128]{1,0:T(8,128)(2,1)} %pad.8.refs_3_.refs_9_, ...), custom_call_target="tpu_custom_call" | custom-call | flops 100000000 | tf_op jit(solution)/shard_map/pallas_call | solution.py:1179
  33.8 16.9 %shard_map.265 = (bf16[1024,768]{1,0:T(8,128)(2,1)}, bf16[256,768]{1,0:T(8,128)(2,1)}, bf16[1024,768]{1,0:T(8,128)(2,1)}, bf16[1024,768]{1,0:T(8,128)(2,1)}, f32...) custom-call(s32[1]{0:T(128)} %bitcast.place, ...), custom_call_target="tpu_custom_call" | custom-call | flops 100000000 | tf_op jit(solution)/shard_map/pallas_call | solution.py:1179
  53.8 6.6 %collective-permute-done.3.refs_1_.refs_5_ = bf16[272,768]{1,0:T(8,128)(2,1)S(1)} collective-permute-done((bf16[272,768]{1,0:T(8,128)(2,1)}, bf16[272,768]{1,0:T(8,128)(2,1)S(1)}, u32[]{:S(2)}, u32[]{:S(2)}) %collective-permute-start.3) | collective-permute-done | bytes 417824 | tf_op jit(solution)/shard_map/ppermute | solution.py:1211
  63.2 7.3 %collective-permute-done.5.refs_3_.refs_7_ = bf16[272,768]{1,0:T(8,128)(2,1)S(1)} collective-permute-done((bf16[272,768]{1,0:T(8,128)(2,1)S(1)}, bf16[272,768]{1,0:T(8,128)(2,1)S(1)}, u32[]{:S(2)}, u32[]{:S(2)}) %collective-permute-start.5) | collective-permute-done | bytes 417824 | tf_op jit(solution)/shard_map/ppermute | solution.py:1211
  73.1 19.7 %shard_map.266 = (f32[1280,128]{1,0:T(8,128)}, bf16[8,160,256]{2,1,0:T(8,128)(2,1)}, bf16[1280,768]{1,0:T(8,128)(2,1)}, bf16[1280,768]{1,0:T(8,128)(2,1)}, bf16[9216,128]{1,0:T(8,128)(2,1)}) custom-call(s32[7]{0:T(128)} %copy-done.2, bf16[272,768]{1,0:T(8,128)(2,1)} %get-tuple-element.76.refs_0_.refs_4_, bf16[272,768]{1,0:T(8,128)(2,1)} %copy-done.8, ...), custom_call_target="tpu_custom_call" | custom-call | flops 100000000 | tf_op jit(solution)/shard_map/pallas_call | solution.py:1179
  92.8 30.4 %shard_map.267 = (bf16[4,256,768]{2,1,0:T(8,128)(2,1)}, bf16[4,256,768]{2,1,0:T(8,128)(2,1)}, bf16[4,256,768]{2,1,0:T(8,128)(2,1)}, bf16[4,256,768]{2,1,0:T(8,12...) custom-call(s32[7]{0:T(128)} %copy-done.2, f32[1280,128]{1,0:T(8,128)} %get-tuple-element.77.refs_0_, ...), custom_call_target="tpu_custom_call" | custom-call | flops 100000000 | tf_op jit(solution)/shard_map/pallas_call | solution.py:1179
  125.1 3.7 %collective-permute-done.11 = bf16[4,256,768]{2,1,0:T(8,128)(2,1)S(1)} collective-permute-done((bf16[4,256,768]{2,1,0:T(8,128)(2,1)S(1)}, bf16[4,256,768]{2,1,0:T(8,128)(2,1)S(1)}, u32[]{:S(2)}, u32[]{:S(2)}) %collective-permute-start.11) | collective-permute-done | bytes 1572896 | tf_op jit(solution)/shard_map/ppermute | solution.py:1211
  135.1 7.8 %collective-permute-done.14.refs_5_.refs_3_ = bf16[256,768]{1,0:T(8,128)(2,1)S(1)} collective-permute-done((bf16[256,768]{1,0:T(8,128)(2,1)S(1)}, bf16[256,768]{1,0:T(8,128)(2,1)S(1)}, u32[]{:S(2)}, u32[]{:S(2)}) %collective-permute-start.14) | collective-permute-done | bytes 393248 | tf_op jit(solution)/shard_map/ppermute | solution.py:1211
  143.0 7.0 %collective-permute-done.13.refs_4_.refs_2_ = bf16[256,768]{1,0:T(8,128)(2,1)S(1)} collective-permute-done((bf16[256,768]{1,0:T(8,128)(2,1)S(1)}, bf16[256,768]{1,0:T(8,128)(2,1)S(1)}, u32[]{:S(2)}, u32[]{:S(2)}) %collective-permute-start.13) | collective-permute-done | bytes 393248 | tf_op jit(solution)/shard_map/ppermute | solution.py:1211
  155.4 18.3 %shard_map.269 = (f32[256,768]{1,0:T(8,128)}, bf16[256,768]{1,0:T(8,128)(2,1)}, bf16[256,384]{1,0:T(8,128)(2,1)}, bf16[1024,768]{1,0:T(8,128)(2,1)}, f32[8,768]{...) custom-call(s32[7]{0:T(128)S(1)} %copy-done.3, ...), custom_call_target="tpu_custom_call" | custom-call | flops 100000000 | tf_op jit(solution)/shard_map/pallas_call | solution.py:1179
  175.4 3.6 %collective-permute-done.18 = bf16[2,2,192,1024]{3,2,1,0:T(8,128)(2,1)S(1)} collective-permute-done((bf16[2,2,192,1024]{3,2,1,0:T(8,128)(2,1)}, bf16[2,2,192,1024]{3,2,1,0:T(8,128)(2,1)S(1)}, u32[]{:S(2)}, u32[]{:S(2)}) %collective-permute-start.18) | collective-permute-done | bytes 1572896 | tf_op jit(solution)/shard_map/ppermute | solution.py:1211
  180.4 2.1 collective-permute-start.21
  183.9 21.6 %shard_map.271 = (f32[256,768]{1,0:T(8,128)}, bf16[256,768]{1,0:T(8,128)(2,1)}, bf16[256,768]{1,0:T(8,128)(2,1)}, bf16[256,768]{1,0:T(8,128)(2,1)}, bf16[2,2,192...) custom-call(s32[7]{0:T(128)S(1)} %copy-done.3, bf16[256,768]{1,0:T(8,128)(2,1)} %bitcast.59, ...), custom_call_target="tpu_custom_call" | custom-call | flops 100000000 | tf_op jit(solution)/shard_map/pallas_call | solution.py:1179
  214.7 2.5 fusion.20
  217.3 21.3 %collective-permute-done.31.refs_2_.refs_19_.refs_8_ = bf16[256,768]{1,0:T(8,128)(2,1)S(1)} collective-permute-done((bf16[256,768]{1,0:T(8,128)(2,1)}, bf16[256,768]{1,0:T(8,128)(2,1)S(1)}, u32[]{:S(2)}, u32[]{:S(2)}) %collective-permute-start.31) | collective-permute-done | bytes 393248 | tf_op jit(solution)/shard_map/ppermute | solution.py:1444
  240.5 3.6 %collective-permute-done.26.refs_8_.refs_18_.refs_7_ = bf16[256,768]{1,0:T(8,128)(2,1)S(1)} collective-permute-done((bf16[256,768]{1,0:T(8,128)(2,1)}, bf16[256,768]{1,0:T(8,128)(2,1)S(1)}, u32[]{:S(2)}, u32[]{:S(2)}) %collective-permute-start.26) | collective-permute-done | bytes 393248 | tf_op jit(solution)/shard_map/ppermute | solution.py:1444
  244.0 2.2 collective-permute-start.25
  253.8 2.2 collective-permute-start.37
  256.0 2.7 collective-permute-done.24.refs_6_
  260.2 2.4 collective-permute-start.39
  265.4 3.9 %collective-permute-done.34.refs_15_.refs_7_ = bf16[576,128]{1,0:T(8,128)(2,1)S(1)} collective-permute-done((bf16[576,128]{1,0:T(8,128)(2,1)S(1)}, bf16[576,128]{1,0:T(8,128)(2,1)S(1)}, u32[]{:S(2)}, u32[]{:S(2)}) %collective-permute-start.34) | collective-permute-done | bytes 147488 | tf_op jit(solution)/shard_map/ppermute | solution.py:1211
  269.4 3.2 %collective-permute-done.33.refs_14_.refs_6_ = bf16[576,128]{1,0:T(8,128)(2,1)S(1)} collective-permute-done((bf16[576,128]{1,0:T(8,128)(2,1)S(1)}, bf16[576,128]{1,0:T(8,128)(2,1)S(1)}, u32[]{:S(2)}, u32[]{:S(2)}) %collective-permute-start.33) | collective-permute-done | bytes 147488 | tf_op jit(solution)/shard_map/ppermute | solution.py:1211
  274.0 3.2 %shard_map.274 = (bf16[48,1664]{1,0:T(8,128)(2,1)}, bf16[48,1664]{1,0:T(8,128)(2,1)}, bf16[48,1664]{1,0:T(8,128)(2,1)}, bf16[48,1664]{1,0:T(8,128)(2,1)}) custom-call(s32[7]{0:T(128)S(1)} %copy-done.3, bf16[192,1024]{1,0:T(8,128)(2,1)} %get-tuple-element.138.refs_18_.refs_0_, bf16[192,1024]{1,0:T(8,128)(2,1)} %copy-done.30, bf16[192,1024]{1,0:T(8,128)(2,1)} %copy-done.29, ...), custom_call_target="tpu_custom_call" | custom-call | flops 100000000 | tf_op jit(solution)/shard_map/pallas_call | solution.py:1179
  277.2 3.8 %collective-permute-start.42 = (bf16[48,1664]{1,0:T(8,128)(2,1)}, bf16[48,1664]{1,0:T(8,128)(2,1)S(1)}, u32[]{:S(2)}, u32[]{:S(2)}) collective-permute-start(bf16[48,1664]{1,0:T(8,128)(2,1)} %get-tuple-element.116), channel_id=1, source_target_pairs={{0,6},{2,0},{4,2},{6,4},{1,7},{3,1},{5,3},{7,5},{8,14},{10,8},{12,... | collective-permute-start | bytes 479240 | tf_op jit(solution)/shard_map/ppermute | solution.py:1408
  282.5 4.3 %shard_map.275 = (f32[2,48,2048]{2,1,0:T(8,128)}, f32[2,48,2048]{2,1,0:T(8,128)}, f32[2,128,768]{2,1,0:T(8,128)}, f32[48,2048]{1,0:T(8,128)}, f32[48,2048]{1,0:T(8,128)}, /*index=5*/f32[128,768]{1,0:T(8,128)}) custom-call(s32[7]{0:T(128)S(1)} %copy-done.3, bf16[384,128]{1,0:T(8,128)(2,1)} %get-tuple-element.158.refs_0_, ...), custom_call_target="tpu_custom_call" | custom-call | flops 100000000 | tf_op jit(solution)/shard_map/pallas_call | solution.py:1179
  286.8 5.3 %collective-permute-done.41.refs_1_ = bf16[48,1664]{1,0:T(8,128)(2,1)S(1)} collective-permute-done((bf16[48,1664]{1,0:T(8,128)(2,1)}, bf16[48,1664]{1,0:T(8,128)(2,1)S(1)}, u32[]{:S(2)}, u32[]{:S(2)}) %collective-permute-start.41) | collective-permute-done | bytes 159776 | tf_op jit(solution)/shard_map/ppermute | solution.py:1408
  295.4 2.0 fusion.16
  297.4 2.5 collective-permute-done.44.refs_1_
  300.6 4.0 %shard_map.277 = (f32[256,768]{1,0:T(8,128)}, f32[48,2304]{1,0:T(8,128)}, f32[48,768]{1,0:T(8,128)}, f32[1,48]{1,0:T(1,128)}, f32[1,48]{1,0:T(1,128)}, /*index=5*/f32[4,48]{1,0:T(4,128)}) custom-call(s32[7]{0:T(128)S(1)} %copy-done.3, bf16[48,1664]{1,0:T(8,128)(2,1)} %copy-done.37, bf16[48,1664]{1,0:T(8,128)(2,1)} %copy-done.55, bf16[256,768]{1,0:T(8,128)(2,1)} %bitcast.60, ...), custom_call_target="tpu_custom_call" | custom-call | flops 100000000 | tf_op jit(solution)/shard_map/pallas_call | solution.py:1179
  (215 shorter events, 64.0 us)
Async XLA Ops:
  7.2 65.1 %all-gather.2.cloned.1.call-start = ((), (), s32[]{:S(2)}) async-start(), calls=%async_computation.2 | async-start | bytes 3538944 | tf_op jit(solution)/shard_map/all_gather | solution.py:1247
  7.9 202.0 %reduce-scatter.3.cloned.1.call-start = ((), (), s32[]{:S(2)}) async-start(), calls=%async_computation.3 | async-start | bytes 2949120 | tf_op jit(solution)/shard_map/reduce_scatter | solution.py:1335
  8.0 14.8 %collective-permute-start = (bf16[256,768]{1,0:T(8,128)(2,1)}, bf16[256,768]{1,0:T(8,128)(2,1)}, u32[]{:S(2)}, u32[]{:S(2)}) collective-permute-start(bf16[256,768]{1,0:T(8,128)(2,1)} %bitcast.56), channel_id=1, source_target_pairs={{0,2},{2,4},{4,6},{1,3},{3,5},{5,7},{8,10},{10,12},{12,14},{9,11},... | collective-permute-start | bytes 1179656 | tf_op jit(solution)/shard_map/ppermute | solution.py:1248
  13.7 20.1 %collective-permute-start.2 = (bf16[256,768]{1,0:T(8,128)(2,1)}, bf16[256,768]{1,0:T(8,128)(2,1)}, u32[]{:S(2)}, u32[]{:S(2)}) collective-permute-start(bf16[256,768]{1,0:T(8,128)(2,1)} %bitcast.57), channel_id=1, source_target_pairs={{0,6},{1,7},{8,14},{9,15},{16,22},{17,23},{24,30},{25,31}} | collective-permute-start | bytes 1179656 | tf_op jit(solution)/shard_map/ppermute | solution.py:1251
  22.7 11.1 %collective-permute-start.1 = (bf16[256,768]{1,0:T(8,128)(2,1)}, bf16[256,768]{1,0:T(8,128)(2,1)}, u32[]{:S(2)}, u32[]{:S(2)}) collective-permute-start(bf16[256,768]{1,0:T(8,128)(2,1)} %collective-permute-done.refs_1_), channel_id=1, source_target_pairs={{2,4},{4,6},{3,5},{5,7},{10,12},{12,14},{11,13},{13,15},{18,20},{2... | collective-permute-start | bytes 1179656 | tf_op jit(solution)/shard_map/ppermute | solution.py:1249
  52.3 11.0 %collective-permute-start.4 = (bf16[272,768]{1,0:T(8,128)(2,1)}, bf16[272,768]{1,0:T(8,128)(2,1)S(1)}, u32[]{:S(2)}, u32[]{:S(2)}) collective-permute-start(bf16[272,768]{1,0:T(8,128)(2,1)} %get-tuple-element.76.refs_0_.refs_4_), channel_id=1, source_target_pairs={{0,16},{1,17},{8,24},{9,25},{16,0},{17,1},{24,8},{25,9},{2,18},{3,... | collective-permute-start | bytes 1253384 | tf_op jit(solution)/shard_map/ppermute | solution.py:1211
  60.3 10.2 %collective-permute-start.5 = (bf16[272,768]{1,0:T(8,128)(2,1)S(1)}, bf16[272,768]{1,0:T(8,128)(2,1)S(1)}, u32[]{:S(2)}, u32[]{:S(2)}) collective-permute-start(bf16[272,768]{1,0:T(8,128)(2,1)S(1)} %collective-permute-done.3.refs_1_.refs_5_), channel_id=1, source_target_pairs={{0,16},{1,17},{8,24},{9,25},{16,0},{17,1},{24,8},{25,9},{2,18},{3,... | collective-permute-start | bytes 1253384 | tf_op jit(solution)/shard_map/ppermute | solution.py:1211
  92.8 147.1 %reduce-scatter.5.cloned.1.call-start = ((), (), s32[]{:S(2)}) async-start(), calls=%async_computation.4 | async-start | bytes 4423680 | tf_op jit(solution)/shard_map/reduce_scatter | solution.py:1354
  130.1 12.9 %collective-permute-start.14 = (bf16[256,768]{1,0:T(8,128)(2,1)S(1)}, bf16[256,768]{1,0:T(8,128)(2,1)S(1)}, u32[]{:S(2)}, u32[]{:S(2)}) collective-permute-start(bf16[256,768]{1,0:T(8,128)(2,1)S(1)} %get-tuple-element.140), channel_id=1, source_target_pairs={{0,17},{1,16},{8,25},{9,24},{16,1},{17,0},{24,9},{25,8},{2,19},{3,... | collective-permute-start | bytes 1179656 | tf_op jit(solution)/shard_map/ppermute | solution.py:1211
  131.8 18.2 %collective-permute-start.13 = (bf16[256,768]{1,0:T(8,128)(2,1)S(1)}, bf16[256,768]{1,0:T(8,128)(2,1)S(1)}, u32[]{:S(2)}, u32[]{:S(2)}) collective-permute-start(bf16[256,768]{1,0:T(8,128)(2,1)S(1)} %get-tuple-element.141), channel_id=1, source_target_pairs={{0,16},{1,17},{8,24},{9,25},{16,0},{17,1},{24,8},{25,9},{2,18},{3,... | collective-permute-start | bytes 1179656 | tf_op jit(solution)/shard_map/ppermute | solution.py:1211
  132.3 18.2 %collective-permute-start.12 = (bf16[256,768]{1,0:T(8,128)(2,1)S(1)}, bf16[256,768]{1,0:T(8,128)(2,1)S(1)}, u32[]{:S(2)}, u32[]{:S(2)}) collective-permute-start(bf16[256,768]{1,0:T(8,128)(2,1)S(1)} %get-tuple-element.142), channel_id=1, source_target_pairs={{0,1},{1,0},{8,9},{9,8},{16,17},{17,16},{24,25},{25,24},{2,3},{3,2... | collective-permute-start | bytes 1179656 | tf_op jit(solution)/shard_map/ppermute | solution.py:1211
  151.8 21.9 %collective-permute-start.15 = (bf16[256,768]{1,0:T(8,128)(2,1)}, bf16[256,768]{1,0:T(8,128)(2,1)S(1)}, u32[]{:S(2)}, u32[]{:S(2)}) collective-permute-start(bf16[256,768]{1,0:T(8,128)(2,1)} %get-tuple-element.87.refs_17_), channel_id=1, source_target_pairs={{0,1},{1,0},{8,9},{9,8},{16,17},{17,16},{24,25},{25,24},{2,3},{3,2... | collective-permute-start | bytes 1179656 | tf_op jit(solution)/shard_map/ppermute | solution.py:1211
  152.7 21.0 %collective-permute-start.16 = (bf16[256,768]{1,0:T(8,128)(2,1)}, bf16[256,768]{1,0:T(8,128)(2,1)S(1)}, u32[]{:S(2)}, u32[]{:S(2)}) collective-permute-start(bf16[256,768]{1,0:T(8,128)(2,1)} %get-tuple-element.88.refs_18_), channel_id=1, source_target_pairs={{0,16},{1,17},{8,24},{9,25},{16,0},{17,1},{24,8},{25,9},{2,18},{3,... | collective-permute-start | bytes 1179656 | tf_op jit(solution)/shard_map/ppermute | solution.py:1211
  154.2 19.6 %collective-permute-start.17 = (bf16[256,768]{1,0:T(8,128)(2,1)}, bf16[256,768]{1,0:T(8,128)(2,1)S(1)}, u32[]{:S(2)}, u32[]{:S(2)}) collective-permute-start(bf16[256,768]{1,0:T(8,128)(2,1)} %get-tuple-element.89.refs_19_), channel_id=1, source_target_pairs={{0,17},{1,16},{8,25},{9,24},{16,1},{17,0},{24,9},{25,8},{2,19},{3,... | collective-permute-start | bytes 1179656 | tf_op jit(solution)/shard_map/ppermute | solution.py:1211
  180.4 25.1 %collective-permute-start.21 = (bf16[192,1024]{1,0:T(8,128)(2,1)S(1)}, bf16[192,1024]{1,0:T(8,128)(2,1)S(1)}, u32[]{:S(2)}, u32[]{:S(2)}) collective-permute-start(bf16[192,1024]{1,0:T(8,128)(2,1)S(1)} %get-tuple-element.135), channel_id=1, source_target_pairs={{0,17},{1,16},{8,25},{9,24},{16,1},{17,0},{24,9},{25,8},{2,19},{3,... | collective-permute-start | bytes 1179656 | tf_op jit(solution)/shard_map/ppermute | solution.py:1211
  182.5 23.0 %collective-permute-start.20 = (bf16[192,1024]{1,0:T(8,128)(2,1)S(1)}, bf16[192,1024]{1,0:T(8,128)(2,1)S(1)}, u32[]{:S(2)}, u32[]{:S(2)}) collective-permute-start(bf16[192,1024]{1,0:T(8,128)(2,1)S(1)} %get-tuple-element.136), channel_id=1, source_target_pairs={{0,16},{1,17},{8,24},{9,25},{16,0},{17,1},{24,8},{25,9},{2,18},{3,... | collective-permute-start | bytes 1179656 | tf_op jit(solution)/shard_map/ppermute | solution.py:1211
  183.1 22.4 %collective-permute-start.19 = (bf16[192,1024]{1,0:T(8,128)(2,1)S(1)}, bf16[192,1024]{1,0:T(8,128)(2,1)S(1)}, u32[]{:S(2)}, u32[]{:S(2)}) collective-permute-start(bf16[192,1024]{1,0:T(8,128)(2,1)S(1)} %get-tuple-element.137), channel_id=1, source_target_pairs={{0,1},{1,0},{8,9},{9,8},{16,17},{17,16},{24,25},{25,24},{2,3},{3,2... | collective-permute-start | bytes 1179656 | tf_op jit(solution)/shard_map/ppermute | solution.py:1211
  207.1 36.9 %collective-permute-start.26 = (bf16[256,768]{1,0:T(8,128)(2,1)}, bf16[256,768]{1,0:T(8,128)(2,1)S(1)}, u32[]{:S(2)}, u32[]{:S(2)}) collective-permute-start(bf16[256,768]{1,0:T(8,128)(2,1)} %get-tuple-element.109), channel_id=1, source_target_pairs={{4,0},{6,2},{5,1},{7,3},{12,8},{14,10},{13,9},{15,11},{20,16},{22,... | collective-permute-start | bytes 1179656 | tf_op jit(solution)/shard_map/ppermute | solution.py:1444
  208.6 30.0 %collective-permute-start.31 = (bf16[256,768]{1,0:T(8,128)(2,1)}, bf16[256,768]{1,0:T(8,128)(2,1)S(1)}, u32[]{:S(2)}, u32[]{:S(2)}) collective-permute-start(bf16[256,768]{1,0:T(8,128)(2,1)} %get-tuple-element.112), channel_id=1, source_target_pairs={{6,0},{7,1},{14,8},{15,9},{22,16},{23,17},{30,24},{31,25}} | collective-permute-start | bytes 1179656 | tf_op jit(solution)/shard_map/ppermute | solution.py:1444
  211.7 34.5 %collective-permute-start.29 = (bf16[384,128]{1,0:T(8,128)(2,1)}, bf16[384,128]{1,0:T(8,128)(2,1)}, u32[]{:S(2)}, u32[]{:S(2)}) collective-permute-start(bf16[384,128]{1,0:T(8,128)(2,1)} %get-tuple-element.159), channel_id=1, source_target_pairs={{0,24},{1,25},{8,16},{9,17},{16,8},{17,9},{24,0},{25,1},{2,26},{3,... | collective-permute-start | bytes 294920 | tf_op jit(solution)/shard_map/ppermute | solution.py:1211
  213.2 33.6 %collective-permute-start.28 = (bf16[384,128]{1,0:T(8,128)(2,1)}, bf16[384,128]{1,0:T(8,128)(2,1)}, u32[]{:S(2)}, u32[]{:S(2)}) collective-permute-start(bf16[384,128]{1,0:T(8,128)(2,1)} %get-tuple-element.160), channel_id=1, source_target_pairs={{0,16},{1,17},{8,24},{9,25},{16,0},{17,1},{24,8},{25,9},{2,18},{3,... | collective-permute-start | bytes 294920 | tf_op jit(solution)/shard_map/ppermute | solution.py:1211
  214.6 34.7 %collective-permute-start.27 = (bf16[384,128]{1,0:T(8,128)(2,1)}, bf16[384,128]{1,0:T(8,128)(2,1)}, u32[]{:S(2)}, u32[]{:S(2)}) collective-permute-start(bf16[384,128]{1,0:T(8,128)(2,1)} %get-tuple-element.161), channel_id=1, source_target_pairs={{0,8},{1,9},{8,0},{9,1},{16,24},{17,25},{24,16},{25,17},{2,10},{3,... | collective-permute-start | bytes 294920 | tf_op jit(solution)/shard_map/ppermute | solution.py:1211
  238.5 12.5 %collective-permute-start.30 = (bf16[768,128]{1,0:T(8,128)(2,1)S(1)}, bf16[768,128]{1,0:T(8,128)(2,1)S(1)}, u32[]{:S(2)}, u32[]{:S(2)}) collective-permute-start(bf16[768,128]{1,0:T(8,128)(2,1)S(1)} %slice.217.refs_12_), channel_id=1, source_target_pairs={{8,0},{24,16},{9,1},{25,17},{10,2},{26,18},{11,3},{27,19},{12,4},{... | collective-permute-start | bytes 589832 | tf_op jit(solution)/shard_map/ppermute | solution.py:1439
  244.0 9.8 %collective-permute-start.25 = (bf16[192,640]{1,0:T(8,128)(2,1)S(1)}, bf16[192,640]{1,0:T(8,128)(2,1)S(1)}, u32[]{:S(2)}, u32[]{:S(2)}) collective-permute-start(bf16[192,640]{1,0:T(8,128)(2,1)S(1)} %copy-done.51), channel_id=1, source_target_pairs={{0,17},{1,16},{8,25},{9,24},{16,1},{17,0},{24,9},{25,8},{2,19},{3,... | collective-permute-start | bytes 737288 | tf_op jit(solution)/shard_map/ppermute | solution.py:1211
  246.2 12.5 %collective-permute-start.24 = (bf16[192,640]{1,0:T(8,128)(2,1)S(1)}, bf16[192,640]{1,0:T(8,128)(2,1)S(1)}, u32[]{:S(2)}, u32[]{:S(2)}) collective-permute-start(bf16[192,640]{1,0:T(8,128)(2,1)S(1)} %copy-done.50), channel_id=1, source_target_pairs={{0,16},{1,17},{8,24},{9,25},{16,0},{17,1},{24,8},{25,9},{2,18},{3,... | collective-permute-start | bytes 737288 | tf_op jit(solution)/shard_map/ppermute | solution.py:1211
  246.8 12.1 %collective-permute-start.23 = (bf16[192,640]{1,0:T(8,128)(2,1)S(1)}, bf16[192,640]{1,0:T(8,128)(2,1)S(1)}, u32[]{:S(2)}, u32[]{:S(2)}) collective-permute-start(bf16[192,640]{1,0:T(8,128)(2,1)S(1)} %copy-done.49), channel_id=1, source_target_pairs={{0,1},{1,0},{8,9},{9,8},{16,17},{17,16},{24,25},{25,24},{2,3},{3,2... | collective-permute-start | bytes 737288 | tf_op jit(solution)/shard_map/ppermute | solution.py:1211
  249.3 10.8 %collective-permute-start.38 = (bf16[192,128]{1,0:T(8,128)(2,1)S(1)}, bf16[192,128]{1,0:T(8,128)(2,1)S(1)}, u32[]{:S(2)}, u32[]{:S(2)}) collective-permute-start(bf16[192,128]{1,0:T(8,128)(2,1)S(1)} %get-tuple-element.154), channel_id=1, source_target_pairs={{0,25},{1,24},{8,17},{9,16},{16,9},{17,8},{24,1},{25,0},{2,27},{3,... | collective-permute-start | bytes 147464 | tf_op jit(solution)/shard_map/ppermute | solution.py:1211
  251.1 30.6 %collective-permute-start.43 = (bf16[256,768]{1,0:T(8,128)(2,1)S(1)}, bf16[256,768]{1,0:T(8,128)(2,1)S(1)}, u32[]{:S(2)}, u32[]{:S(2)}) collective-permute-start(bf16[256,768]{1,0:T(8,128)(2,1)S(1)} %copy-done.45), channel_id=1, source_target_pairs={{2,0},{4,2},{6,4},{3,1},{5,3},{7,5},{10,8},{12,10},{14,12},{11,9},... | collective-permute-start | bytes 1179656 | tf_op jit(solution)/shard_map/ppermute | solution.py:1444
  260.2 12.4 %collective-permute-start.39 = (bf16[768,128]{1,0:T(8,128)(2,1)S(1)}, bf16[768,128]{1,0:T(8,128)(2,1)S(1)}, u32[]{:S(2)}, u32[]{:S(2)}) collective-permute-start(bf16[768,128]{1,0:T(8,128)(2,1)S(1)} %slice.226), channel_id=1, source_target_pairs={{0,8},{16,24},{1,9},{17,25},{2,10},{18,26},{3,11},{19,27},{4,12},{... | collective-permute-start | bytes 589832 | tf_op jit(solution)/shard_map/ppermute | solution.py:1455
  277.1 9.7 %collective-permute-start.40 = (bf16[48,1664]{1,0:T(8,128)(2,1)}, bf16[48,1664]{1,0:T(8,128)(2,1)S(1)}, u32[]{:S(2)}, u32[]{:S(2)}) collective-permute-start(bf16[48,1664]{1,0:T(8,128)(2,1)} %get-tuple-element.114), channel_id=1, source_target_pairs={{0,2},{2,4},{4,6},{6,0},{1,3},{3,5},{5,7},{7,1},{8,10},{10,12},{12... | collective-permute-start | bytes 479240 | tf_op jit(solution)/shard_map/ppermute | solution.py:1408
  277.1 15.0 %collective-permute-start.41 = (bf16[48,1664]{1,0:T(8,128)(2,1)}, bf16[48,1664]{1,0:T(8,128)(2,1)S(1)}, u32[]{:S(2)}, u32[]{:S(2)}) collective-permute-start(bf16[48,1664]{1,0:T(8,128)(2,1)} %get-tuple-element.115), channel_id=1, source_target_pairs={{0,4},{2,6},{4,0},{6,2},{1,5},{3,7},{5,1},{7,3},{8,12},{10,14},{12... | collective-permute-start | bytes 479240 | tf_op jit(solution)/shard_map/ppermute | solution.py:1408
  277.2 14.9 %collective-permute-start.42 = (bf16[48,1664]{1,0:T(8,128)(2,1)}, bf16[48,1664]{1,0:T(8,128)(2,1)S(1)}, u32[]{:S(2)}, u32[]{:S(2)}) collective-permute-start(bf16[48,1664]{1,0:T(8,128)(2,1)} %get-tuple-element.116), channel_id=1, source_target_pairs={{0,6},{2,0},{4,2},{6,4},{1,7},{3,1},{5,3},{7,5},{8,14},{10,8},{12,... | collective-permute-start | bytes 479240 | tf_op jit(solution)/shard_map/ppermute | solution.py:1408
  (73 other events, 485.3 us)
Sparse Core Ops, SparseCore 0:
  9.9 35.0 all-gather.1
  92.9 54.6 reduce-scatter.2
  149.9 65.8 reduce-scatter.4

commit v2 on v1

--- a/solution.py
+++ b/solution.py
@@ -618,45 +618,17 @@
     return grad_gate.astype(bf16), (grad_hidden * active).astype(bf16)
 
 
-def run_through(x_all, dz_all, weights, produced, received, hidden, dgate, dup):
-    gate_w, up_w, down_w = weights
-    tile = x_all.shape[0] // 2
-    for t in range(2):
-        rows = slice(t * tile, (t + 1) * tile)
-        gate_part = dot_nn(x_all[rows, :], gate_w[...])
-        up_part = dot_nn(x_all[rows, :], up_w[...])
-        sigmoid_value, active, u = silu_parts(gate_part, up_part)
-        hidden[rows, :] = u
-        out = dot_nn(u, down_w[...])
-        grad_hidden = dot_nt(dz_all[rows, :], down_w[...])
-        da, db = silu_grads(grad_hidden, gate_part, up_part, sigmoid_value, active)
-        dgate[rows, :] = da
-        dup[rows, :] = db
-        grad = dot_nt(da, gate_w[...]) + dot_nt(db, up_w[...])
-        produced[rows, :] = out.astype(produced.dtype)
-        received[rows, :] = grad.astype(received.dtype)
-
-
-def run_weights(copies, sources, targets, core, chip, run):
-    gate_hbm, up_hbm, down_hbm = sources
-    gate_w, up_w, down_w = targets
-    columns = gate_w.shape[1]
-    part = pl.ds(pl.multiple_of((2 * chip + run) * columns, columns), columns)
-    return [
-        copies.start(gate_hbm.at[core, :, part], gate_w),
-        copies.start(up_hbm.at[core, :, part], up_w),
-        copies.start(down_hbm.at[core, part, :], down_w),
-    ]
-
-
-def enter_kernel(masks, n_context, n_dp, layout, place, *refs):
+def feed_kernel(masks, n_context, n_dp, layout, place, *refs):
     inputs = refs[:8]
-    (cot_hbm, router, gate_hbm, up_hbm, down_hbm) = refs[8:13]
-    outs_hbm, bundle = refs[13:17], refs[17]
-    (aux, hots, produced, received) = kept = refs[18:22]
-    (x_all, dz_all, field, cot, gate_w, up_w, down_w, hidden, dgate, dup, notes, sems) = refs[22:]
+    (cot_hbm, router, router_t, gate_s_hbm, up_s_hbm, down_s_hbm, gate_hbm, up_hbm, down_hbm) = refs[8:17]
+    (grad_keep_hbm, grad_send_hbm, mix_keep_hbm, mix_send_hbm, router_grad, bundle_hbm) = refs[17:23]
+    (
+        aux, hots, x_all, dz_all, g_all, produced, received, field, cot, gate_w, up_w, down_w, gate_s_w, up_s_w,
+        down_s_w, hidden, dgate, dup, hidden_s, dgate_s, dup_s, grad_tokens, mix_tokens, bundle, notes, sems,
+    ) = refs[23:]
     index, dp, expert, core, chip = place[0], place[1], place[2], place[3], place[4]
     rows = cot.shape[0] // 8
+    width = field.shape[1]
     slots = hots.shape[1]
     copies = Copies(sems)
     ins = []
@@ -667,8 +639,19 @@
             copies.start(inputs[i].at[:rows], field.at[rows_of]),
             copies.start(cot_hbm.at[lax.bitwise_xor(index, masks[i])], cot.at[rows_of]),
         ))
-    weights = (gate_w, up_w, down_w)
-    weights_in = run_weights(copies, (gate_hbm, up_hbm, down_hbm), weights, core, chip, 0)
+    columns = layout.blocks * 128
+    weights_in = []
+    for run in range(2):
+        part = pl.ds(pl.multiple_of((2 * chip + run) * columns, columns), columns)
+        weights_in.append([
+            copies.start(gate_hbm.at[core, :, part], gate_w.at[run]),
+            copies.start(up_hbm.at[core, :, part], up_w.at[run]),
+            copies.start(down_hbm.at[core, part, :], down_w.at[run]),
+        ])
+    shared_in = [
+        copies.start(source, target)
+        for source, target in ((gate_s_hbm, gate_s_w), (up_s_hbm, up_s_w), (down_s_hbm, down_s_w))
+    ]
 
     lanes = lax.broadcasted_iota(jnp.int32, (slots, 128), 1)
     mine = (lanes == expert).astype(f32)
@@ -699,77 +682,37 @@
         theirs = (lanes.astype(f32) == other).astype(f32)
         gate = jax.nn.sigmoid(jnp.sum((mine - theirs) * logits, axis=-1, keepdims=True))
         dz_all[slots_of, :] = (gate * g_slot).astype(bf16)
+        g_all[slots_of, :] = g_slot.astype(bf16)
         aux[slots_of, :] = jnp.where(lanes == 64, gate, gate * (1.0 - gate) * (mine - theirs))
-    outs = [copies.start(source, target) for source, target in zip(kept[:2], outs_hbm[:2])]
-
-    for copy in weights_in:
-        copy.wait()
-    run_through(x_all, dz_all, weights, produced, received, hidden, dgate, dup)
-    outs += [copies.start(source, target) for source, target in zip(kept[2:], outs_hbm[2:])]
-    expert_grads(
-        bundle, x_all, dz_all, hidden, dgate, dup, 0, n_dp * layout.run_place, layout.run_place, dp, n_context, n_dp
-    )
-    for copy in outs:
-        copy.wait()
-
-
-def leave_kernel(masks, n_context, n_dp, layout, place, *refs):
-    kept_hbm, inputs, cot_hbm = refs[:4], refs[4:12], refs[12]
-    (router_t, gate_s_hbm, up_s_hbm, down_s_hbm, gate_hbm, up_hbm, down_hbm) = refs[13:20]
-    (grad_keep_hbm, grad_send_hbm, mix_keep_hbm, mix_send_hbm, router_grad, bundle) = refs[20:26]
-    (aux, hots, produced0, received0) = kept = refs[26:30]
-    (
-        x_all, dz_all, g_all, produced, received, field, cot, gate_w, up_w, down_w, gate_s_w, up_s_w, down_s_w,
-        hidden, dgate, dup, hidden_s, dgate_s, dup_s, grad_tokens, mix_tokens, slot_out, sems,
-    ) = refs[30:]
-    index, dp, core, chip = place[0], place[1], place[3], place[4]
-    rows = cot.shape[0] // 8
-    width = field.shape[1]
-    slots = hots.shape[1]
-    copies = Copies(sems)
-    kept_in = [copies.start(source, target) for source, target in zip(kept_hbm[:2], kept[:2])]
-    ins = []
-    for i in range(8):
-        rows_of = slice(i * rows, (i + 1) * rows)
-        ins.append((
-            copies.start(inputs[i].at[:rows], field.at[rows_of]),
-            copies.start(cot_hbm.at[lax.bitwise_xor(index, masks[i])], cot.at[rows_of]),
-        ))
-    weights = (gate_w, up_w, down_w)
-    weights_in = run_weights(copies, (gate_hbm, up_hbm, down_hbm), weights, core, chip, 1)
-    shared_in = [
-        copies.start(source, target)
-        for source, target in (
-            (gate_s_hbm, gate_s_w), (up_s_hbm, up_s_w), (down_s_hbm, down_s_w), *zip(kept_hbm[2:], kept[2:])
-        )
-    ]
-    for copy in kept_in:
-        copy.wait()
-    for i in range(8):
-        rows_of = slice(i * rows, (i + 1) * rows)
-        slots_of = slice(i * slots, (i + 1) * slots)
-        for copy in ins[i]:
+
+    tile = x_all.shape[0] // 2
+    for run in range(2):
+        for copy in weights_in[run]:
             copy.wait()
-        x_all[slots_of, :] = dot_nn(hots[i], field[rows_of, :]).astype(bf16)
-        g_slot = dot_nn(hots[i], cot[rows_of, :])
-        g_all[slots_of, :] = g_slot.astype(bf16)
-        dz_all[slots_of, :] = (aux[slots_of, 64:65] * g_slot).astype(bf16)
-    for copy in weights_in:
-        copy.wait()
-    run_through(x_all, dz_all, weights, produced, received, hidden, dgate, dup)
+        for t in range(2):
+            part = slice(t * tile, (t + 1) * tile)
+            gate_part = dot_nn(x_all[part, :], gate_w[run])
+            up_part = dot_nn(x_all[part, :], up_w[run])
+            sigmoid_value, active, u = silu_parts(gate_part, up_part)
+            hidden[part, :] = u
+            out = dot_nn(u, down_w[run])
+            grad_hidden = dot_nt(dz_all[part, :], down_w[run])
+            da, db = silu_grads(grad_hidden, gate_part, up_part, sigmoid_value, active)
+            dgate[part, :] = da
+            dup[part, :] = db
+            grad = dot_nt(da, gate_w[run]) + dot_nt(db, up_w[run])
+            if run == 0:
+                produced[part, :] = out
+                received[part, :] = grad
+            else:
+                produced[part, :] += out
+                received[part, :] += grad
+        expert_grads(bundle, x_all, dz_all, hidden, dgate, dup, layout, run, dp, n_context, n_dp)
 
     for copy in shared_in:
         copy.wait()
-    z = produced[...] + produced0[...].astype(f32)
-    gate = aux[:, 64:65]
-    pick = jnp.sum(z.astype(bf16).astype(f32) * g_all[...].astype(f32), axis=-1, keepdims=True)
-    lanes = lax.broadcasted_iota(jnp.int32, aux.shape, 1)
-    dlogits = (jnp.where(lanes < 64, aux[...], 0.0) * pick).astype(bf16)
-    slot_out[:, width:] = (gate * z).astype(bf16)
-    grad = received[...] + received0[...].astype(f32)
-    slot_out[:, :width] = (grad + dot_nn(dlogits, router_t[...])).astype(bf16)
-    router_grad[...] = dot_tn(x_all[...], dlogits)
-    outs = []
+    router_sum = jnp.zeros((width, 128), f32)
+    outs, last = [], {}
     for t in range(4):
         tile = slice(2 * t * rows, 2 * (t + 1) * rows)
         gate_part = dot_nn(field[tile, :], gate_s_w[...])
@@ -782,74 +725,78 @@
         dgate_s[tile, :] = da
         dup_s[tile, :] = db
         grad_in = dot_nt(da, gate_s_w[...]) + dot_nt(db, up_s_w[...])
+        for copy in last.pop(t - 2, []):
+            copy.wait()
         for half in range(2):
             i = 2 * t + half
             rows_of = slice(half * rows, (half + 1) * rows)
-            back = dot_tn(hots[i], slot_out[i * slots:(i + 1) * slots, :])
-            grad_tokens[i] = (grad_in[rows_of, :] + back[:, :width]).astype(bf16)
-            mix_tokens[i] = (mixed[rows_of, :] + back[:, width:]).astype(bf16)
-        for i in (2 * t, 2 * t + 1):
+            slots_of = slice(i * slots, (i + 1) * slots)
+            z = produced[slots_of, :]
+            extra = aux[slots_of, :]
+            gate = extra[:, 64:65]
+            pick = jnp.sum(z.astype(bf16).astype(f32) * g_all[slots_of, :].astype(f32), axis=-1, keepdims=True)
+            dlogits = (jnp.where(lanes < 64, extra, 0.0) * pick).astype(bf16)
+            router_sum = router_sum + dot_tn(x_all[slots_of, :], dlogits)
+            grad = (received[slots_of, :] + dot_nn(dlogits, router_t[...])).astype(bf16)
+            back = dot_tn(hots[i], jnp.concatenate([grad, (gate * z).astype(bf16)], axis=1))
+            slot = (2 * t + half) % 4
+            grad_tokens[slot] = (grad_in[rows_of, :] + back[:, :width]).astype(bf16)
+            mix_tokens[slot] = (mixed[rows_of, :] + back[:, width:]).astype(bf16)
+        last[t] = []
+        for half in range(2):
+            i = 2 * t + half
             for source, targets in (
                 (grad_tokens, (grad_keep_hbm, grad_send_hbm)), (mix_tokens, (mix_keep_hbm, mix_send_hbm))
             ):
-                outs.append(copies.start(source.at[i], targets[i // 4].at[i % 4]))
-
-    every = slice(None)
-    shared_place, run_place = layout.shared_place, layout.run_place
-    slab_rows = shared_place + run_place
+                last[t].append(copies.start(source.at[i % 4], targets[i // 4].at[i % 4]))
+    router_grad[...] = router_sum
+
     for mat, source in enumerate((dgate_s, dup_s)):
         offset = mat * layout.shared_blocks * layout.piece
-        matrix_grads(bundle, field, source, offset, slab_rows, dp, n_context, n_dp)
+        matrix_grads(bundle, field, source, offset, layout, dp, n_context, n_dp)
+    outs += [
+        copies.start(bundle.at[start:start + layout.shared_down_at], bundle_hbm.at[start:start + layout.shared_down_at])
+        for start in range(0, n_context * layout.total, layout.total)
+    ]
     grad = dot_tn(hidden_s[...], cot[...]).astype(bf16)
     down_rows = layout.down_rows
-    total_rows = bundle.shape[0] // n_context
     for z in range(n_context):
         for lane in range(width // 128):
-            start = z * total_rows + n_dp * slab_rows + lane * down_rows
+            start = z * layout.total + layout.shared_down_at + lane * down_rows
             bundle[start:start + down_rows, :] = grad[z * down_rows:(z + 1) * down_rows, lane * 128:(lane + 1) * 128]
-    expert_grads(
-        bundle, x_all, dz_all, hidden, dgate, dup, shared_place, total_rows - width, slab_rows, dp, n_context, n_dp
-    )
-    for copy in outs:
+    for z in range(n_context):
+        part = slice(z * layout.total + layout.shared_down_at, (z + 1) * layout.total)
+        outs.append(copies.start(bundle.at[part], bundle_hbm.at[part]))
+    for copy in sum(last.values(), outs):
         copy.wait()
 
 
-def store_grads(bundle, grad, part, offset, place_rows, dp, n_context, piece):
-    total_rows = bundle.shape[0] // n_context
-    slab = lax.bitwise_xor(part, dp) * place_rows
-    for z in range(n_context):
-        for lane in range(grad.shape[1] // 128):
-            start = z * total_rows + slab + offset + lane * piece
-            bundle[pl.ds(pl.multiple_of(start, 16), piece), :] = grad[
-                z * piece:(z + 1) * piece, lane * 128:(lane + 1) * 128
-            ]
-
-
-def matrix_grads(bundle, left, right, offset, place_rows, dp, n_context, n_dp):
+def matrix_grads(bundle, left, right, offset, layout, dp, n_context, n_dp):
     block = left.shape[1] // n_dp
+    piece = block // n_context
     tile = 2 * block
     for t in range(n_dp // 2):
         grad = dot_tn(left[:, t * tile:(t + 1) * tile], right[...]).astype(bf16)
         for half in range(2):
-            store_grads(
-                bundle, grad[half * block:(half + 1) * block], 2 * t + half, offset, place_rows, dp, n_context,
-                block // n_context,
-            )
-
-
-def expert_grads(bundle, x, dz, hidden, dgate, dup, offset, down_at, place_rows, dp, n_context, n_dp):
-    width, columns = x.shape[1], hidden.shape[1]
+            slab = lax.bitwise_xor(2 * t + half, dp) * layout.place
+            for z in range(n_context):
+                for lane in range(grad.shape[1] // 128):
+                    start = z * layout.total + slab + offset + lane * piece
+                    bundle[pl.ds(pl.multiple_of(start, 16), piece), :] = grad[
+                        half * block + z * piece:half * block + (z + 1) * piece, lane * 128:(lane + 1) * 128
+                    ]
+
+
+def expert_grads(bundle, x, dz, hidden, dgate, dup, layout, run, dp, n_context, n_dp):
+    width = x.shape[1]
     tile = 2 * width // n_dp
-    total_rows = bundle.shape[0] // n_context
     for mat, source in enumerate((dgate, dup)):
-        matrix_grads(
-            bundle, x, source, offset + mat * (columns // 128) * (width // n_dp // n_context), place_rows, dp,
-            n_context, n_dp,
-        )
+        offset = layout.shared_place + run * layout.run_place + mat * layout.blocks * layout.piece
+        matrix_grads(bundle, x, source, offset, layout, dp, n_context, n_dp)
     for t in range(n_dp // 2):
         grad = dot_tn(dz[:, t * tile:(t + 1) * tile], hidden[...]).astype(bf16)
         for z in range(n_context):
-            start = z * total_rows + down_at + t * tile
+            start = z * layout.total + layout.down_at + run * width + t * tile
             bundle[start:start + tile, :] = grad[:, z * 128:(z + 1) * 128]
 
 
@@ -859,8 +806,11 @@
         self.shared_blocks, self.blocks = hidden // 8 // 128, hidden // 4 // 128
         self.shared_place = 2 * self.shared_blocks * self.piece
         self.run_place = 2 * self.blocks * self.piece
+        self.place = self.shared_place + 2 * self.run_place
+        self.shared_down_at = n_dp * self.place
         self.down_rows = hidden // 8 // n_context
-        self.shared_down = self.down_rows * (width // 128)
+        self.down_at = self.shared_down_at + self.down_rows * (width // 128)
+        self.total = self.down_at + 2 * width
 
 
 def feed_grads_kernel(n_dp, layout, place, *refs):
@@ -871,9 +821,10 @@
         del refs[:count]
         return part
 
-    runs = [take(n_dp), take(n_dp)]
+    slabs = take(n_dp)
     shared_far = take(n_dp)
-    downs, got_downs = take(2), take(2)
+    downs = take(1)[0]
+    got_downs = take(2)
     (gate, up, down, gate_s, up_s, down_s) = refs
     dp, side = place[1], place[5]
     core = place[3]
@@ -889,12 +840,12 @@
             begin = (source // 2) * (2 * columns) + run * columns
             for mat, target in enumerate((gate, up)):
                 for lane in range(layout.blocks):
-                    start = run * layout.shared_place + (mat * layout.blocks + lane) * piece
-                    target[which, :, pl.ds(pl.multiple_of(begin + lane * 128, 128), 128)] = runs[run][mask][
+                    start = layout.shared_place + run * layout.run_place + (mat * layout.blocks + lane) * piece
+                    target[which, :, pl.ds(pl.multiple_of(begin + lane * 128, 128), 128)] = slabs[mask][
                         start:start + piece, :
                     ].astype(f32)
-    shared_down = layout.shared_down
-    kept = jnp.where(core == 0, downs[0][...], downs[1][shared_down:, :])
+    base = layout.down_at - layout.shared_down_at
+    kept = jnp.where(core == 0, downs[base:base + width, :], downs[base + width:, :])
     got = jnp.where(core == 0, got_downs[0][...], got_downs[1][...])
     down[core] = kept.astype(f32).T
     down[1 - core] = got.astype(f32).T
@@ -905,7 +856,7 @@
         for mat, target in enumerate((gate_s, up_s)):
             for lane in range(layout.shared_blocks):
                 start = (mat * layout.shared_blocks + lane) * piece
-                own = runs[1][mask][start:start + piece, :].astype(f32)
+                own = slabs[mask][start:start + piece, :].astype(f32)
                 far = shared_far[mask][start:start + piece, :].astype(f32)
                 first = jnp.where(side == 0, own, far)
                 second = jnp.where(side == 0, far, own)
@@ -921,7 +872,7 @@
         rows = slice(lane * down_rows, (lane + 1) * down_rows)
         far_rows = slice(layout.shared_place + rows.start, layout.shared_place + rows.stop)
         lanes = slice(lane * 128, (lane + 1) * 128)
-        down_s[pl.ds(pl.multiple_of(side * down_rows, 16), down_rows), lanes] = downs[1][rows, :].astype(f32)
+        down_s[pl.ds(pl.multiple_of(side * down_rows, 16), down_rows), lanes] = downs[rows, :].astype(f32)
         down_s[pl.ds(pl.multiple_of((1 - side) * down_rows, 16), down_rows), lanes] = shared_far[0][
             far_rows, :
         ].astype(f32)
@@ -929,8 +880,8 @@
 
 def last_kernel(blocks, place, *refs):
     packs, (token, gain1, grad_own, grad_middle) = refs[:2], refs[2:6]
-    pulled = refs[6:5 + blocks]
-    (input_grad, qkv, out, norm1, norm2, router) = refs[5 + blocks:]
+    pulled = refs[6:4 + blocks]
+    (input_grad, qkv, out, norm1, norm2, router) = refs[4 + blocks:]
     side = place[5]
     piece, width = out.shape
     own, far_half = packs[0][...].astype(f32), packs[1][...].astype(f32)
@@ -1310,48 +1261,29 @@
     for mask in keep_masks:
         near[mask ^ 2] = swap(near[mask], 2)
 
-    slot_act, slot_chunk, slot_notes = (8 * slots, width), (8 * slots, chunk_columns), (8 * slots, 128)
-    row_act, row_hidden = (8 * rows, width), (8 * rows, shared_columns)
     layout = Layout(width, hidden, n_dp, n_context)
-    rows0 = n_context * (n_dp * layout.run_place + width)
-    rows1 = n_context * (n_dp * (layout.shared_place + layout.run_place) + layout.shared_down + width)
-    run_scratch = [
-        *[pltpu.VMEM((width, chunk_columns), bf16)] * 2, pltpu.VMEM((chunk_columns, width), bf16),
-    ]
-    kept = [(slot_notes, f32), ((8, slots, rows), bf16), *[(slot_act, bf16)] * 2]
-    every = [near[mask] for mask in all_masks]
-    *entered, bundle0 = call(
-        partial(enter_kernel, all_masks, n_context, n_dp, layout),
-        [*[(*out, far) for out in kept], ((rows0, 128), bf16, copied)],
+    slot_act, row_act, four = (8 * slots, width), (8 * rows, width), (4, rows, width)
+    bundle_rows = n_context * layout.total
+    grad_keep, grad_send, mix_keep, mix_send, router_part, bundle = call(
+        partial(feed_kernel, all_masks, n_context, n_dp, layout),
+        [*[(four, bf16, far)] * 4, ((width, 128), f32, copied), ((bundle_rows, 128), bf16, far)],
         [
-            *[pltpu.VMEM(*out) for out in kept], *[pltpu.VMEM(slot_act, bf16)] * 2, *[pltpu.VMEM(row_act, bf16)] * 2,
-            *run_scratch, *[pltpu.VMEM(slot_chunk, bf16)] * 3, pltpu.VMEM((8, 16, width), bf16),
-            pltpu.SemaphoreType.DMA((40,)),
-        ],
-        scalars,
-        [*many(far, *every, cot_all), (router, copied), *many(far, expert_gate, expert_up, expert_down)],
-        limit=56,
-    )
-    sum0 = lax.psum_scatter(bundle0, CONTEXT, scatter_dimension=0, tiled=True)
-    four = (4, rows, width)
-    grad_keep, grad_send, mix_keep, mix_send, router_part, bundle1 = call(
-        partial(leave_kernel, all_masks, n_context, n_dp, layout),
-        [*[(four, bf16, far)] * 4, ((width, 128), f32, copied), ((rows1, 128), bf16, copied)],
-        [
-            *[pltpu.VMEM(*out) for out in kept], *[pltpu.VMEM(slot_act, bf16)] * 3, *[pltpu.VMEM(slot_act, f32)] * 2,
-            *[pltpu.VMEM(row_act, bf16)] * 2, *run_scratch, *[pltpu.VMEM((width, shared_columns), bf16)] * 2, pltpu.VMEM((shared_columns, width), bf16),
-            *[pltpu.VMEM(slot_chunk, bf16)] * 3, *[pltpu.VMEM(row_hidden, bf16)] * 3,
-            *[pltpu.VMEM((8, rows, width), bf16)] * 2, pltpu.VMEM((8 * slots, 2 * width), bf16),
-            pltpu.SemaphoreType.DMA((56,)),
+            pltpu.VMEM((8 * slots, 128), f32), pltpu.VMEM((8, slots, rows), bf16), *[pltpu.VMEM(slot_act, bf16)] * 3,
+            *[pltpu.VMEM(slot_act, f32)] * 2, *[pltpu.VMEM(row_act, bf16)] * 2,
+            *[pltpu.VMEM((2, width, chunk_columns), bf16)] * 2, pltpu.VMEM((2, chunk_columns, width), bf16),
+            *[pltpu.VMEM((width, shared_columns), bf16)] * 2, pltpu.VMEM((shared_columns, width), bf16),
+            *[pltpu.VMEM((8 * slots, chunk_columns), bf16)] * 3, *[pltpu.VMEM((8 * rows, shared_columns), bf16)] * 3,
+            *[pltpu.VMEM(four, bf16)] * 2, pltpu.VMEM((bundle_rows, 128), bf16), pltpu.VMEM((8, 16, width), bf16),
+            pltpu.SemaphoreType.DMA((64,)),
         ],
         scalars,
         [
-            *many(far, *entered, *every, cot_all), (router_t, copied),
+            *many(far, *[near[mask] for mask in all_masks], cot_all), *many(copied, router, router_t),
             *many(far, *picked, expert_gate, expert_up, expert_down),
         ],
-        limit=58,
-    )
-    sum1 = lax.psum_scatter(bundle1, CONTEXT, scatter_dimension=0, tiled=True)
+        limit=60,
+    )
+    reduced = lax.psum_scatter(bundle, CONTEXT, scatter_dimension=0, tiled=True)
 
     def add_blocks(left, right):
         return [
@@ -1433,30 +1365,33 @@
     )
     grad_own, keep1 = results[0], results[blocks]
     *grad_far, send1 = hold_until(scalars, [*results[1:blocks], results[blocks + 1]], arrived0[1:])
-    run0 = [sum0[m * layout.run_place:(m + 1) * layout.run_place] for m in range(n_dp)]
-    run0 = [run0[0]] + [swap(run0[m], 2 * m) for m in range(1, n_dp)]
-    down0 = sum0[n_dp * layout.run_place:]
-    got_down0 = lax.ppermute(down0, DP, [(i, i ^ 1) for i in range(n_dp) if i % 2 == 1])
     output = sum(value.astype(f32) for value in mix_parts).astype(bf16)[None]
 
     arrived1 = by_chips(keep1, send1)
-    pulled = [
-        lax.ppermute(grad_far[r - 1], CONTEXT, [(i, i - r) for i in range(r, n_context)])
-        for r in range(1, blocks)
+    passed = lax.ppermute(grad_far[1], CONTEXT, [(i, i - 1) for i in range(2, n_context)])
+    farther = [
+        lax.ppermute(grad_far[r - 1], CONTEXT, [(i, i - r) for i in range(r, n_context)]) for r in range(3, blocks)
     ]
-    sum1, = hold_until(scalars, [sum1], [arrived1[0], *pulled[2:]])
-    slab_rows = layout.shared_place + layout.run_place
-    run1 = [sum1[m * slab_rows:(m + 1) * slab_rows] for m in range(n_dp)]
-    downs1 = sum1[n_dp * slab_rows:]
-    shared = [slab[:layout.shared_place] for slab in run1]
-    shared[0] = jnp.concatenate([shared[0], downs1[:layout.shared_down]], axis=0)
+    nearest = (grad_far[0].astype(f32) + passed.astype(f32)).astype(bf16)
+    pulled = [lax.ppermute(nearest, CONTEXT, [(i, i - 1) for i in range(1, n_context)]), *farther]
+    shares = by_context([arrived0, arrived1], [passed, *farther])
+    reduced, = hold_until(scalars, [reduced], [shares[0]])
+    slabs = [reduced[m * layout.place:(m + 1) * layout.place] for m in range(n_dp)]
+    downs = reduced[layout.shared_down_at:]
+    base = layout.down_at - layout.shared_down_at
+    shared = [slab[:layout.shared_place] for slab in slabs]
+    shared[0] = jnp.concatenate([shared[0], downs[:base]], axis=0)
     shared_far = [swap(value, 2 * m + 1) for m, value in enumerate(shared)]
-    run1 = [run1[0]] + [swap(run1[m], 2 * m) for m in range(1, n_dp)]
-    got_down1 = lax.ppermute(
-        downs1[layout.shared_down:], DP, [(i, i ^ 1) for i in range(n_dp) if i % 2 == 0]
-    )
-
-    shares = by_context([arrived0, arrived1], [pulled[1], *run0[1:], got_down0, *run1[1:], *shared_far, got_down1])
+    slabs = [slabs[0]] + [swap(slabs[m], 2 * m) for m in range(1, n_dp)]
+    got_downs = [
+        lax.ppermute(
+            downs[base + run * width:base + (run + 1) * width], DP, [(i, i ^ 1) for i in range(n_dp) if i % 2 != run]
+        )
+        for run in range(2)
+    ]
+
+    shares = [shares[0], *hold_until(scalars, shares[1:], [pulled[0], *slabs[1:], *shared_far, *got_downs])]
+    spread = total(shares)
     gate_grad, up_grad, down_grad, gate_s_grad, up_s_grad, down_s_grad = call(
         partial(feed_grads_kernel, n_dp, layout),
         [
@@ -1468,11 +1403,10 @@
         ],
         [],
         scalars,
-        many(copied, *run0, *run1, *shared_far, down0, downs1, got_down0, got_down1),
-        [shares[0], *pulled],
+        many(copied, *slabs, *shared_far, downs, *got_downs),
+        [spread[0]],
         limit=32,
     )
-    shares = [shares[0], *hold_until(scalars, shares[1:], [down_s_grad])]
     input_grad, qkv_grad, out_grad, norm1_grad, norm2_grad, router_grad = call(
         partial(last_kernel, blocks),
         [
@@ -1481,7 +1415,7 @@
         ],
         [],
         scalars,
-        many(copied, *total(shares), own, gain1, grad_own, grad_middle, *pulled),
+        many(copied, *spread, own, gain1, grad_own, grad_middle, *pulled),
         limit=32,
     )
     return (

time: 318 us -> 308 us (0.969)
  Pallas kernels: 125 us -> 119 us
  waiting for transfers between devices: 90.4 us -> 94.8 us
  local copies, waits for them, and re-layouts: 21 us -> 17.4 us
    ppermute x3 -> x1, waiting for transfers between devices: 24.8 us -> 35 us  [on_block(): lax.ppermute(grad_far[r - 1], CONTEXT, [(i, i - r) for i in range(r, n_co...]
    ppermute x34 -> x31, waiting for transfers between devices: 53.8 us -> 46.2 us  [swap(): return lax.ppermute(value, group, [(i, i ^ mask) for i in range(8)])]
    pallas_call x14 -> x13, Pallas kernels: 125 us -> 119 us  [call(): pl.pallas_call(body, grid_spec=pltpu.PrefetchScalarGridSpec(num_scalar_pr...]
    slice x7 -> x5, local copies, waits for them, and re-layouts: 6.88 us -> 3.03 us  [the longest x1 2.17 us: on_block(): reduced[m * layout.place:(m + 1) * layout.place]]
    ppermute x34 -> x31, starting transfers between devices: 28.5 us -> 27.6 us  [swap(): return lax.ppermute(value, group, [(i, i ^ mask) for i in range(8)])]
    unnamed x115 -> x103, local copies, waits for them, and re-layouts: 9.36 us -> 9.59 us
  transfers between devices with their start and end apart: 48 -> 44, of which waited for: 20 -> 17; matrix products, arithmetic and copies ran while one was open for 7% -> 6% of each run, Pallas kernels for 32% -> 23%
where the time goes in v2:
time: 308 us; the launch traced here: 302 us
  Pallas kernels  119 us (39%)
  waiting for transfers between devices  94.8 us (31%)
  starting transfers between devices  47.4 us (15%)
  local copies, waits for them, and re-layouts  17.4 us (6%)
  between operations  15 us (5%)
  other arithmetic  9.17 us (3%)
    pallas_call x13, Pallas kernels, call(): pl.pallas_call(body, grid_spec=pltpu.PrefetchScalarGridSpec(num_scalar_pr...  119 us
    ppermute x31, waiting for transfers between devices, swap(): return lax.ppermute(value, group, [(i, i ^ mask) for i in range(8)])  46.2 us
    ppermute x1, waiting for transfers between devices, on_block(): lax.ppermute(grad_far[r - 1], CONTEXT, [(i, i - r) for i in range(r, n_co...  35 us
    ppermute x31, starting transfers between devices, swap(): return lax.ppermute(value, group, [(i, i ^ mask) for i in range(8)])  27.6 us
    unnamed x103, local copies, waits for them, and re-layouts  9.59 us
    ppermute x1, waiting for transfers between devices, on_block(): lax.ppermute(own, CONTEXT, [(i, i + 1) for i in range(n_context - 1)])  6.44 us
  transfers between devices with their start and end apart: 44, of which 17 were waited for; matrix products, arithmetic and copies ran while one was open for 6% of the time, Pallas kernels for 23%

profile of v2, /device:TPU:0, one launch (start us, length us, event | category | flops | bytes accessed | tf_op | source)
XLA Modules:
  0.0 302.4 jit_solution(8230836126422529460)
XLA Ops:
  8.0 5.0 %collective-permute-start = (bf16[256,768]{1,0:T(8,128)(2,1)}, bf16[256,768]{1,0:T(8,128)(2,1)S(1)}, u32[]{:S(2)}, u32[]{:S(2)}) collective-permute-start(bf16[256,768]{1,0:T(8,128)(2,1)} %bitcast.56), channel_id=1, source_target_pairs={{0,2},{2,4},{4,6},{1,3},{3,5},{5,7},{8,10},{10,12},{12,14},{9,11},... | collective-permute-start | bytes 1179656 | tf_op jit(solution)/shard_map/ppermute | solution.py:1199
  12.9 3.4 %collective-permute-start.2 = (bf16[256,768]{1,0:T(8,128)(2,1)}, bf16[256,768]{1,0:T(8,128)(2,1)S(1)}, u32[]{:S(2)}, u32[]{:S(2)}) collective-permute-start(bf16[256,768]{1,0:T(8,128)(2,1)} %bitcast.57), channel_id=1, source_target_pairs={{0,6},{1,7},{8,14},{9,15},{16,22},{17,23},{24,30},{25,31}} | collective-permute-start | bytes 1179656 | tf_op jit(solution)/shard_map/ppermute | solution.py:1202
  16.3 6.4 %collective-permute-done.refs_1_ = bf16[256,768]{1,0:T(8,128)(2,1)S(1)} collective-permute-done((bf16[256,768]{1,0:T(8,128)(2,1)}, bf16[256,768]{1,0:T(8,128)(2,1)S(1)}, u32[]{:S(2)}, u32[]{:S(2)}) %collective-permute-start) | collective-permute-done | bytes 393248 | tf_op jit(solution)/shard_map/ppermute | solution.py:1199
  29.1 4.0 %shard_map.264 = (bf16[768,256]{1,0:T(8,128)(2,1)}, bf16[768,256]{1,0:T(8,128)(2,1)}, bf16[256,768]{1,0:T(8,128)(2,1)}) custom-call(s32[7]{0:T(128)S(1)} %stack.32.place, bf16[768,2048]{1,0:T(8,128)(2,1)} %refs_0_.1, bf16[768,2048]{1,0:T(8,128)(2,1)} %refs_1_.1, bf16[2048,768]{1,0:T(8,128)(2,1)} %refs_2_.1, bf16[768,128]{1,0:T(8,128)(2,1)} %pad.8.refs_3_.refs_9_, ...), custom_call_target="tpu_custom_call" | custom-call | flops 100000000 | tf_op jit(solution)/shard_map/pallas_call | solution.py:1130
  34.0 16.9 %shard_map.265 = (bf16[1024,768]{1,0:T(8,128)(2,1)}, bf16[256,768]{1,0:T(8,128)(2,1)}, bf16[1024,768]{1,0:T(8,128)(2,1)}, bf16[1024,768]{1,0:T(8,128)(2,1)}, f32...) custom-call(s32[1]{0:T(128)} %bitcast.place, ...), custom_call_target="tpu_custom_call" | custom-call | flops 100000000 | tf_op jit(solution)/shard_map/pallas_call | solution.py:1130
  50.9 1.6 collective-permute-start.3
  54.0 6.6 %collective-permute-done.3.refs_1_ = bf16[272,768]{1,0:T(8,128)(2,1)S(1)} collective-permute-done((bf16[272,768]{1,0:T(8,128)(2,1)}, bf16[272,768]{1,0:T(8,128)(2,1)S(1)}, u32[]{:S(2)}, u32[]{:S(2)}) %collective-permute-start.3) | collective-permute-done | bytes 417824 | tf_op jit(solution)/shard_map/ppermute | solution.py:1162
  63.4 7.3 %collective-permute-done.5.refs_3_ = bf16[272,768]{1,0:T(8,128)(2,1)S(1)} collective-permute-done((bf16[272,768]{1,0:T(8,128)(2,1)S(1)}, bf16[272,768]{1,0:T(8,128)(2,1)S(1)}, u32[]{:S(2)}, u32[]{:S(2)}) %collective-permute-start.5) | collective-permute-done | bytes 417824 | tf_op jit(solution)/shard_map/ppermute | solution.py:1162
  70.8 1.7 collective-permute-done.9.refs_7_
  73.3 43.9 %shard_map.266 = (bf16[4,256,768]{2,1,0:T(8,128)(2,1)}, bf16[4,256,768]{2,1,0:T(8,128)(2,1)}, bf16[4,256,768]{2,1,0:T(8,128)(2,1)}, bf16[4,256,768]{2,1,0:T(8,12...) custom-call(s32[7]{0:T(128)} %copy-done.2, bf16[272,768]{1,0:T(8,128)(2,1)} %get-tuple-element.71.refs_0_, ...), custom_call_target="tpu_custom_call" | custom-call | flops 100000000 | tf_op jit(solution)/shard_map/pallas_call | solution.py:1130
  119.1 3.7 %collective-permute-done.11 = bf16[4,256,768]{2,1,0:T(8,128)(2,1)S(1)} collective-permute-done((bf16[4,256,768]{2,1,0:T(8,128)(2,1)S(1)}, bf16[4,256,768]{2,1,0:T(8,128)(2,1)S(1)}, u32[]{:S(2)}, u32[]{:S(2)}) %collective-permute-start.11) | collective-permute-done | bytes 1572896 | tf_op jit(solution)/shard_map/ppermute | solution.py:1162
  122.8 2.6 fusion.11
  125.4 1.6 collective-permute-start.14
  127.3 1.6 collective-permute-start.12
  130.0 8.3 %collective-permute-done.14.refs_5_.refs_3_ = bf16[256,768]{1,0:T(8,128)(2,1)S(1)} collective-permute-done((bf16[256,768]{1,0:T(8,128)(2,1)S(1)}, bf16[256,768]{1,0:T(8,128)(2,1)S(1)}, u32[]{:S(2)}, u32[]{:S(2)}) %collective-permute-start.14) | collective-permute-done | bytes 393248 | tf_op jit(solution)/shard_map/ppermute | solution.py:1162
  138.3 6.6 %collective-permute-done.13.refs_4_.refs_2_ = bf16[256,768]{1,0:T(8,128)(2,1)S(1)} collective-permute-done((bf16[256,768]{1,0:T(8,128)(2,1)S(1)}, bf16[256,768]{1,0:T(8,128)(2,1)S(1)}, u32[]{:S(2)}, u32[]{:S(2)}) %collective-permute-start.13) | collective-permute-done | bytes 393248 | tf_op jit(solution)/shard_map/ppermute | solution.py:1162
  150.7 18.4 %shard_map.268 = (f32[256,768]{1,0:T(8,128)}, bf16[256,768]{1,0:T(8,128)(2,1)}, bf16[256,384]{1,0:T(8,128)(2,1)}, bf16[1024,768]{1,0:T(8,128)(2,1)}, f32[8,768]{...) custom-call(s32[7]{0:T(128)S(1)} %copy-done.3, ...), custom_call_target="tpu_custom_call" | custom-call | flops 100000000 | tf_op jit(solution)/shard_map/pallas_call | solution.py:1130
  170.8 3.6 %collective-permute-done.18 = bf16[2,2,192,1024]{3,2,1,0:T(8,128)(2,1)S(1)} collective-permute-done((bf16[2,2,192,1024]{3,2,1,0:T(8,128)(2,1)}, bf16[2,2,192,1024]{3,2,1,0:T(8,128)(2,1)S(1)}, u32[]{:S(2)}, u32[]{:S(2)}) %collective-permute-start.18) | collective-permute-done | bytes 1572896 | tf_op jit(solution)/shard_map/ppermute | solution.py:1162
  175.8 1.7 collective-permute-start.21
  179.3 21.3 %shard_map.270 = (f32[256,768]{1,0:T(8,128)}, bf16[256,768]{1,0:T(8,128)(2,1)}, bf16[256,768]{1,0:T(8,128)(2,1)}, bf16[256,768]{1,0:T(8,128)(2,1)}, bf16[2,2,192...) custom-call(s32[7]{0:T(128)S(1)} %copy-done.3, bf16[256,768]{1,0:T(8,128)(2,1)} %bitcast.59, ...), custom_call_target="tpu_custom_call" | custom-call | flops 100000000 | tf_op jit(solution)/shard_map/pallas_call | solution.py:1130
  206.0 1.7 collective-permute-start.25
  211.7 35.0 %collective-permute-done.27.refs_9_.refs_7_ = bf16[256,768]{1,0:T(8,128)(2,1)S(1)} collective-permute-done((bf16[256,768]{1,0:T(8,128)(2,1)}, bf16[256,768]{1,0:T(8,128)(2,1)S(1)}, u32[]{:S(2)}, u32[]{:S(2)}) %collective-permute-start.27) | collective-permute-done | bytes 393248 | tf_op jit(solution)/shard_map/ppermute | solution.py:1373
  247.7 3.2 %shard_map.272 = (bf16[48,1664]{1,0:T(8,128)(2,1)}, bf16[48,1664]{1,0:T(8,128)(2,1)}, bf16[48,1664]{1,0:T(8,128)(2,1)}, bf16[48,1664]{1,0:T(8,128)(2,1)}) custom-call(s32[7]{0:T(128)S(1)} %copy-done.3, bf16[192,1024]{1,0:T(8,128)(2,1)} %get-tuple-element.128.refs_18_.refs_0_, bf16[192,1024]{1,0:T(8,128)(2,1)} %copy-done.26, bf16[192,1024]{1,0:T(8,128)(2,1)} %copy-done.25, ...), custom_call_target="tpu_custom_call" | custom-call | flops 100000000 | tf_op jit(solution)/shard_map/pallas_call | solution.py:1130
  251.1 3.6 %collective-permute-start.30 = (bf16[48,1664]{1,0:T(8,128)(2,1)}, bf16[48,1664]{1,0:T(8,128)(2,1)}, u32[]{:S(2)}, u32[]{:S(2)}) collective-permute-start(bf16[48,1664]{1,0:T(8,128)(2,1)} %get-tuple-element.105), channel_id=1, source_target_pairs={{0,6},{2,0},{4,2},{6,4},{1,7},{3,1},{5,3},{7,5},{8,14},{10,8},{12,... | collective-permute-start | bytes 479240 | tf_op jit(solution)/shard_map/ppermute | solution.py:1340
  255.2 2.2 fusion.21
  261.4 4.4 %collective-permute-done.29.refs_1_ = bf16[48,1664]{1,0:T(8,128)(2,1)} collective-permute-done((bf16[48,1664]{1,0:T(8,128)(2,1)}, bf16[48,1664]{1,0:T(8,128)(2,1)}, u32[]{:S(2)}, u32[]{:S(2)}) %collective-permute-start.29) | collective-permute-done | bytes 159776 | tf_op jit(solution)/shard_map/ppermute | solution.py:1340
  267.3 1.5 collective-permute-start.33
  269.3 2.2 collective-permute-start.40
  272.9 2.0 collective-permute-done.39.refs_11_.refs_9_
  275.6 5.3 %collective-permute-done.33.refs_5_.refs_2_ = bf16[960,128]{1,0:T(8,128)(2,1)S(1)} collective-permute-done((bf16[960,128]{1,0:T(8,128)(2,1)S(1)}, bf16[960,128]{1,0:T(8,128)(2,1)S(1)}, u32[]{:S(2)}, u32[]{:S(2)}) %collective-permute-start.33) | collective-permute-done | bytes 245792 | tf_op jit(solution)/shard_map/ppermute | solution.py:1162
  286.4 4.3 %shard_map.276 = (f32[2,48,2048]{2,1,0:T(8,128)}, f32[2,48,2048]{2,1,0:T(8,128)}, f32[2,128,768]{2,1,0:T(8,128)}, f32[48,2048]{1,0:T(8,128)}, f32[48,2048]{1,0:T(8,128)}, /*index=5*/f32[128,768]{1,0:T(8,128)}) custom-call(s32[7]{0:T(128)S(1)} %copy-done.3, bf16[960,128]{1,0:T(8,128)(2,1)} %get-tuple-element.140.refs_0_, bf16[960,128]{1,0:T(8,128)(2,1)} %copy-done.31, ...), custom_call_target="tpu_custom_call" | custom-call | flops 100000000 | tf_op jit(solution)/shard_map/pallas_call | solution.py:1130
  291.4 3.9 %shard_map.275 = (f32[256,768]{1,0:T(8,128)}, f32[48,2304]{1,0:T(8,128)}, f32[48,768]{1,0:T(8,128)}, f32[1,48]{1,0:T(1,128)}, f32[1,48]{1,0:T(1,128)}, /*index=5*/f32[4,48]{1,0:T(4,128)}) custom-call(s32[7]{0:T(128)S(1)} %copy-done.3, bf16[48,1664]{1,0:T(8,128)(2,1)} %copy-done.27, bf16[48,1664]{1,0:T(8,128)(2,1)} %copy-done.49, bf16[256,768]{1,0:T(8,128)(2,1)} %bitcast.60, ...), custom_call_target="tpu_custom_call" | custom-call | flops 100000000 | tf_op jit(solution)/shard_map/pallas_call | solution.py:1130
  (192 shorter events, 51.9 us)
Async XLA Ops:
  7.2 65.3 %all-gather.2.cloned.1.call-start = ((), (), s32[]{:S(2)}) async-start(), calls=%async_computation.1 | async-start | bytes 3538944 | tf_op jit(solution)/shard_map/all_gather | solution.py:1198
  7.9 246.8 %reduce-scatter.2.cloned.1.call-start = ((), (), s32[]{:S(2)}) async-start(), calls=%async_computation.2 | async-start | bytes 7372800 | tf_op jit(solution)/shard_map/reduce_scatter | solution.py:1286
  8.0 14.8 %collective-permute-start = (bf16[256,768]{1,0:T(8,128)(2,1)}, bf16[256,768]{1,0:T(8,128)(2,1)S(1)}, u32[]{:S(2)}, u32[]{:S(2)}) collective-permute-start(bf16[256,768]{1,0:T(8,128)(2,1)} %bitcast.56), channel_id=1, source_target_pairs={{0,2},{2,4},{4,6},{1,3},{3,5},{5,7},{8,10},{10,12},{12,14},{9,11},... | collective-permute-start | bytes 1179656 | tf_op jit(solution)/shard_map/ppermute | solution.py:1199
  12.9 20.2 %collective-permute-start.2 = (bf16[256,768]{1,0:T(8,128)(2,1)}, bf16[256,768]{1,0:T(8,128)(2,1)S(1)}, u32[]{:S(2)}, u32[]{:S(2)}) collective-permute-start(bf16[256,768]{1,0:T(8,128)(2,1)} %bitcast.57), channel_id=1, source_target_pairs={{0,6},{1,7},{8,14},{9,15},{16,22},{17,23},{24,30},{25,31}} | collective-permute-start | bytes 1179656 | tf_op jit(solution)/shard_map/ppermute | solution.py:1202
  22.7 10.4 %collective-permute-start.1 = (bf16[256,768]{1,0:T(8,128)(2,1)S(1)}, bf16[256,768]{1,0:T(8,128)(2,1)S(1)}, u32[]{:S(2)}, u32[]{:S(2)}) collective-permute-start(bf16[256,768]{1,0:T(8,128)(2,1)S(1)} %collective-permute-done.refs_1_), channel_id=1, source_target_pairs={{2,4},{4,6},{3,5},{5,7},{10,12},{12,14},{11,13},{13,15},{18,20},{2... | collective-permute-start | bytes 1179656 | tf_op jit(solution)/shard_map/ppermute | solution.py:1200
  50.9 9.6 %collective-permute-start.3 = (bf16[272,768]{1,0:T(8,128)(2,1)}, bf16[272,768]{1,0:T(8,128)(2,1)S(1)}, u32[]{:S(2)}, u32[]{:S(2)}) collective-permute-start(bf16[272,768]{1,0:T(8,128)(2,1)} %get-tuple-element.71.refs_0_), channel_id=1, source_target_pairs={{0,1},{1,0},{8,9},{9,8},{16,17},{17,16},{24,25},{25,24},{2,3},{3,2... | collective-permute-start | bytes 1253384 | tf_op jit(solution)/shard_map/ppermute | solution.py:1162
  52.5 11.0 %collective-permute-start.4 = (bf16[272,768]{1,0:T(8,128)(2,1)}, bf16[272,768]{1,0:T(8,128)(2,1)S(1)}, u32[]{:S(2)}, u32[]{:S(2)}) collective-permute-start(bf16[272,768]{1,0:T(8,128)(2,1)} %get-tuple-element.71.refs_0_), channel_id=1, source_target_pairs={{0,16},{1,17},{8,24},{9,25},{16,0},{17,1},{24,8},{25,9},{2,18},{3,... | collective-permute-start | bytes 1253384 | tf_op jit(solution)/shard_map/ppermute | solution.py:1162
  60.5 10.2 %collective-permute-start.5 = (bf16[272,768]{1,0:T(8,128)(2,1)S(1)}, bf16[272,768]{1,0:T(8,128)(2,1)S(1)}, u32[]{:S(2)}, u32[]{:S(2)}) collective-permute-start(bf16[272,768]{1,0:T(8,128)(2,1)S(1)} %collective-permute-done.3.refs_1_), channel_id=1, source_target_pairs={{0,16},{1,17},{8,24},{9,25},{16,0},{17,1},{24,8},{25,9},{2,18},{3,... | collective-permute-start | bytes 1253384 | tf_op jit(solution)/shard_map/ppermute | solution.py:1162
  62.0 8.7 %collective-permute-start.7 = (bf16[272,768]{1,0:T(8,128)(2,1)S(1)}, bf16[272,768]{1,0:T(8,128)(2,1)S(1)}, u32[]{:S(2)}, u32[]{:S(2)}) collective-permute-start(bf16[272,768]{1,0:T(8,128)(2,1)S(1)} %collective-permute-done.3.refs_1_), channel_id=1, source_target_pairs={{0,8},{1,9},{8,0},{9,1},{16,24},{17,25},{24,16},{25,17},{2,10},{3,... | collective-permute-start | bytes 1253384 | tf_op jit(solution)/shard_map/ppermute | solution.py:1162
  118.7 10.1 %collective-permute-start.10 = (bf16[4,256,768]{2,1,0:T(8,128)(2,1)}, bf16[4,256,768]{2,1,0:T(8,128)(2,1)S(1)}, u32[]{:S(2)}, u32[]{:S(2)}) collective-permute-start(bf16[4,256,768]{2,1,0:T(8,128)(2,1)} %get-tuple-element.75), channel_id=1, source_target_pairs={{0,8},{1,9},{8,0},{9,1},{16,24},{17,25},{24,16},{25,17},{2,10},{3,... | collective-permute-start | bytes 4718600 | tf_op jit(solution)/shard_map/ppermute | solution.py:1162
  125.4 12.9 %collective-permute-start.14 = (bf16[256,768]{1,0:T(8,128)(2,1)S(1)}, bf16[256,768]{1,0:T(8,128)(2,1)S(1)}, u32[]{:S(2)}, u32[]{:S(2)}) collective-permute-start(bf16[256,768]{1,0:T(8,128)(2,1)S(1)} %get-tuple-element.130), channel_id=1, source_target_pairs={{0,17},{1,16},{8,25},{9,24},{16,1},{17,0},{24,9},{25,8},{2,19},{3,... | collective-permute-start | bytes 1179656 | tf_op jit(solution)/shard_map/ppermute | solution.py:1162
  127.0 17.9 %collective-permute-start.13 = (bf16[256,768]{1,0:T(8,128)(2,1)S(1)}, bf16[256,768]{1,0:T(8,128)(2,1)S(1)}, u32[]{:S(2)}, u32[]{:S(2)}) collective-permute-start(bf16[256,768]{1,0:T(8,128)(2,1)S(1)} %get-tuple-element.131), channel_id=1, source_target_pairs={{0,16},{1,17},{8,24},{9,25},{16,0},{17,1},{24,8},{25,9},{2,18},{3,... | collective-permute-start | bytes 1179656 | tf_op jit(solution)/shard_map/ppermute | solution.py:1162
  127.3 18.6 %collective-permute-start.12 = (bf16[256,768]{1,0:T(8,128)(2,1)S(1)}, bf16[256,768]{1,0:T(8,128)(2,1)S(1)}, u32[]{:S(2)}, u32[]{:S(2)}) collective-permute-start(bf16[256,768]{1,0:T(8,128)(2,1)S(1)} %get-tuple-element.132), channel_id=1, source_target_pairs={{0,1},{1,0},{8,9},{9,8},{16,17},{17,16},{24,25},{25,24},{2,3},{3,2... | collective-permute-start | bytes 1179656 | tf_op jit(solution)/shard_map/ppermute | solution.py:1162
  147.2 22.0 %collective-permute-start.15 = (bf16[256,768]{1,0:T(8,128)(2,1)}, bf16[256,768]{1,0:T(8,128)(2,1)S(1)}, u32[]{:S(2)}, u32[]{:S(2)}) collective-permute-start(bf16[256,768]{1,0:T(8,128)(2,1)} %get-tuple-element.78.refs_17_), channel_id=1, source_target_pairs={{0,1},{1,0},{8,9},{9,8},{16,17},{17,16},{24,25},{25,24},{2,3},{3,2... | collective-permute-start | bytes 1179656 | tf_op jit(solution)/shard_map/ppermute | solution.py:1162
  148.0 21.2 %collective-permute-start.16 = (bf16[256,768]{1,0:T(8,128)(2,1)}, bf16[256,768]{1,0:T(8,128)(2,1)S(1)}, u32[]{:S(2)}, u32[]{:S(2)}) collective-permute-start(bf16[256,768]{1,0:T(8,128)(2,1)} %get-tuple-element.79.refs_18_), channel_id=1, source_target_pairs={{0,16},{1,17},{8,24},{9,25},{16,0},{17,1},{24,8},{25,9},{2,18},{3,... | collective-permute-start | bytes 1179656 | tf_op jit(solution)/shard_map/ppermute | solution.py:1162
  149.5 19.7 %collective-permute-start.17 = (bf16[256,768]{1,0:T(8,128)(2,1)}, bf16[256,768]{1,0:T(8,128)(2,1)S(1)}, u32[]{:S(2)}, u32[]{:S(2)}) collective-permute-start(bf16[256,768]{1,0:T(8,128)(2,1)} %get-tuple-element.80.refs_19_), channel_id=1, source_target_pairs={{0,17},{1,16},{8,25},{9,24},{16,1},{17,0},{24,9},{25,8},{2,19},{3,... | collective-permute-start | bytes 1179656 | tf_op jit(solution)/shard_map/ppermute | solution.py:1162
  175.8 24.8 %collective-permute-start.21 = (bf16[192,1024]{1,0:T(8,128)(2,1)S(1)}, bf16[192,1024]{1,0:T(8,128)(2,1)S(1)}, u32[]{:S(2)}, u32[]{:S(2)}) collective-permute-start(bf16[192,1024]{1,0:T(8,128)(2,1)S(1)} %get-tuple-element.125), channel_id=1, source_target_pairs={{0,17},{1,16},{8,25},{9,24},{16,1},{17,0},{24,9},{25,8},{2,19},{3,... | collective-permute-start | bytes 1179656 | tf_op jit(solution)/shard_map/ppermute | solution.py:1162
  177.6 23.1 %collective-permute-start.20 = (bf16[192,1024]{1,0:T(8,128)(2,1)S(1)}, bf16[192,1024]{1,0:T(8,128)(2,1)S(1)}, u32[]{:S(2)}, u32[]{:S(2)}) collective-permute-start(bf16[192,1024]{1,0:T(8,128)(2,1)S(1)} %get-tuple-element.126), channel_id=1, source_target_pairs={{0,16},{1,17},{8,24},{9,25},{16,0},{17,1},{24,8},{25,9},{2,18},{3,... | collective-permute-start | bytes 1179656 | tf_op jit(solution)/shard_map/ppermute | solution.py:1162
  178.1 22.6 %collective-permute-start.19 = (bf16[192,1024]{1,0:T(8,128)(2,1)S(1)}, bf16[192,1024]{1,0:T(8,128)(2,1)S(1)}, u32[]{:S(2)}, u32[]{:S(2)}) collective-permute-start(bf16[192,1024]{1,0:T(8,128)(2,1)S(1)} %get-tuple-element.127), channel_id=1, source_target_pairs={{0,1},{1,0},{8,9},{9,8},{16,17},{17,16},{24,25},{25,24},{2,3},{3,2... | collective-permute-start | bytes 1179656 | tf_op jit(solution)/shard_map/ppermute | solution.py:1162
  203.2 43.5 %collective-permute-start.27 = (bf16[256,768]{1,0:T(8,128)(2,1)}, bf16[256,768]{1,0:T(8,128)(2,1)S(1)}, u32[]{:S(2)}, u32[]{:S(2)}) collective-permute-start(bf16[256,768]{1,0:T(8,128)(2,1)} %get-tuple-element.101), channel_id=1, source_target_pairs={{6,0},{7,1},{14,8},{15,9},{22,16},{23,17},{30,24},{31,25}} | collective-permute-start | bytes 1179656 | tf_op jit(solution)/shard_map/ppermute | solution.py:1373
  206.0 40.6 %collective-permute-start.25 = (bf16[192,640]{1,0:T(8,128)(2,1)S(1)}, bf16[192,640]{1,0:T(8,128)(2,1)S(1)}, u32[]{:S(2)}, u32[]{:S(2)}) collective-permute-start(bf16[192,640]{1,0:T(8,128)(2,1)S(1)} %get-tuple-element.136), channel_id=1, source_target_pairs={{0,17},{1,16},{8,25},{9,24},{16,1},{17,0},{24,9},{25,8},{2,19},{3,... | collective-permute-start | bytes 737288 | tf_op jit(solution)/shard_map/ppermute | solution.py:1162
  207.8 38.9 %collective-permute-start.24 = (bf16[192,640]{1,0:T(8,128)(2,1)S(1)}, bf16[192,640]{1,0:T(8,128)(2,1)S(1)}, u32[]{:S(2)}, u32[]{:S(2)}) collective-permute-start(bf16[192,640]{1,0:T(8,128)(2,1)S(1)} %get-tuple-element.137), channel_id=1, source_target_pairs={{0,16},{1,17},{8,24},{9,25},{16,0},{17,1},{24,8},{25,9},{2,18},{3,... | collective-permute-start | bytes 737288 | tf_op jit(solution)/shard_map/ppermute | solution.py:1162
  208.3 38.4 %collective-permute-start.23 = (bf16[192,640]{1,0:T(8,128)(2,1)S(1)}, bf16[192,640]{1,0:T(8,128)(2,1)S(1)}, u32[]{:S(2)}, u32[]{:S(2)}) collective-permute-start(bf16[192,640]{1,0:T(8,128)(2,1)S(1)} %get-tuple-element.138), channel_id=1, source_target_pairs={{0,1},{1,0},{8,9},{9,8},{16,17},{17,16},{24,25},{25,24},{2,3},{3,2... | collective-permute-start | bytes 737288 | tf_op jit(solution)/shard_map/ppermute | solution.py:1162
  210.4 48.4 %collective-permute-start.31 = (bf16[256,768]{1,0:T(8,128)(2,1)}, bf16[256,768]{1,0:T(8,128)(2,1)S(1)}, u32[]{:S(2)}, u32[]{:S(2)}) collective-permute-start(bf16[256,768]{1,0:T(8,128)(2,1)} %add_convert_fusion), channel_id=1, source_target_pairs={{2,0},{4,2},{6,4},{3,1},{5,3},{7,5},{10,8},{12,10},{14,12},{11,9},... | collective-permute-start | bytes 1179656 | tf_op jit(solution)/shard_map/ppermute | solution.py:1376
  250.8 9.2 %collective-permute-start.28 = (bf16[48,1664]{1,0:T(8,128)(2,1)}, bf16[48,1664]{1,0:T(8,128)(2,1)}, u32[]{:S(2)}, u32[]{:S(2)}) collective-permute-start(bf16[48,1664]{1,0:T(8,128)(2,1)} %get-tuple-element.103), channel_id=1, source_target_pairs={{0,2},{2,4},{4,6},{6,0},{1,3},{3,5},{5,7},{7,1},{8,10},{10,12},{12... | collective-permute-start | bytes 479240 | tf_op jit(solution)/shard_map/ppermute | solution.py:1340
  250.8 15.0 %collective-permute-start.29 = (bf16[48,1664]{1,0:T(8,128)(2,1)}, bf16[48,1664]{1,0:T(8,128)(2,1)}, u32[]{:S(2)}, u32[]{:S(2)}) collective-permute-start(bf16[48,1664]{1,0:T(8,128)(2,1)} %get-tuple-element.104), channel_id=1, source_target_pairs={{0,4},{2,6},{4,0},{6,2},{1,5},{3,7},{5,1},{7,3},{8,12},{10,14},{12... | collective-permute-start | bytes 479240 | tf_op jit(solution)/shard_map/ppermute | solution.py:1340
  251.1 16.3 %collective-permute-start.30 = (bf16[48,1664]{1,0:T(8,128)(2,1)}, bf16[48,1664]{1,0:T(8,128)(2,1)}, u32[]{:S(2)}, u32[]{:S(2)}) collective-permute-start(bf16[48,1664]{1,0:T(8,128)(2,1)} %get-tuple-element.105), channel_id=1, source_target_pairs={{0,6},{2,0},{4,2},{6,4},{1,7},{3,1},{5,3},{7,5},{8,14},{10,8},{12,... | collective-permute-start | bytes 479240 | tf_op jit(solution)/shard_map/ppermute | solution.py:1340
  257.4 9.9 %collective-permute-start.38 = (bf16[192,128]{1,0:T(8,128)(2,1)S(1)}, bf16[192,128]{1,0:T(8,128)(2,1)S(1)}, u32[]{:S(2)}, u32[]{:S(2)}) collective-permute-start(bf16[192,128]{1,0:T(8,128)(2,1)S(1)} %get-tuple-element.146), channel_id=1, source_target_pairs={{0,25},{1,24},{8,17},{9,16},{16,9},{17,8},{24,1},{25,0},{2,27},{3,... | collective-permute-start | bytes 147464 | tf_op jit(solution)/shard_map/ppermute | solution.py:1162
  258.8 10.1 %collective-permute-start.37 = (bf16[192,128]{1,0:T(8,128)(2,1)S(1)}, bf16[192,128]{1,0:T(8,128)(2,1)S(1)}, u32[]{:S(2)}, u32[]{:S(2)}) collective-permute-start(bf16[192,128]{1,0:T(8,128)(2,1)S(1)} %get-tuple-element.147), channel_id=1, source_target_pairs={{0,17},{1,16},{8,25},{9,24},{16,1},{17,0},{24,9},{25,8},{2,19},{3,... | collective-permute-start | bytes 147464 | tf_op jit(solution)/shard_map/ppermute | solution.py:1162
  260.1 9.2 %collective-permute-start.36 = (bf16[192,128]{1,0:T(8,128)(2,1)S(1)}, bf16[192,128]{1,0:T(8,128)(2,1)S(1)}, u32[]{:S(2)}, u32[]{:S(2)}) collective-permute-start(bf16[192,128]{1,0:T(8,128)(2,1)S(1)} %get-tuple-element.148), channel_id=1, source_target_pairs={{0,9},{1,8},{8,1},{9,0},{16,25},{17,24},{24,17},{25,16},{2,11},{3,... | collective-permute-start | bytes 147464 | tf_op jit(solution)/shard_map/ppermute | solution.py:1162
  267.3 13.5 %collective-permute-start.33 = (bf16[960,128]{1,0:T(8,128)(2,1)S(1)}, bf16[960,128]{1,0:T(8,128)(2,1)S(1)}, u32[]{:S(2)}, u32[]{:S(2)}) collective-permute-start(bf16[960,128]{1,0:T(8,128)(2,1)S(1)} %get-tuple-element.142), channel_id=1, source_target_pairs={{0,16},{1,17},{8,24},{9,25},{16,0},{17,1},{24,8},{25,9},{2,18},{3,... | collective-permute-start | bytes 737288 | tf_op jit(solution)/shard_map/ppermute | solution.py:1162
  268.9 12.0 %collective-permute-start.32 = (bf16[960,128]{1,0:T(8,128)(2,1)S(1)}, bf16[960,128]{1,0:T(8,128)(2,1)S(1)}, u32[]{:S(2)}, u32[]{:S(2)}) collective-permute-start(bf16[960,128]{1,0:T(8,128)(2,1)S(1)} %get-tuple-element.143), channel_id=1, source_target_pairs={{0,8},{1,9},{8,0},{9,1},{16,24},{17,25},{24,16},{25,17},{2,10},{3,... | collective-permute-start | bytes 737288 | tf_op jit(solution)/shard_map/ppermute | solution.py:1162
  (63 other events, 391.5 us)
Sparse Core Ops, SparseCore 0:
  9.9 35.0 all-gather.1
  117.3 118.6 reduce-scatter.1

commit v3 on v2

--- a/solution.py
+++ b/solution.py
@@ -1390,7 +1390,7 @@
         for run in range(2)
     ]
 
-    shares = [shares[0], *hold_until(scalars, shares[1:], [pulled[0], *slabs[1:], *shared_far, *got_downs])]
+    shares = [shares[0], *hold_until(scalars, shares[1:], [pulled[0]])]
     spread = total(shares)
     gate_grad, up_grad, down_grad, gate_s_grad, up_s_grad, down_s_grad = call(
         partial(feed_grads_kernel, n_dp, layout),

time: 308 us -> 314 us (1.019)
  waiting for transfers between devices: 94.8 us -> 99.4 us
    ppermute x3, waiting for transfers between devices: 4.46 us -> 10.9 us  [by_context(): lax.ppermute(shares[r], CONTEXT, [(i, (i + r) % n_context) for i in range...]
    unnamed x103 -> x107, local copies, waits for them, and re-layouts: 9.59 us -> 9.73 us
  transfers between devices with their start and end apart: 44 -> 44, of which waited for: 17 -> 16; matrix products, arithmetic and copies ran while one was open for 6% -> 6% of each run, Pallas kernels for 23% -> 23%
where the time goes in v3:
time: 314 us; the launch traced here: 309 us
  Pallas kernels  119 us (38%)
  waiting for transfers between devices  99.4 us (32%)
  starting transfers between devices  47.4 us (15%)
  local copies, waits for them, and re-layouts  19.5 us (6%)
  between operations  15 us (5%)
  other arithmetic  8.62 us (3%)
    pallas_call x13, Pallas kernels, call(): pl.pallas_call(body, grid_spec=pltpu.PrefetchScalarGridSpec(num_scalar_pr...  119 us
    ppermute x31, waiting for transfers between devices, swap(): return lax.ppermute(value, group, [(i, i ^ mask) for i in range(8)])  45.7 us
    ppermute x1, waiting for transfers between devices, on_block(): lax.ppermute(grad_far[r - 1], CONTEXT, [(i, i - r) for i in range(r, n_co...  35.4 us
    ppermute x31, starting transfers between devices, swap(): return lax.ppermute(value, group, [(i, i ^ mask) for i in range(8)])  28.5 us
    ppermute x3, waiting for transfers between devices, by_context(): lax.ppermute(shares[r], CONTEXT, [(i, (i + r) % n_context) for i in range...  10.9 us
    unnamed x107, local copies, waits for them, and re-layouts  9.73 us
    ppermute x1, waiting for transfers between devices, on_block(): lax.ppermute(own, CONTEXT, [(i, i + 1) for i in range(n_context - 1)])  6.44 us
  transfers between devices with their start and end apart: 44, of which 16 were waited for; matrix products, arithmetic and copies ran while one was open for 6% of the time, Pallas kernels for 23%

profile of v3, /device:TPU:0, one launch (start us, length us, event | category | flops | bytes accessed | tf_op | source)
XLA Modules:
  0.0 308.6 jit_solution(17867701321117042297)
XLA Ops:
  8.0 5.0 %collective-permute-start = (bf16[256,768]{1,0:T(8,128)(2,1)}, bf16[256,768]{1,0:T(8,128)(2,1)S(1)}, u32[]{:S(2)}, u32[]{:S(2)}) collective-permute-start(bf16[256,768]{1,0:T(8,128)(2,1)} %bitcast.56), channel_id=1, source_target_pairs={{0,2},{2,4},{4,6},{1,3},{3,5},{5,7},{8,10},{10,12},{12,14},{9,11},... | collective-permute-start | bytes 1179656 | tf_op jit(solution)/shard_map/ppermute | solution.py:1199
  12.9 3.4 %collective-permute-start.2 = (bf16[256,768]{1,0:T(8,128)(2,1)}, bf16[256,768]{1,0:T(8,128)(2,1)S(1)}, u32[]{:S(2)}, u32[]{:S(2)}) collective-permute-start(bf16[256,768]{1,0:T(8,128)(2,1)} %bitcast.57), channel_id=1, source_target_pairs={{0,6},{1,7},{8,14},{9,15},{16,22},{17,23},{24,30},{25,31}} | collective-permute-start | bytes 1179656 | tf_op jit(solution)/shard_map/ppermute | solution.py:1202
  16.3 6.4 %collective-permute-done.refs_1_ = bf16[256,768]{1,0:T(8,128)(2,1)S(1)} collective-permute-done((bf16[256,768]{1,0:T(8,128)(2,1)}, bf16[256,768]{1,0:T(8,128)(2,1)S(1)}, u32[]{:S(2)}, u32[]{:S(2)}) %collective-permute-start) | collective-permute-done | bytes 393248 | tf_op jit(solution)/shard_map/ppermute | solution.py:1199
  29.1 4.1 %shard_map.264 = (bf16[768,256]{1,0:T(8,128)(2,1)}, bf16[768,256]{1,0:T(8,128)(2,1)}, bf16[256,768]{1,0:T(8,128)(2,1)}) custom-call(s32[7]{0:T(128)S(1)} %stack.32.place, bf16[768,2048]{1,0:T(8,128)(2,1)} %refs_0_.1, bf16[768,2048]{1,0:T(8,128)(2,1)} %refs_1_.1, bf16[2048,768]{1,0:T(8,128)(2,1)} %refs_2_.1, bf16[768,128]{1,0:T(8,128)(2,1)} %pad.8.refs_3_.refs_9_, ...), custom_call_target="tpu_custom_call" | custom-call | flops 100000000 | tf_op jit(solution)/shard_map/pallas_call | solution.py:1130
  34.0 16.9 %shard_map.265 = (bf16[1024,768]{1,0:T(8,128)(2,1)}, bf16[256,768]{1,0:T(8,128)(2,1)}, bf16[1024,768]{1,0:T(8,128)(2,1)}, bf16[1024,768]{1,0:T(8,128)(2,1)}, f32...) custom-call(s32[1]{0:T(128)} %bitcast.place, ...), custom_call_target="tpu_custom_call" | custom-call | flops 100000000 | tf_op jit(solution)/shard_map/pallas_call | solution.py:1130
  50.9 1.6 collective-permute-start.3
  54.0 6.6 %collective-permute-done.3.refs_1_ = bf16[272,768]{1,0:T(8,128)(2,1)S(1)} collective-permute-done((bf16[272,768]{1,0:T(8,128)(2,1)}, bf16[272,768]{1,0:T(8,128)(2,1)S(1)}, u32[]{:S(2)}, u32[]{:S(2)}) %collective-permute-start.3) | collective-permute-done | bytes 417824 | tf_op jit(solution)/shard_map/ppermute | solution.py:1162
  63.4 7.3 %collective-permute-done.5.refs_3_ = bf16[272,768]{1,0:T(8,128)(2,1)S(1)} collective-permute-done((bf16[272,768]{1,0:T(8,128)(2,1)S(1)}, bf16[272,768]{1,0:T(8,128)(2,1)S(1)}, u32[]{:S(2)}, u32[]{:S(2)}) %collective-permute-start.5) | collective-permute-done | bytes 417824 | tf_op jit(solution)/shard_map/ppermute | solution.py:1162
  70.8 1.7 collective-permute-done.9.refs_7_
  73.3 43.9 %shard_map.266 = (bf16[4,256,768]{2,1,0:T(8,128)(2,1)}, bf16[4,256,768]{2,1,0:T(8,128)(2,1)}, bf16[4,256,768]{2,1,0:T(8,128)(2,1)}, bf16[4,256,768]{2,1,0:T(8,12...) custom-call(s32[7]{0:T(128)} %copy-done.2, bf16[272,768]{1,0:T(8,128)(2,1)} %get-tuple-element.71.refs_0_, ...), custom_call_target="tpu_custom_call" | custom-call | flops 100000000 | tf_op jit(solution)/shard_map/pallas_call | solution.py:1130
  119.1 3.8 %collective-permute-done.11 = bf16[4,256,768]{2,1,0:T(8,128)(2,1)S(1)} collective-permute-done((bf16[4,256,768]{2,1,0:T(8,128)(2,1)S(1)}, bf16[4,256,768]{2,1,0:T(8,128)(2,1)S(1)}, u32[]{:S(2)}, u32[]{:S(2)}) %collective-permute-start.11) | collective-permute-done | bytes 1572896 | tf_op jit(solution)/shard_map/ppermute | solution.py:1162
  123.0 2.6 fusion.11
  125.6 1.5 collective-permute-start.14
  130.2 8.2 %collective-permute-done.14.refs_5_.refs_3_ = bf16[256,768]{1,0:T(8,128)(2,1)S(1)} collective-permute-done((bf16[256,768]{1,0:T(8,128)(2,1)S(1)}, bf16[256,768]{1,0:T(8,128)(2,1)S(1)}, u32[]{:S(2)}, u32[]{:S(2)}) %collective-permute-start.14) | collective-permute-done | bytes 393248 | tf_op jit(solution)/shard_map/ppermute | solution.py:1162
  138.5 6.7 %collective-permute-done.13.refs_4_.refs_2_ = bf16[256,768]{1,0:T(8,128)(2,1)S(1)} collective-permute-done((bf16[256,768]{1,0:T(8,128)(2,1)S(1)}, bf16[256,768]{1,0:T(8,128)(2,1)S(1)}, u32[]{:S(2)}, u32[]{:S(2)}) %collective-permute-start.13) | collective-permute-done | bytes 393248 | tf_op jit(solution)/shard_map/ppermute | solution.py:1162
  150.9 18.5 %shard_map.268 = (f32[256,768]{1,0:T(8,128)}, bf16[256,768]{1,0:T(8,128)(2,1)}, bf16[256,384]{1,0:T(8,128)(2,1)}, bf16[1024,768]{1,0:T(8,128)(2,1)}, f32[8,768]{...) custom-call(s32[7]{0:T(128)S(1)} %copy-done.3, ...), custom_call_target="tpu_custom_call" | custom-call | flops 100000000 | tf_op jit(solution)/shard_map/pallas_call | solution.py:1130
  171.0 3.6 %collective-permute-done.18 = bf16[2,2,192,1024]{3,2,1,0:T(8,128)(2,1)S(1)} collective-permute-done((bf16[2,2,192,1024]{3,2,1,0:T(8,128)(2,1)}, bf16[2,2,192,1024]{3,2,1,0:T(8,128)(2,1)S(1)}, u32[]{:S(2)}, u32[]{:S(2)}) %collective-permute-start.18) | collective-permute-done | bytes 1572896 | tf_op jit(solution)/shard_map/ppermute | solution.py:1162
  176.1 1.7 collective-permute-start.21
  179.6 21.3 %shard_map.270 = (f32[256,768]{1,0:T(8,128)}, bf16[256,768]{1,0:T(8,128)(2,1)}, bf16[256,768]{1,0:T(8,128)(2,1)}, bf16[256,768]{1,0:T(8,128)(2,1)}, bf16[2,2,192...) custom-call(s32[7]{0:T(128)S(1)} %copy-done.3, bf16[256,768]{1,0:T(8,128)(2,1)} %bitcast.59, ...), custom_call_target="tpu_custom_call" | custom-call | flops 100000000 | tf_op jit(solution)/shard_map/pallas_call | solution.py:1130
  206.3 1.7 collective-permute-start.25
  211.2 35.4 %collective-permute-done.27.refs_9_.refs_7_ = bf16[256,768]{1,0:T(8,128)(2,1)S(1)} collective-permute-done((bf16[256,768]{1,0:T(8,128)(2,1)}, bf16[256,768]{1,0:T(8,128)(2,1)S(1)}, u32[]{:S(2)}, u32[]{:S(2)}) %collective-permute-start.27) | collective-permute-done | bytes 393248 | tf_op jit(solution)/shard_map/ppermute | solution.py:1373
  247.7 3.2 %shard_map.272 = (bf16[48,1664]{1,0:T(8,128)(2,1)}, bf16[48,1664]{1,0:T(8,128)(2,1)}, bf16[48,1664]{1,0:T(8,128)(2,1)}, bf16[48,1664]{1,0:T(8,128)(2,1)}) custom-call(s32[7]{0:T(128)S(1)} %copy-done.3, bf16[192,1024]{1,0:T(8,128)(2,1)} %get-tuple-element.128.refs_18_.refs_0_, bf16[192,1024]{1,0:T(8,128)(2,1)} %copy-done.26, bf16[192,1024]{1,0:T(8,128)(2,1)} %copy-done.25, ...), custom_call_target="tpu_custom_call" | custom-call | flops 100000000 | tf_op jit(solution)/shard_map/pallas_call | solution.py:1130
  251.2 3.6 %collective-permute-start.30 = (bf16[48,1664]{1,0:T(8,128)(2,1)}, bf16[48,1664]{1,0:T(8,128)(2,1)S(1)}, u32[]{:S(2)}, u32[]{:S(2)}) collective-permute-start(bf16[48,1664]{1,0:T(8,128)(2,1)} %get-tuple-element.105), channel_id=1, source_target_pairs={{0,6},{2,0},{4,2},{6,4},{1,7},{3,1},{5,3},{7,5},{8,14},{10,8},{12,... | collective-permute-start | bytes 479240 | tf_op jit(solution)/shard_map/ppermute | solution.py:1340
  255.0 5.1 %collective-permute-done.28.refs_0_ = bf16[48,1664]{1,0:T(8,128)(2,1)S(1)} collective-permute-done((bf16[48,1664]{1,0:T(8,128)(2,1)}, bf16[48,1664]{1,0:T(8,128)(2,1)S(1)}, u32[]{:S(2)}, u32[]{:S(2)}) %collective-permute-start.28) | collective-permute-done | bytes 159776 | tf_op jit(solution)/shard_map/ppermute | solution.py:1340
  260.1 5.8 %collective-permute-done.29.refs_1_ = bf16[48,1664]{1,0:T(8,128)(2,1)S(1)} collective-permute-done((bf16[48,1664]{1,0:T(8,128)(2,1)}, bf16[48,1664]{1,0:T(8,128)(2,1)S(1)}, u32[]{:S(2)}, u32[]{:S(2)}) %collective-permute-start.29) | collective-permute-done | bytes 159776 | tf_op jit(solution)/shard_map/ppermute | solution.py:1340
  269.0 1.5 collective-permute-start.32
  273.0 2.2 fusion.23
  278.2 1.5 collective-permute-start.36
  282.4 2.3 collective-permute-start.35
  286.4 3.9 %shard_map.274 = (f32[256,768]{1,0:T(8,128)}, f32[48,2304]{1,0:T(8,128)}, f32[48,768]{1,0:T(8,128)}, f32[1,48]{1,0:T(1,128)}, f32[1,48]{1,0:T(1,128)}, /*index=5*/f32[4,48]{1,0:T(4,128)}) custom-call(s32[7]{0:T(128)S(1)} %copy-done.3, bf16[48,1664]{1,0:T(8,128)(2,1)} %copy-done.27, bf16[48,1664]{1,0:T(8,128)(2,1)} %copy-done.47, bf16[256,768]{1,0:T(8,128)(2,1)} %bitcast.60, ...), custom_call_target="tpu_custom_call" | custom-call | flops 100000000 | tf_op jit(solution)/shard_map/pallas_call | solution.py:1130
  291.1 5.3 %collective-permute-done.34.refs_2_ = bf16[960,128]{1,0:T(8,128)(2,1)S(1)} collective-permute-done((bf16[960,128]{1,0:T(8,128)(2,1)S(1)}, bf16[960,128]{1,0:T(8,128)(2,1)S(1)}, u32[]{:S(2)}, u32[]{:S(2)}) %collective-permute-start.34) | collective-permute-done | bytes 245792 | tf_op jit(solution)/shard_map/ppermute | solution.py:1162
  297.3 4.3 %shard_map.276 = (f32[2,48,2048]{2,1,0:T(8,128)}, f32[2,48,2048]{2,1,0:T(8,128)}, f32[2,128,768]{2,1,0:T(8,128)}, f32[48,2048]{1,0:T(8,128)}, f32[48,2048]{1,0:T(8,128)}, /*index=5*/f32[128,768]{1,0:T(8,128)}) custom-call(s32[7]{0:T(128)S(1)} %copy-done.3, bf16[960,128]{1,0:T(8,128)(2,1)} %get-tuple-element.149.refs_0_, bf16[960,128]{1,0:T(8,128)(2,1)} %copy-done.41, ...), custom_call_target="tpu_custom_call" | custom-call | flops 100000000 | tf_op jit(solution)/shard_map/pallas_call | solution.py:1130
  (196 shorter events, 52.9 us)
Async XLA Ops:
  7.2 65.4 %all-gather.2.cloned.1.call-start = ((), (), s32[]{:S(2)}) async-start(), calls=%async_computation.1 | async-start | bytes 3538944 | tf_op jit(solution)/shard_map/all_gather | solution.py:1198
  7.9 262.6 %reduce-scatter.2.cloned.1.call-start = ((), (), s32[]{:S(2)}) async-start(), calls=%async_computation.2 | async-start | bytes 7372800 | tf_op jit(solution)/shard_map/reduce_scatter | solution.py:1286
  8.0 14.8 %collective-permute-start = (bf16[256,768]{1,0:T(8,128)(2,1)}, bf16[256,768]{1,0:T(8,128)(2,1)S(1)}, u32[]{:S(2)}, u32[]{:S(2)}) collective-permute-start(bf16[256,768]{1,0:T(8,128)(2,1)} %bitcast.56), channel_id=1, source_target_pairs={{0,2},{2,4},{4,6},{1,3},{3,5},{5,7},{8,10},{10,12},{12,14},{9,11},... | collective-permute-start | bytes 1179656 | tf_op jit(solution)/shard_map/ppermute | solution.py:1199
  12.9 20.2 %collective-permute-start.2 = (bf16[256,768]{1,0:T(8,128)(2,1)}, bf16[256,768]{1,0:T(8,128)(2,1)S(1)}, u32[]{:S(2)}, u32[]{:S(2)}) collective-permute-start(bf16[256,768]{1,0:T(8,128)(2,1)} %bitcast.57), channel_id=1, source_target_pairs={{0,6},{1,7},{8,14},{9,15},{16,22},{17,23},{24,30},{25,31}} | collective-permute-start | bytes 1179656 | tf_op jit(solution)/shard_map/ppermute | solution.py:1202
  22.7 10.4 %collective-permute-start.1 = (bf16[256,768]{1,0:T(8,128)(2,1)S(1)}, bf16[256,768]{1,0:T(8,128)(2,1)S(1)}, u32[]{:S(2)}, u32[]{:S(2)}) collective-permute-start(bf16[256,768]{1,0:T(8,128)(2,1)S(1)} %collective-permute-done.refs_1_), channel_id=1, source_target_pairs={{2,4},{4,6},{3,5},{5,7},{10,12},{12,14},{11,13},{13,15},{18,20},{2... | collective-permute-start | bytes 1179656 | tf_op jit(solution)/shard_map/ppermute | solution.py:1200
  50.9 9.7 %collective-permute-start.3 = (bf16[272,768]{1,0:T(8,128)(2,1)}, bf16[272,768]{1,0:T(8,128)(2,1)S(1)}, u32[]{:S(2)}, u32[]{:S(2)}) collective-permute-start(bf16[272,768]{1,0:T(8,128)(2,1)} %get-tuple-element.71.refs_0_), channel_id=1, source_target_pairs={{0,1},{1,0},{8,9},{9,8},{16,17},{17,16},{24,25},{25,24},{2,3},{3,2... | collective-permute-start | bytes 1253384 | tf_op jit(solution)/shard_map/ppermute | solution.py:1162
  52.5 10.9 %collective-permute-start.4 = (bf16[272,768]{1,0:T(8,128)(2,1)}, bf16[272,768]{1,0:T(8,128)(2,1)S(1)}, u32[]{:S(2)}, u32[]{:S(2)}) collective-permute-start(bf16[272,768]{1,0:T(8,128)(2,1)} %get-tuple-element.71.refs_0_), channel_id=1, source_target_pairs={{0,16},{1,17},{8,24},{9,25},{16,0},{17,1},{24,8},{25,9},{2,18},{3,... | collective-permute-start | bytes 1253384 | tf_op jit(solution)/shard_map/ppermute | solution.py:1162
  60.6 10.2 %collective-permute-start.5 = (bf16[272,768]{1,0:T(8,128)(2,1)S(1)}, bf16[272,768]{1,0:T(8,128)(2,1)S(1)}, u32[]{:S(2)}, u32[]{:S(2)}) collective-permute-start(bf16[272,768]{1,0:T(8,128)(2,1)S(1)} %collective-permute-done.3.refs_1_), channel_id=1, source_target_pairs={{0,16},{1,17},{8,24},{9,25},{16,0},{17,1},{24,8},{25,9},{2,18},{3,... | collective-permute-start | bytes 1253384 | tf_op jit(solution)/shard_map/ppermute | solution.py:1162
  62.1 8.7 %collective-permute-start.7 = (bf16[272,768]{1,0:T(8,128)(2,1)S(1)}, bf16[272,768]{1,0:T(8,128)(2,1)S(1)}, u32[]{:S(2)}, u32[]{:S(2)}) collective-permute-start(bf16[272,768]{1,0:T(8,128)(2,1)S(1)} %collective-permute-done.3.refs_1_), channel_id=1, source_target_pairs={{0,8},{1,9},{8,0},{9,1},{16,24},{17,25},{24,16},{25,17},{2,10},{3,... | collective-permute-start | bytes 1253384 | tf_op jit(solution)/shard_map/ppermute | solution.py:1162
  118.8 10.3 %collective-permute-start.10 = (bf16[4,256,768]{2,1,0:T(8,128)(2,1)}, bf16[4,256,768]{2,1,0:T(8,128)(2,1)S(1)}, u32[]{:S(2)}, u32[]{:S(2)}) collective-permute-start(bf16[4,256,768]{2,1,0:T(8,128)(2,1)} %get-tuple-element.75), channel_id=1, source_target_pairs={{0,8},{1,9},{8,0},{9,1},{16,24},{17,25},{24,16},{25,17},{2,10},{3,... | collective-permute-start | bytes 4718600 | tf_op jit(solution)/shard_map/ppermute | solution.py:1162
  125.6 12.9 %collective-permute-start.14 = (bf16[256,768]{1,0:T(8,128)(2,1)S(1)}, bf16[256,768]{1,0:T(8,128)(2,1)S(1)}, u32[]{:S(2)}, u32[]{:S(2)}) collective-permute-start(bf16[256,768]{1,0:T(8,128)(2,1)S(1)} %get-tuple-element.130), channel_id=1, source_target_pairs={{0,17},{1,16},{8,25},{9,24},{16,1},{17,0},{24,9},{25,8},{2,19},{3,... | collective-permute-start | bytes 1179656 | tf_op jit(solution)/shard_map/ppermute | solution.py:1162
  127.1 18.1 %collective-permute-start.13 = (bf16[256,768]{1,0:T(8,128)(2,1)S(1)}, bf16[256,768]{1,0:T(8,128)(2,1)S(1)}, u32[]{:S(2)}, u32[]{:S(2)}) collective-permute-start(bf16[256,768]{1,0:T(8,128)(2,1)S(1)} %get-tuple-element.131), channel_id=1, source_target_pairs={{0,16},{1,17},{8,24},{9,25},{16,0},{17,1},{24,8},{25,9},{2,18},{3,... | collective-permute-start | bytes 1179656 | tf_op jit(solution)/shard_map/ppermute | solution.py:1162
  127.6 18.5 %collective-permute-start.12 = (bf16[256,768]{1,0:T(8,128)(2,1)S(1)}, bf16[256,768]{1,0:T(8,128)(2,1)S(1)}, u32[]{:S(2)}, u32[]{:S(2)}) collective-permute-start(bf16[256,768]{1,0:T(8,128)(2,1)S(1)} %get-tuple-element.132), channel_id=1, source_target_pairs={{0,1},{1,0},{8,9},{9,8},{16,17},{17,16},{24,25},{25,24},{2,3},{3,2... | collective-permute-start | bytes 1179656 | tf_op jit(solution)/shard_map/ppermute | solution.py:1162
  147.3 22.0 %collective-permute-start.15 = (bf16[256,768]{1,0:T(8,128)(2,1)}, bf16[256,768]{1,0:T(8,128)(2,1)S(1)}, u32[]{:S(2)}, u32[]{:S(2)}) collective-permute-start(bf16[256,768]{1,0:T(8,128)(2,1)} %get-tuple-element.78.refs_17_), channel_id=1, source_target_pairs={{0,1},{1,0},{8,9},{9,8},{16,17},{17,16},{24,25},{25,24},{2,3},{3,2... | collective-permute-start | bytes 1179656 | tf_op jit(solution)/shard_map/ppermute | solution.py:1162
  148.1 21.2 %collective-permute-start.16 = (bf16[256,768]{1,0:T(8,128)(2,1)}, bf16[256,768]{1,0:T(8,128)(2,1)S(1)}, u32[]{:S(2)}, u32[]{:S(2)}) collective-permute-start(bf16[256,768]{1,0:T(8,128)(2,1)} %get-tuple-element.79.refs_18_), channel_id=1, source_target_pairs={{0,16},{1,17},{8,24},{9,25},{16,0},{17,1},{24,8},{25,9},{2,18},{3,... | collective-permute-start | bytes 1179656 | tf_op jit(solution)/shard_map/ppermute | solution.py:1162
  149.6 19.8 %collective-permute-start.17 = (bf16[256,768]{1,0:T(8,128)(2,1)}, bf16[256,768]{1,0:T(8,128)(2,1)S(1)}, u32[]{:S(2)}, u32[]{:S(2)}) collective-permute-start(bf16[256,768]{1,0:T(8,128)(2,1)} %get-tuple-element.80.refs_19_), channel_id=1, source_target_pairs={{0,17},{1,16},{8,25},{9,24},{16,1},{17,0},{24,9},{25,8},{2,19},{3,... | collective-permute-start | bytes 1179656 | tf_op jit(solution)/shard_map/ppermute | solution.py:1162
  176.1 24.8 %collective-permute-start.21 = (bf16[192,1024]{1,0:T(8,128)(2,1)S(1)}, bf16[192,1024]{1,0:T(8,128)(2,1)S(1)}, u32[]{:S(2)}, u32[]{:S(2)}) collective-permute-start(bf16[192,1024]{1,0:T(8,128)(2,1)S(1)} %get-tuple-element.125), channel_id=1, source_target_pairs={{0,17},{1,16},{8,25},{9,24},{16,1},{17,0},{24,9},{25,8},{2,19},{3,... | collective-permute-start | bytes 1179656 | tf_op jit(solution)/shard_map/ppermute | solution.py:1162
  177.8 23.2 %collective-permute-start.20 = (bf16[192,1024]{1,0:T(8,128)(2,1)S(1)}, bf16[192,1024]{1,0:T(8,128)(2,1)S(1)}, u32[]{:S(2)}, u32[]{:S(2)}) collective-permute-start(bf16[192,1024]{1,0:T(8,128)(2,1)S(1)} %get-tuple-element.126), channel_id=1, source_target_pairs={{0,16},{1,17},{8,24},{9,25},{16,0},{17,1},{24,8},{25,9},{2,18},{3,... | collective-permute-start | bytes 1179656 | tf_op jit(solution)/shard_map/ppermute | solution.py:1162
  178.3 22.7 %collective-permute-start.19 = (bf16[192,1024]{1,0:T(8,128)(2,1)S(1)}, bf16[192,1024]{1,0:T(8,128)(2,1)S(1)}, u32[]{:S(2)}, u32[]{:S(2)}) collective-permute-start(bf16[192,1024]{1,0:T(8,128)(2,1)S(1)} %get-tuple-element.127), channel_id=1, source_target_pairs={{0,1},{1,0},{8,9},{9,8},{16,17},{17,16},{24,25},{25,24},{2,3},{3,2... | collective-permute-start | bytes 1179656 | tf_op jit(solution)/shard_map/ppermute | solution.py:1162
  203.4 43.2 %collective-permute-start.27 = (bf16[256,768]{1,0:T(8,128)(2,1)}, bf16[256,768]{1,0:T(8,128)(2,1)S(1)}, u32[]{:S(2)}, u32[]{:S(2)}) collective-permute-start(bf16[256,768]{1,0:T(8,128)(2,1)} %get-tuple-element.101), channel_id=1, source_target_pairs={{6,0},{7,1},{14,8},{15,9},{22,16},{23,17},{30,24},{31,25}} | collective-permute-start | bytes 1179656 | tf_op jit(solution)/shard_map/ppermute | solution.py:1373
  206.3 40.3 %collective-permute-start.25 = (bf16[192,640]{1,0:T(8,128)(2,1)S(1)}, bf16[192,640]{1,0:T(8,128)(2,1)S(1)}, u32[]{:S(2)}, u32[]{:S(2)}) collective-permute-start(bf16[192,640]{1,0:T(8,128)(2,1)S(1)} %get-tuple-element.136), channel_id=1, source_target_pairs={{0,17},{1,16},{8,25},{9,24},{16,1},{17,0},{24,9},{25,8},{2,19},{3,... | collective-permute-start | bytes 737288 | tf_op jit(solution)/shard_map/ppermute | solution.py:1162
  208.0 38.6 %collective-permute-start.24 = (bf16[192,640]{1,0:T(8,128)(2,1)S(1)}, bf16[192,640]{1,0:T(8,128)(2,1)S(1)}, u32[]{:S(2)}, u32[]{:S(2)}) collective-permute-start(bf16[192,640]{1,0:T(8,128)(2,1)S(1)} %get-tuple-element.137), channel_id=1, source_target_pairs={{0,16},{1,17},{8,24},{9,25},{16,0},{17,1},{24,8},{25,9},{2,18},{3,... | collective-permute-start | bytes 737288 | tf_op jit(solution)/shard_map/ppermute | solution.py:1162
  208.6 38.1 %collective-permute-start.23 = (bf16[192,640]{1,0:T(8,128)(2,1)S(1)}, bf16[192,640]{1,0:T(8,128)(2,1)S(1)}, u32[]{:S(2)}, u32[]{:S(2)}) collective-permute-start(bf16[192,640]{1,0:T(8,128)(2,1)S(1)} %get-tuple-element.138), channel_id=1, source_target_pairs={{0,1},{1,0},{8,9},{9,8},{16,17},{17,16},{24,25},{25,24},{2,3},{3,2... | collective-permute-start | bytes 737288 | tf_op jit(solution)/shard_map/ppermute | solution.py:1162
  209.9 45.0 %collective-permute-start.31 = (bf16[256,768]{1,0:T(8,128)(2,1)S(1)}, bf16[256,768]{1,0:T(8,128)(2,1)S(1)}, u32[]{:S(2)}, u32[]{:S(2)}) collective-permute-start(bf16[256,768]{1,0:T(8,128)(2,1)S(1)} %add_convert_fusion), channel_id=1, source_target_pairs={{2,0},{4,2},{6,4},{3,1},{5,3},{7,5},{10,8},{12,10},{14,12},{11,9},... | collective-permute-start | bytes 1179656 | tf_op jit(solution)/shard_map/ppermute | solution.py:1376
  251.0 9.1 %collective-permute-start.28 = (bf16[48,1664]{1,0:T(8,128)(2,1)}, bf16[48,1664]{1,0:T(8,128)(2,1)S(1)}, u32[]{:S(2)}, u32[]{:S(2)}) collective-permute-start(bf16[48,1664]{1,0:T(8,128)(2,1)} %get-tuple-element.103), channel_id=1, source_target_pairs={{0,2},{2,4},{4,6},{6,0},{1,3},{3,5},{5,7},{7,1},{8,10},{10,12},{12... | collective-permute-start | bytes 479240 | tf_op jit(solution)/shard_map/ppermute | solution.py:1340
  251.0 14.9 %collective-permute-start.29 = (bf16[48,1664]{1,0:T(8,128)(2,1)}, bf16[48,1664]{1,0:T(8,128)(2,1)S(1)}, u32[]{:S(2)}, u32[]{:S(2)}) collective-permute-start(bf16[48,1664]{1,0:T(8,128)(2,1)} %get-tuple-element.104), channel_id=1, source_target_pairs={{0,4},{2,6},{4,0},{6,2},{1,5},{3,7},{5,1},{7,3},{8,12},{10,14},{12... | collective-permute-start | bytes 479240 | tf_op jit(solution)/shard_map/ppermute | solution.py:1340
  251.2 14.7 %collective-permute-start.30 = (bf16[48,1664]{1,0:T(8,128)(2,1)}, bf16[48,1664]{1,0:T(8,128)(2,1)S(1)}, u32[]{:S(2)}, u32[]{:S(2)}) collective-permute-start(bf16[48,1664]{1,0:T(8,128)(2,1)} %get-tuple-element.105), channel_id=1, source_target_pairs={{0,6},{2,0},{4,2},{6,4},{1,7},{3,1},{5,3},{7,5},{8,14},{10,8},{12,... | collective-permute-start | bytes 479240 | tf_op jit(solution)/shard_map/ppermute | solution.py:1340
  269.0 10.8 %collective-permute-start.32 = (bf16[48,1664]{1,0:T(8,128)(2,1)S(1)}, bf16[48,1664]{1,0:T(8,128)(2,1)S(1)}, u32[]{:S(2)}, u32[]{:S(2)}) collective-permute-start(bf16[48,1664]{1,0:T(8,128)(2,1)S(1)} %add_convert_fusion.17.refs_0_.refs_11_), channel_id=1, source_target_pairs={{0,1},{1,0},{8,9},{9,8},{16,17},{17,16},{24,25},{25,24},{2,3},{3,2... | collective-permute-start | bytes 479240 | tf_op jit(solution)/shard_map/ppermute | solution.py:1162
  279.8 11.3 %collective-permute-start.41 = (bf16[768,128]{1,0:T(8,128)(2,1)S(1)}, bf16[768,128]{1,0:T(8,128)(2,1)S(1)}, u32[]{:S(2)}, u32[]{:S(2)}) collective-permute-start(bf16[768,128]{1,0:T(8,128)(2,1)S(1)} %get-tuple-element.140), channel_id=1, source_target_pairs={{0,8},{16,24},{1,9},{17,25},{2,10},{18,26},{3,11},{19,27},{4,12},{... | collective-permute-start | bytes 589832 | tf_op jit(solution)/shard_map/ppermute | solution.py:1387
  281.1 10.0 %collective-permute-start.40 = (bf16[768,128]{1,0:T(8,128)(2,1)S(1)}, bf16[768,128]{1,0:T(8,128)(2,1)S(1)}, u32[]{:S(2)}, u32[]{:S(2)}) collective-permute-start(bf16[768,128]{1,0:T(8,128)(2,1)S(1)} %get-tuple-element.141), channel_id=1, source_target_pairs={{8,0},{24,16},{9,1},{25,17},{10,2},{26,18},{11,3},{27,19},{12,4},{... | collective-permute-start | bytes 589832 | tf_op jit(solution)/shard_map/ppermute | solution.py:1387
  284.7 11.8 %collective-permute-start.34 = (bf16[960,128]{1,0:T(8,128)(2,1)S(1)}, bf16[960,128]{1,0:T(8,128)(2,1)S(1)}, u32[]{:S(2)}, u32[]{:S(2)}) collective-permute-start(bf16[960,128]{1,0:T(8,128)(2,1)S(1)} %get-tuple-element.147), channel_id=1, source_target_pairs={{0,16},{1,17},{8,24},{9,25},{16,0},{17,1},{24,8},{25,9},{2,18},{3,... | collective-permute-start | bytes 737288 | tf_op jit(solution)/shard_map/ppermute | solution.py:1162
  285.2 11.2 %collective-permute-start.33 = (bf16[960,128]{1,0:T(8,128)(2,1)S(1)}, bf16[960,128]{1,0:T(8,128)(2,1)S(1)}, u32[]{:S(2)}, u32[]{:S(2)}) collective-permute-start(bf16[960,128]{1,0:T(8,128)(2,1)S(1)} %get-tuple-element.148), channel_id=1, source_target_pairs={{0,8},{1,9},{8,0},{9,1},{16,24},{17,25},{24,16},{25,17},{2,10},{3,... | collective-permute-start | bytes 737288 | tf_op jit(solution)/shard_map/ppermute | solution.py:1162
  (65 other events, 337.6 us)
Sparse Core Ops, SparseCore 0:
  9.9 35.0 all-gather.1
  117.4 118.6 reduce-scatter.1
